TPU v7x, 32 devices: a whole 2x2x4 slice. The times are simulated.
32 devices in a mesh: rep: 2 (over x), fsdp: 16 (over z, y, core).
Axes of the slice: x: 2, y: 2, z: 4, core: 2. Of those that a mesh axis runs over, the one named last changes fastest.
Arguments:
- hidden: bfloat16 [8192, 4096], P(('rep', 'fsdp')), may hold values from -6 to 6
- weight: bfloat16 [512, 4096], P('fsdp'), may hold values from -0.09375 to 0.09375
- adapter_a: float32 [4096, 128], P('fsdp'), may hold values from -0.09375 to 0.09375
- adapter_b: float32 [512, 128], P('fsdp'), may hold values from -0.25 to 0.25
- grad_a: float32 [2, 4096, 128], P('rep', 'fsdp'), may hold values from -0.09375 to 0.09375
- grad_b: float32 [2, 512, 128], P('rep', 'fsdp'), may hold values from -0.25 to 0.25
Outputs:
- projected: bfloat16 [8192, 512], P(('rep', 'fsdp'))
- merged: bfloat16 [512, 4096], P('fsdp')
All inputs are finite; a program needn't handle non-finite values.
Results may differ from a plain program's by a relative error of at most 0.0049.
Values may be sent and summed in bfloat16 or wider, within the bound.
No kernel may reach another device: no remote copies, remote signals or barrier semaphores. Data moves between devices by JAX's collectives and lax.ppermute only.
A program may use at most 64 MiB of HBM per device.

v0:
```python
import jax
import jax.numpy as jnp
from jax import lax
from jax.sharding import PartitionSpec as P

step_size = 0.5


def low_rank(b_rows, full_a):
    return lax.dot_general(
        b_rows,
        full_a,
        (((1,), (1,)), ((), ())),
        precision=lax.Precision.HIGHEST,
        preferred_element_type=jnp.float32,
    )


def merge_rows(rows, b_rows, full_a):
    return (rows.astype(jnp.float32) + low_rank(b_rows, full_a)).astype(jnp.bfloat16)


def shards(hidden, weight, adapter_a, adapter_b, grad_a, grad_b):
    replicas = lax.axis_size("rep")
    summed = lax.psum((grad_a[0], grad_b[0]), "rep")
    new_a = adapter_a - step_size * (summed[0] / replicas)
    new_b = adapter_b - step_size * (summed[1] / replicas)
    full_a = lax.all_gather(new_a, "fsdp", axis=0, tiled=True)
    own_rows = merge_rows(weight, new_b, full_a)
    output = lax.dot_general(
        hidden,
        lax.all_gather(own_rows, "fsdp", axis=0, tiled=True),
        (((1,), (1,)), ((), ())),
        preferred_element_type=jnp.float32,
    )
    return (output.astype(jnp.bfloat16), own_rows)


def solution(mesh):
    return jax.shard_map(
        shards,
        mesh=mesh,
        in_specs=(
            P(("rep", "fsdp"), None),
            P("fsdp", None),
            P("fsdp", None),
            P("fsdp", None),
            P("rep", "fsdp", None),
            P("rep", "fsdp", None),
        ),
        out_specs=(P(("rep", "fsdp"), None), P("fsdp", None)),
        check_vma=False,
    )
```

profile of v0, /device:TPU:0, one launch (start us, length us, event | category | flops | bytes accessed | tf_op | source)
XLA Modules:
  0.0 143.6 jit_solution(15575241683331066186)
XLA Ops:
  7.2 0.0 copy-start
  7.2 0.0 all-reduce.2.cloned.1.call-start
  7.2 0.7 all-reduce.2.cloned.1.call-update
  7.9 0.0 all-gather.3.cloned.1.call-start
  8.0 26.5 %all-reduce.2.cloned.1.call-done = f32[256,128]{1,0:T(8,128)} async-done(((f32[256,128]{1,0:T(8,128)}), f32[256,128]{1,0:T(8,128)}) %all-reduce.2.cloned.1.call-update) | async-done | bytes 131088 | tf_op jit(solution)/shard_map/psum | solution.py:25
  34.4 1.6 %multiply_subtract_fusion = f32[256,128]{1,0:T(8,128)} fusion(f32[256,128]{1,0:T(8,128)} %param.8, f32[256,128]{1,0:T(8,128)} %all-reduce.2.cloned.1.call-done), kind=kLoop, calls=%fused_computation.4 | loop fusion | flops 65536 | bytes 393216 | tf_op jit(solution)/shard_map/sub | solution.py:26
  36.1 0.0 all-gather.3.cloned.1.call-update
  36.1 0.0 all-gather.5.cloned.1.call-start
  36.1 7.5 %psum.14 = f32[32,128]{1,0:T(8,128)S(1)} all-reduce(f32[32,128]{1,0:T(8,128)} %bitcast.8), channel_id=1, replica_groups=mesh['rep'=2,'fsdp'=16] {'rep'}, use_global_device_ids=true, to_apply=%region_0.0 | all-reduce | flops 4096 | bytes 32768 | tf_op jit(solution)/shard_map/psum | solution.py:25
  43.6 35.0 %all-gather.3.cloned.1.call-done = f32[4096,128]{1,0:T(8,128)} async-done(((f32[256,128]{1,0:T(8,128)}), f32[4096,128]{1,0:T(8,128)}) %all-gather.3.cloned.1.call-update) | async-done | bytes 2097168 | tf_op jit(solution)/shard_map/all_gather | solution.py:28
  78.6 4.5 %fusion = bf16[32,4096]{1,0:T(8,128)(2,1)} fusion(f32[4096,128]{1,0:T(8,128)} %all-gather.3.cloned.1.call-done, bf16[32,4096]{1,0:T(8,128)(2,1)} %param.7, f32[32,128]{1,0:T(8,128)} %param.9, f32[32,128]{1,0:T(8,128)S(1)} %psum.14), kind=kOutput, calls=%fused_computation.1 | convolution fusion | flops 201728000 | bytes 2654208 | tf_op jit(solution)/shard_map/dot_general | solution.py:10
  83.1 0.0 all-gather.5.cloned.1.call-update
  83.1 49.6 %all-gather.5.cloned.1.call-done = bf16[512,4096]{1,0:T(8,128)(2,1)} async-done(((bf16[32,4096]{1,0:T(8,128)(2,1)}), bf16[512,4096]{1,0:T(8,128)(2,1)}) %all-gather.5.cloned.1.call-update) | async-done | bytes 4194320 | tf_op jit(solution)/shard_map/all_gather | solution.py:32
  132.7 0.0 copy-done
  132.7 3.5 %fusion.1 = bf16[256,512]{0,1:T(8,128)(2,1)S(1)} fusion(bf16[512,4096]{1,0:T(8,128)(2,1)} %all-gather.5.cloned.1.call-done, bf16[256,4096]{1,0:T(8,128)(2,1)S(1)} %copy-done), kind=kOutput, calls=%fused_computation.3 | convolution fusion | flops 1073872896 | bytes 6553600 | tf_op jit(solution)/shard_map/dot_general | solution.py:30
  136.2 0.8 copy.8
Async XLA Ops:
  7.2 125.6 %copy-start = (bf16[256,4096]{1,0:T(8,128)(2,1)S(1)}, bf16[256,4096]{1,0:T(8,128)(2,1)}, u32[]{:S(2)}) copy-start(bf16[256,4096]{1,0:T(8,128)(2,1)} %param.6) | copy-start | bytes 6291460
  7.2 27.3 %all-reduce.2.cloned.1.call-start = ((), (), s32[]{:S(2)}) async-start(), calls=%async_computation | async-start | bytes 262144 | tf_op jit(solution)/shard_map/psum | solution.py:25
  7.9 70.7 %all-gather.3.cloned.1.call-start = ((), (), s32[]{:S(2)}) async-start(), calls=%async_computation.1 | async-start | bytes 2228224 | tf_op jit(solution)/shard_map/all_gather | solution.py:28
  36.1 96.6 %all-gather.5.cloned.1.call-start = ((), (), s32[]{:S(2)}) async-start(), calls=%async_computation.2 | async-start | bytes 4456448 | tf_op jit(solution)/shard_map/all_gather | solution.py:32
Sparse Core Ops, SparseCore 0:
  10.3 24.1 all-reduce.1
  37.2 41.3 all-gather.2
  83.2 49.4 all-gather.4
where the time goes:
time: 144 us
  waiting for transfers between devices  112 us (78%)
  between operations  13.8 us (10%)
  matrix products  7.93 us (6%)
  blocking collectives  7.48 us (5%)
  other arithmetic  1.64 us (1%)
    all_gather x1, waiting for transfers between devices, shards(): lax.all_gather(own_rows, 'fsdp', axis=0, tiled=True)  49.6 us
    all_gather x1, waiting for transfers between devices, shards(): full_a = lax.all_gather(new_a, 'fsdp', axis=0, tiled=True)  35 us
    psum x1, waiting for transfers between devices, shards(): summed = lax.psum((grad_a[0], grad_b[0]), 'rep')  26.5 us
    psum x1, blocking collectives, shards(): summed = lax.psum((grad_a[0], grad_b[0]), 'rep')  7.48 us
    dot_general x1, matrix products, low_rank(): lax.dot_general(b_rows, full_a, (((1,), (1,)), ((), ())), precision=lax.P...  4.46 us
    dot_general x1, matrix products, shards(): lax.dot_general(hidden, lax.all_gather(own_rows, 'fsdp', axis=0, tiled=Tr...  3.47 us
  transfers between devices with their start and end apart: 3, of which 3 were waited for; matrix products, arithmetic and copies ran while one was open for 0% of the time, Pallas kernels for 0%

commit v1 on v0

v1 whole, which is shorter than its diff:
```python
import functools

import jax
import jax.numpy as jnp
from jax import lax
from jax.experimental import pallas as pl
from jax.experimental.pallas import tpu as pltpu
from jax.sharding import PartitionSpec as P

step_size = 0.5
AXES = ("rep", "fsdp")
NT = (((1,), (1,)), ((), ()))
NN = (((1,), (0,)), ((), ()))


def permute(rows, group, flip_rep, flip_fsdp):
    reps, shards = group
    pairs = [
        (r * shards + f, (r ^ flip_rep) * shards + (f ^ flip_fsdp))
        for r in range(reps)
        for f in range(shards)
    ]
    return lax.ppermute(rows, AXES, pairs)


def dot(a, b, dims):
    return lax.dot_general(a, b, dims, preferred_element_type=jnp.float32)


def general(hidden, weight, adapter_a, adapter_b, grad_a, grad_b):
    replicas = lax.axis_size("rep")
    summed = lax.psum((grad_a[0], grad_b[0]), "rep")
    new_a = adapter_a - step_size * (summed[0] / replicas)
    new_b = adapter_b - step_size * (summed[1] / replicas)
    full_a = lax.all_gather(new_a, "fsdp", axis=0, tiled=True)
    delta = lax.dot_general(new_b, full_a, NT, precision=lax.Precision.HIGHEST, preferred_element_type=jnp.float32)
    own_rows = (weight.astype(jnp.float32) + delta).astype(jnp.bfloat16)
    output = dot(hidden, lax.all_gather(own_rows, "fsdp", axis=0, tiled=True), NT)
    return output.astype(jnp.bfloat16), own_rows


def project_kernel(pieces, planes, *refs):
    n_w = len(pieces)
    w_refs, rest = refs[:n_w], refs[n_w:]
    ab_refs, rest = rest[:8], rest[8:]
    h_ref, hs_ref, own_ref, sib_ref, merged_ref = rest[:5]
    w_all, a_all, b_all, h_all, b_own, sems = rest[5:]
    x, f = lax.axis_index("rep"), lax.axis_index("fsdp")
    core = f & 1
    place = f >> 1
    half_w = w_all.shape[0] // (2 * 2 * planes)
    half_a = a_all.shape[0] // (4 * 2 * planes)
    half_b = half_w
    tokens = h_ref.shape[0]

    copies_h, copies_w, copies_a = [], [], []

    def copy(group, source, target):
        sem = sems.at[len(copies_h) + len(copies_w) + len(copies_a)]
        group.append(pltpu.make_async_copy(source, target, sem))

    copy(copies_h, h_ref, h_all.at[pl.ds(0, tokens)])
    copy(copies_h, hs_ref, h_all.at[pl.ds(tokens, tokens)])
    for ref, (dz, dy, dh) in zip(w_refs, pieces):
        at = place ^ (dz * 2 + dy)
        if dh is None:
            start, size = at * (2 * half_w), 2 * half_w
        else:
            start, size = at * (2 * half_w) + (x ^ dh) * half_w, half_w
        copy(copies_w, ref, w_all.at[pl.ds(pl.multiple_of(start, size), size)])
    for i, ref in enumerate(ab_refs):
        other, dy, dh = i // 4, (i % 4) // 2, i % 2
        for dz in range(planes):
            at = place ^ (dz * 2 + dy)
            row = dz * (half_a + half_b)
            shard = at * 2 + (core ^ other)
            start = pl.multiple_of(shard * (2 * half_a) + (x ^ dh) * half_a, half_a)
            copy(copies_a, ref.at[pl.ds(row, half_a)], a_all.at[pl.ds(start, half_a)])
            if not other:
                start = pl.multiple_of(at * (2 * half_b) + (x ^ dh) * half_b, half_b)
                copy(copies_a, ref.at[pl.ds(row + half_a, half_b)], b_all.at[pl.ds(start, half_b)])
    for c in copies_h + copies_w + copies_a:
        c.start()
    for c in copies_h:
        c.wait()
    for c in copies_a:
        c.wait()
    t = dot(h_all[...], a_all[...], NN)
    t_high = t.astype(jnp.bfloat16)
    t_low = (t - t_high.astype(jnp.float32)).astype(jnp.bfloat16)
    low = dot(t_high, b_all[...], NT) + dot(t_low, b_all[...], NT)
    for c in copies_w:
        c.wait()
    mine = pl.ds(pl.multiple_of(place * (2 * half_w), 2 * half_w), 2 * half_w)
    b_own[...] = b_all[mine, :]
    merged_ref[...] = (w_all[mine, :].astype(jnp.float32) + dot(b_own[...], a_all[...], NT)).astype(jnp.bfloat16)
    out = (dot(h_all[...], w_all[...], NT) + low).astype(jnp.bfloat16)
    own_ref[...] = out[:tokens]
    sib_ref[...] = out[tokens:]


def join_kernel(block, own_ref, other_ref, out_ref):
    core = lax.axis_index("fsdp") & 1
    n, m = own_ref.shape[1], out_ref.shape[1]
    source = lax.broadcasted_iota(jnp.int32, (n, m), 0)
    target = lax.broadcasted_iota(jnp.int32, (n, m), 1)
    base = (source // block) * (2 * block) + source % block
    here = (target == base + core * block).astype(jnp.bfloat16)
    there = (target == base + (1 - core) * block).astype(jnp.bfloat16)
    out_ref[...] = (dot(own_ref[...], here, NN) + dot(other_ref[...], there, NN)).astype(jnp.bfloat16)


def paired(hidden, weight, adapter_a, adapter_b, grad_a, grad_b):
    group = (lax.axis_size("rep"), lax.axis_size("fsdp"))
    planes = group[1] // 4
    x = lax.axis_index("rep")
    tokens, depth = hidden.shape
    rank = adapter_a.shape[1]
    ra, rb, rw = adapter_a.shape[0] // 2, adapter_b.shape[0] // 2, weight.shape[0] // 2

    def send(rows, dx=0, dz=0, dy=0, dc=0):
        return permute(rows, group, dx, dz * 4 + dy * 2 + dc)

    def half(rows, size, which):
        return lax.dynamic_slice_in_dim(rows, which * size, size, 0)

    grads = jnp.concatenate([half(grad_a[0], ra, 1 - x), half(grad_b[0], rb, 1 - x)])
    other = send(grads, dx=1)

    w_half = half(weight, rw, x)
    far = send(w_half, dz=2)
    near = send(w_half, dz=1)
    beside = send(weight, dy=1)
    sibling_hidden = send(hidden, dc=1)

    own = jnp.concatenate([half(grad_a[0], ra, x), half(grad_b[0], rb, x)])
    old = jnp.concatenate([half(adapter_a, ra, x), half(adapter_b, rb, x)])
    ab = (old - step_size * ((own + other) / group[0])).astype(jnp.bfloat16)
    ab_z = [ab] + [send(ab, dz=d) for d in range(1, planes)]

    w = {(0, 0, None): weight, (2, 0, 0): far, (1, 0, 0): near, (0, 1, None): beside}
    w[1, 0, 1] = send(near, dx=1)
    w[2, 0, 1] = send(far, dx=1)
    w[2, 1, 0] = send(far, dy=1)
    w[3, 0, 0] = send(far, dz=1)
    w[1, 1, None] = send(beside, dz=1)

    ab_00 = jnp.concatenate(ab_z)
    ab_01 = send(ab_00, dx=1)
    ab_10 = send(ab_00, dy=1)
    w[3, 0, 1] = send(w[3, 0, 0], dx=1)
    w[3, 1, 0] = send(w[3, 0, 0], dy=1)
    w[2, 1, 1] = send(w[2, 1, 0], dx=1)
    ab_11 = send(ab_01, dy=1)
    w[3, 1, 1] = send(w[3, 1, 0], dx=1)
    ab_c = [ab_00, ab_01, ab_10, ab_11]
    ab_c = ab_c + [send(v, dc=1) for v in ab_c]

    pieces = tuple(w)
    any_space = pl.BlockSpec(memory_space=pl.ANY)
    vmem = pl.BlockSpec(memory_space=pltpu.VMEM)
    columns = weight.shape[0] * group[1] // 2
    n_in = len(pieces) + len(ab_c) + 2
    half_out, half_sib, merged = pl.pallas_call(
        functools.partial(project_kernel, pieces, planes),
        out_shape=(
            jax.ShapeDtypeStruct((tokens, columns), jnp.bfloat16),
            jax.ShapeDtypeStruct((tokens, columns), jnp.bfloat16),
            jax.ShapeDtypeStruct(weight.shape, jnp.bfloat16),
        ),
        in_specs=[any_space] * n_in,
        out_specs=(vmem, vmem, vmem),
        scratch_shapes=[
            pltpu.VMEM((columns, depth), jnp.bfloat16),
            pltpu.VMEM((depth, rank), jnp.bfloat16),
            pltpu.VMEM((columns, rank), jnp.bfloat16),
            pltpu.VMEM((2 * tokens, depth), jnp.bfloat16),
            pltpu.VMEM((2 * rb, rank), jnp.bfloat16),
            pltpu.SemaphoreType.DMA((2 + len(pieces) + 12 * planes,)),
        ],
        compiler_params=pltpu.CompilerParams(vmem_limit_bytes=32 * 1024 * 1024),
        name="project",
    )(*[w[p] for p in pieces], *ab_c, hidden, sibling_hidden)
    received = send(half_sib, dc=1)
    projected = pl.pallas_call(
        functools.partial(join_kernel, weight.shape[0]),
        out_shape=jax.ShapeDtypeStruct((tokens, 2 * columns), jnp.bfloat16),
        in_specs=[vmem, vmem],
        out_specs=vmem,
        name="join",
    )(half_out, received)
    return projected, merged


def solution(mesh):
    paired_fits = mesh.shape["rep"] == 2 and mesh.shape["fsdp"] == 16
    return jax.shard_map(
        paired if paired_fits else general,
        mesh=mesh,
        in_specs=(
            P(("rep", "fsdp"), None),
            P("fsdp", None),
            P("fsdp", None),
            P("fsdp", None),
            P("rep", "fsdp", None),
            P("rep", "fsdp", None),
        ),
        out_specs=(P(("rep", "fsdp"), None), P("fsdp", None)),
        check_vma=False,
    )
```

time: 144 us -> 71.1 us (0.49)
  waiting for transfers between devices: 112 us -> 25.5 us
  starting transfers between devices: 0.12 us -> 25.3 us
  between operations: 13.8 us -> 0.73 us
  Pallas kernels: 0 us -> 12.1 us
  matrix products: 7.93 us -> 0 us
  blocking collectives: 7.48 us -> 0 us
  local copies, waits for them, and re-layouts: 0.85 us -> 7.06 us
  other arithmetic: 1.64 us -> 0.04 us
    all_gather x2 -> x0, waiting for transfers between devices: 84.6 us -> none  [the longest x1 49.6 us: shards(): lax.all_gather(own_rows, 'fsdp', axis=0, tiled=True)]
    psum x1 -> x0, waiting for transfers between devices: 26.5 us -> none  [shards(): summed = lax.psum((grad_a[0], grad_b[0]), 'rep')]
    ppermute x0 -> x25, waiting for transfers between devices: none -> 25.5 us  [permute(): return lax.ppermute(rows, AXES, pairs)]
    ppermute x0 -> x25, starting transfers between devices: none -> 25.3 us  [permute(): return lax.ppermute(rows, AXES, pairs)]
    pallas_call x0 -> x2, Pallas kernels: none -> 12.1 us  [the longest x1 10.2 us: paired(): pl.pallas_call(functools.partial(project_kernel, pieces, planes), out_sha...]
    dot_general x2 -> x0, matrix products: 7.93 us -> none  [the longest x1 4.46 us: low_rank(): lax.dot_general(b_rows, full_a, (((1,), (1,)), ((), ())), precision=lax.P...]
    psum x1 -> x0, blocking collectives: 7.48 us -> none  [shards(): summed = lax.psum((grad_a[0], grad_b[0]), 'rep')]
    dynamic_slice x0 -> x5, local copies, waits for them, and re-layouts: none -> 3.22 us  [half(): return lax.dynamic_slice_in_dim(rows, which * size, size, 0)]
  transfers between devices with their start and end apart: 3 -> 25, of which waited for: 3 -> 9; matrix products, arithmetic and copies ran while one was open for 0% -> 5% of each run, Pallas kernels for 0% -> 0%
where the time goes in v1:
time: 71.1 us; the launch traced here: 70.8 us
  waiting for transfers between devices  25.5 us (36%)
  starting transfers between devices  25.3 us (36%)
  Pallas kernels  12.1 us (17%)
  local copies, waits for them, and re-layouts  7.06 us (10%)
  between operations  0.73 us (1%)
    ppermute x25, waiting for transfers between devices, permute(): return lax.ppermute(rows, AXES, pairs)  25.5 us
    ppermute x25, starting transfers between devices, permute(): return lax.ppermute(rows, AXES, pairs)  25.3 us
    pallas_call x1, Pallas kernels, paired(): pl.pallas_call(functools.partial(project_kernel, pieces, planes), out_sha...  10.2 us
    unnamed x10, local copies, waits for them, and re-layouts  3.84 us
    dynamic_slice x5, local copies, waits for them, and re-layouts, half(): return lax.dynamic_slice_in_dim(rows, which * size, size, 0)  3.22 us
    pallas_call x1, Pallas kernels, paired(): pl.pallas_call(functools.partial(join_kernel, weight.shape[0]), out_shape...  1.99 us
  transfers between devices with their start and end apart: 25, of which 9 were waited for; matrix products, arithmetic and copies ran while one was open for 5% of the time, Pallas kernels for 0%

profile of v1, /device:TPU:0, one launch (start us, length us, event | category | flops | bytes accessed | tf_op | source)
XLA Modules:
  0.0 70.8 jit_solution(18381698408293043547)
XLA Ops:
  2.8 2.6 %collective-permute-start.12 = (f32[144,128]{1,0:T(8,128)S(1)}, f32[144,128]{1,0:T(8,128)S(1)}, u32[]{:S(2)}, u32[]{:S(2)}) collective-permute-start(f32[144,128]{1,0:T(8,128)S(1)} %pad_maximum_fusion.1), channel_id=1, source_target_pairs={{0,16},{1,17},{2,18},{3,19},{4,20},{5,21},{6,22},{7,23},{8,24},{9,... | collective-permute-start | bytes 221192 | tf_op jit(solution)/shard_map/ppermute | solution.py:23
  6.1 2.2 %collective-permute-done.12 = f32[144,128]{1,0:T(8,128)S(1)} collective-permute-done((f32[144,128]{1,0:T(8,128)S(1)}, f32[144,128]{1,0:T(8,128)S(1)}, u32[]{:S(2)}, u32[]{:S(2)}) %collective-permute-start.12) | collective-permute-done | bytes 73760 | tf_op jit(solution)/shard_map/ppermute | solution.py:23
  8.3 3.9 %collective-permute-start.15 = (bf16[144,128]{1,0:T(8,128)(2,1)S(1)}, bf16[144,128]{1,0:T(8,128)(2,1)S(1)}, u32[]{:S(2)}, u32[]{:S(2)}) collective-permute-start(bf16[144,128]{1,0:T(8,128)(2,1)S(1)} %fusion), channel_id=1, source_target_pairs={{0,12},{1,13},{2,14},{3,15},{4,8},{5,9},{6,10},{7,11},{8,4},{9,5},... | collective-permute-start | bytes 110600 | tf_op jit(solution)/shard_map/ppermute | solution.py:23
  13.8 1.5 %collective-permute-start.1 = (bf16[16,4096]{1,0:T(8,128)(2,1)S(1)}, bf16[16,4096]{1,0:T(8,128)(2,1)S(1)}, u32[]{:S(2)}, u32[]{:S(2)}) collective-permute-start(bf16[16,4096]{1,0:T(8,128)(2,1)S(1)} %constant_dynamic-slice_fusion.2), channel_id=1, source_target_pairs={{0,4},{1,5},{2,6},{3,7},{4,0},{5,1},{6,2},{7,3},{8,12},{9,13},{10,... | collective-permute-start | bytes 393224 | tf_op jit(solution)/shard_map/ppermute | solution.py:23
  15.2 1.9 %collective-permute-done.14 = bf16[144,128]{1,0:T(8,128)(2,1)S(1)} collective-permute-done((bf16[144,128]{1,0:T(8,128)(2,1)S(1)}, bf16[144,128]{1,0:T(8,128)(2,1)S(1)}, u32[]{:S(2)}, u32[]{:S(2)}) %collective-permute-start.14) | collective-permute-done | bytes 36896 | tf_op jit(solution)/shard_map/ppermute | solution.py:23
  17.3 1.6 %collective-permute-start.17 = (bf16[576,128]{1,0:T(8,128)(2,1)S(1)}, bf16[576,128]{1,0:T(8,128)(2,1)S(1)}, u32[]{:S(2)}, u32[]{:S(2)}) collective-permute-start(bf16[576,128]{1,0:T(8,128)(2,1)S(1)} %pad_maximum_fusion.refs_13_), channel_id=1, source_target_pairs={{0,2},{1,3},{2,0},{3,1},{4,6},{5,7},{6,4},{7,5},{8,10},{9,11},{10,... | collective-permute-start | bytes 442376 | tf_op jit(solution)/shard_map/ppermute | solution.py:23
  18.9 2.3 %collective-permute-start = (bf16[16,4096]{1,0:T(8,128)(2,1)S(1)}, bf16[16,4096]{1,0:T(8,128)(2,1)S(1)}, u32[]{:S(2)}, u32[]{:S(2)}) collective-permute-start(bf16[16,4096]{1,0:T(8,128)(2,1)S(1)} %constant_dynamic-slice_fusion.2), channel_id=1, source_target_pairs={{0,8},{1,9},{2,10},{3,11},{4,12},{5,13},{6,14},{7,15},{8,0},{9,1},... | collective-permute-start | bytes 393224 | tf_op jit(solution)/shard_map/ppermute | solution.py:23
  21.1 1.5 %collective-permute-start.16 = (bf16[576,128]{1,0:T(8,128)(2,1)S(1)}, bf16[576,128]{1,0:T(8,128)(2,1)S(1)}, u32[]{:S(2)}, u32[]{:S(2)}) collective-permute-start(bf16[576,128]{1,0:T(8,128)(2,1)S(1)} %pad_maximum_fusion.refs_13_), channel_id=1, source_target_pairs={{0,16},{1,17},{2,18},{3,19},{4,20},{5,21},{6,22},{7,23},{8,24},{9,... | collective-permute-start | bytes 442376 | tf_op jit(solution)/shard_map/ppermute | solution.py:23
  22.6 4.7 %collective-permute-done.refs_1_ = bf16[16,4096]{1,0:T(8,128)(2,1)S(1)} collective-permute-done((bf16[16,4096]{1,0:T(8,128)(2,1)S(1)}, bf16[16,4096]{1,0:T(8,128)(2,1)S(1)}, u32[]{:S(2)}, u32[]{:S(2)}) %collective-permute-start) | collective-permute-done | bytes 131104 | tf_op jit(solution)/shard_map/ppermute | solution.py:23
  27.3 1.5 %collective-permute-start.3 = (bf16[16,4096]{1,0:T(8,128)(2,1)S(1)}, bf16[16,4096]{1,0:T(8,128)(2,1)S(1)}, u32[]{:S(2)}, u32[]{:S(2)}) collective-permute-start(bf16[16,4096]{1,0:T(8,128)(2,1)S(1)} %collective-permute-done.1.refs_2_), channel_id=1, source_target_pairs={{0,16},{1,17},{2,18},{3,19},{4,20},{5,21},{6,22},{7,23},{8,24},{9,... | collective-permute-start | bytes 393224 | tf_op jit(solution)/shard_map/ppermute | solution.py:23
  29.4 1.6 %collective-permute-start.5 = (bf16[16,4096]{1,0:T(8,128)(2,1)S(1)}, bf16[16,4096]{1,0:T(8,128)(2,1)S(1)}, u32[]{:S(2)}, u32[]{:S(2)}) collective-permute-start(bf16[16,4096]{1,0:T(8,128)(2,1)S(1)} %collective-permute-done.refs_1_), channel_id=1, source_target_pairs={{0,2},{1,3},{2,0},{3,1},{4,6},{5,7},{6,4},{7,5},{8,10},{9,11},{10,... | collective-permute-start | bytes 393224 | tf_op jit(solution)/shard_map/ppermute | solution.py:23
  30.9 1.8 %collective-permute-done.3.refs_4_ = bf16[16,4096]{1,0:T(8,128)(2,1)S(1)} collective-permute-done((bf16[16,4096]{1,0:T(8,128)(2,1)S(1)}, bf16[16,4096]{1,0:T(8,128)(2,1)S(1)}, u32[]{:S(2)}, u32[]{:S(2)}) %collective-permute-start.3) | collective-permute-done | bytes 131104 | tf_op jit(solution)/shard_map/ppermute | solution.py:23
  32.8 1.5 %collective-permute-start.4 = (bf16[16,4096]{1,0:T(8,128)(2,1)S(1)}, bf16[16,4096]{1,0:T(8,128)(2,1)S(1)}, u32[]{:S(2)}, u32[]{:S(2)}) collective-permute-start(bf16[16,4096]{1,0:T(8,128)(2,1)S(1)} %collective-permute-done.refs_1_), channel_id=1, source_target_pairs={{0,16},{1,17},{2,18},{3,19},{4,20},{5,21},{6,22},{7,23},{8,24},{9,... | collective-permute-start | bytes 393224 | tf_op jit(solution)/shard_map/ppermute | solution.py:23
  34.3 1.5 %collective-permute-start.9 = (bf16[16,4096]{1,0:T(8,128)(2,1)S(1)}, bf16[16,4096]{1,0:T(8,128)(2,1)S(1)}, u32[]{:S(2)}, u32[]{:S(2)}) collective-permute-start(bf16[16,4096]{1,0:T(8,128)(2,1)S(1)} %collective-permute-done.6.refs_7_), channel_id=1, source_target_pairs={{0,2},{1,3},{2,0},{3,1},{4,6},{5,7},{6,4},{7,5},{8,10},{9,11},{10,... | collective-permute-start | bytes 393224 | tf_op jit(solution)/shard_map/ppermute | solution.py:23
  35.8 5.2 %collective-permute-done.5.refs_6_ = bf16[16,4096]{1,0:T(8,128)(2,1)S(1)} collective-permute-done((bf16[16,4096]{1,0:T(8,128)(2,1)S(1)}, bf16[16,4096]{1,0:T(8,128)(2,1)S(1)}, u32[]{:S(2)}, u32[]{:S(2)}) %collective-permute-start.5) | collective-permute-done | bytes 131104 | tf_op jit(solution)/shard_map/ppermute | solution.py:23
  42.1 1.5 %collective-permute-start.10 = (bf16[16,4096]{1,0:T(8,128)(2,1)S(1)}, bf16[16,4096]{1,0:T(8,128)(2,1)S(1)}, u32[]{:S(2)}, u32[]{:S(2)}) collective-permute-start(bf16[16,4096]{1,0:T(8,128)(2,1)S(1)} %collective-permute-done.5.refs_6_), channel_id=1, source_target_pairs={{0,16},{1,17},{2,18},{3,19},{4,20},{5,21},{6,22},{7,23},{8,24},{9,... | collective-permute-start | bytes 393224 | tf_op jit(solution)/shard_map/ppermute | solution.py:23
  43.7 2.4 %collective-permute-done.8.refs_9_ = bf16[16,4096]{1,0:T(8,128)(2,1)S(1)} collective-permute-done((bf16[16,4096]{1,0:T(8,128)(2,1)S(1)}, bf16[16,4096]{1,0:T(8,128)(2,1)S(1)}, u32[]{:S(2)}, u32[]{:S(2)}) %collective-permute-start.8) | collective-permute-done | bytes 131104 | tf_op jit(solution)/shard_map/ppermute | solution.py:23
  46.0 1.4 %collective-permute-done.10.refs_11_ = bf16[16,4096]{1,0:T(8,128)(2,1)S(1)} collective-permute-done((bf16[16,4096]{1,0:T(8,128)(2,1)S(1)}, bf16[16,4096]{1,0:T(8,128)(2,1)S(1)}, u32[]{:S(2)}, u32[]{:S(2)}) %collective-permute-start.10) | collective-permute-done | bytes 131104 | tf_op jit(solution)/shard_map/ppermute | solution.py:23
  48.0 1.1 %collective-permute-start.11 = (bf16[16,4096]{1,0:T(8,128)(2,1)S(1)}, bf16[16,4096]{1,0:T(8,128)(2,1)S(1)}, u32[]{:S(2)}, u32[]{:S(2)}) collective-permute-start(bf16[16,4096]{1,0:T(8,128)(2,1)S(1)} %collective-permute-done.9.refs_10_), channel_id=1, source_target_pairs={{0,16},{1,17},{2,18},{3,19},{4,20},{5,21},{6,22},{7,23},{8,24},{9,... | collective-permute-start | bytes 393224 | tf_op jit(solution)/shard_map/ppermute | solution.py:23
  49.1 4.3 %collective-permute-done.11.refs_12_ = bf16[16,4096]{1,0:T(8,128)(2,1)S(1)} collective-permute-done((bf16[16,4096]{1,0:T(8,128)(2,1)S(1)}, bf16[16,4096]{1,0:T(8,128)(2,1)S(1)}, u32[]{:S(2)}, u32[]{:S(2)}) %collective-permute-start.11) | collective-permute-done | bytes 131104 | tf_op jit(solution)/shard_map/ppermute | solution.py:23
  53.5 1.6 %copy-done.1 = bf16[256,4096]{1,0:T(8,128)(2,1)S(1)} copy-done((bf16[256,4096]{1,0:T(8,128)(2,1)S(1)}, bf16[256,4096]{1,0:T(8,128)(2,1)}, u32[]{:S(2)}) %copy-start.1) | copy-done | bytes 2097176
  56.0 10.2 %project.1 = (bf16[256,256]{1,0:T(8,128)(2,1)S(1)}, bf16[256,256]{1,0:T(8,128)(2,1)S(1)}, bf16[32,4096]{1,0:T(8,128)(2,1)}) custom-call(bf16[32,4096]{1,0:T(8,128)(2,1)S(1)} %copy-done.2, bf16[16,4096]{1,0:T(8,128)(2,1)S(1)} %collective-permute-done.refs_1_, bf16[16,4096]{1,0:T(8,128)(2,1)S(1)} %collective-permute-done.1.refs_2_, ...), custom_call_target="tpu_custom_call" | custom-call | tf_op jit(solution)/shard_map/project/pallas_call | solution.py:164
  66.8 1.3 %collective-permute-done.24.other_ref = bf16[256,256]{1,0:T(8,128)(2,1)S(1)} collective-permute-done((bf16[256,256]{1,0:T(8,128)(2,1)S(1)}, bf16[256,256]{1,0:T(8,128)(2,1)S(1)}, u32[]{:S(2)}, u32[]{:S(2)}) %collective-permute-start.24) | collective-permute-done | bytes 131104 | tf_op jit(solution)/shard_map/ppermute | solution.py:23
  68.8 2.0 %join.1 = bf16[256,512]{1,0:T(8,128)(2,1)} custom-call(bf16[256,256]{1,0:T(8,128)(2,1)} %copy-done.3, bf16[256,256]{1,0:T(8,128)(2,1)} %copy-done.4), custom_call_target="tpu_custom_call" | custom-call | tf_op jit(solution)/shard_map/join/pallas_call | solution.py:185
  (46 shorter events, 8.9 us)
Async XLA Ops:
  0.6 52.8 %collective-permute-start.23 = (bf16[256,4096]{1,0:T(8,128)(2,1)}, bf16[256,4096]{1,0:T(8,128)(2,1)S(1)}, u32[]{:S(2)}, u32[]{:S(2)}) collective-permute-start(bf16[256,4096]{1,0:T(8,128)(2,1)} %refs_21_.1), channel_id=1, source_target_pairs={{0,1},{1,0},{2,3},{3,2},{4,5},{5,4},{6,7},{7,6},{8,9},{9,8},{10,11... | collective-permute-start | bytes 6291464 | tf_op jit(solution)/shard_map/ppermute | solution.py:23
  2.8 5.5 %collective-permute-start.12 = (f32[144,128]{1,0:T(8,128)S(1)}, f32[144,128]{1,0:T(8,128)S(1)}, u32[]{:S(2)}, u32[]{:S(2)}) collective-permute-start(f32[144,128]{1,0:T(8,128)S(1)} %pad_maximum_fusion.1), channel_id=1, source_target_pairs={{0,16},{1,17},{2,18},{3,19},{4,20},{5,21},{6,22},{7,23},{8,24},{9,... | collective-permute-start | bytes 221192 | tf_op jit(solution)/shard_map/ppermute | solution.py:23
  8.3 6.9 %collective-permute-start.15 = (bf16[144,128]{1,0:T(8,128)(2,1)S(1)}, bf16[144,128]{1,0:T(8,128)(2,1)S(1)}, u32[]{:S(2)}, u32[]{:S(2)}) collective-permute-start(bf16[144,128]{1,0:T(8,128)(2,1)S(1)} %fusion), channel_id=1, source_target_pairs={{0,12},{1,13},{2,14},{3,15},{4,8},{5,9},{6,10},{7,11},{8,4},{9,5},... | collective-permute-start | bytes 110600 | tf_op jit(solution)/shard_map/ppermute | solution.py:23
  12.2 5.0 %collective-permute-start.14 = (bf16[144,128]{1,0:T(8,128)(2,1)S(1)}, bf16[144,128]{1,0:T(8,128)(2,1)S(1)}, u32[]{:S(2)}, u32[]{:S(2)}) collective-permute-start(bf16[144,128]{1,0:T(8,128)(2,1)S(1)} %fusion), channel_id=1, source_target_pairs={{0,8},{1,9},{2,10},{3,11},{4,12},{5,13},{6,14},{7,15},{8,0},{9,1},... | collective-permute-start | bytes 110600 | tf_op jit(solution)/shard_map/ppermute | solution.py:23
  12.2 5.0 %collective-permute-start.13 = (bf16[144,128]{1,0:T(8,128)(2,1)S(1)}, bf16[144,128]{1,0:T(8,128)(2,1)S(1)}, u32[]{:S(2)}, u32[]{:S(2)}) collective-permute-start(bf16[144,128]{1,0:T(8,128)(2,1)S(1)} %fusion), channel_id=1, source_target_pairs={{0,4},{1,5},{2,6},{3,7},{4,0},{5,1},{6,2},{7,3},{8,12},{9,13},{10,... | collective-permute-start | bytes 110600 | tf_op jit(solution)/shard_map/ppermute | solution.py:23
  13.8 7.4 %collective-permute-start.1 = (bf16[16,4096]{1,0:T(8,128)(2,1)S(1)}, bf16[16,4096]{1,0:T(8,128)(2,1)S(1)}, u32[]{:S(2)}, u32[]{:S(2)}) collective-permute-start(bf16[16,4096]{1,0:T(8,128)(2,1)S(1)} %constant_dynamic-slice_fusion.2), channel_id=1, source_target_pairs={{0,4},{1,5},{2,6},{3,7},{4,0},{5,1},{6,2},{7,3},{8,12},{9,13},{10,... | collective-permute-start | bytes 393224 | tf_op jit(solution)/shard_map/ppermute | solution.py:23
  17.2 11.7 %collective-permute-start.19 = (bf16[576,128]{1,0:T(8,128)(2,1)S(1)}, bf16[576,128]{1,0:T(8,128)(2,1)S(1)}, u32[]{:S(2)}, u32[]{:S(2)}) collective-permute-start(bf16[576,128]{1,0:T(8,128)(2,1)S(1)} %pad_maximum_fusion.refs_13_), channel_id=1, source_target_pairs={{0,1},{1,0},{2,3},{3,2},{4,5},{5,4},{6,7},{7,6},{8,9},{9,8},{10,11... | collective-permute-start | bytes 442376 | tf_op jit(solution)/shard_map/ppermute | solution.py:23
  17.3 12.1 %collective-permute-start.17 = (bf16[576,128]{1,0:T(8,128)(2,1)S(1)}, bf16[576,128]{1,0:T(8,128)(2,1)S(1)}, u32[]{:S(2)}, u32[]{:S(2)}) collective-permute-start(bf16[576,128]{1,0:T(8,128)(2,1)S(1)} %pad_maximum_fusion.refs_13_), channel_id=1, source_target_pairs={{0,2},{1,3},{2,0},{3,1},{4,6},{5,7},{6,4},{7,5},{8,10},{9,11},{10,... | collective-permute-start | bytes 442376 | tf_op jit(solution)/shard_map/ppermute | solution.py:23
  18.9 8.5 %collective-permute-start = (bf16[16,4096]{1,0:T(8,128)(2,1)S(1)}, bf16[16,4096]{1,0:T(8,128)(2,1)S(1)}, u32[]{:S(2)}, u32[]{:S(2)}) collective-permute-start(bf16[16,4096]{1,0:T(8,128)(2,1)S(1)} %constant_dynamic-slice_fusion.2), channel_id=1, source_target_pairs={{0,8},{1,9},{2,10},{3,11},{4,12},{5,13},{6,14},{7,15},{8,0},{9,1},... | collective-permute-start | bytes 393224 | tf_op jit(solution)/shard_map/ppermute | solution.py:23
  21.1 8.2 %collective-permute-start.16 = (bf16[576,128]{1,0:T(8,128)(2,1)S(1)}, bf16[576,128]{1,0:T(8,128)(2,1)S(1)}, u32[]{:S(2)}, u32[]{:S(2)}) collective-permute-start(bf16[576,128]{1,0:T(8,128)(2,1)S(1)} %pad_maximum_fusion.refs_13_), channel_id=1, source_target_pairs={{0,16},{1,17},{2,18},{3,19},{4,20},{5,21},{6,22},{7,23},{8,24},{9,... | collective-permute-start | bytes 442376 | tf_op jit(solution)/shard_map/ppermute | solution.py:23
  27.3 5.4 %collective-permute-start.3 = (bf16[16,4096]{1,0:T(8,128)(2,1)S(1)}, bf16[16,4096]{1,0:T(8,128)(2,1)S(1)}, u32[]{:S(2)}, u32[]{:S(2)}) collective-permute-start(bf16[16,4096]{1,0:T(8,128)(2,1)S(1)} %collective-permute-done.1.refs_2_), channel_id=1, source_target_pairs={{0,16},{1,17},{2,18},{3,19},{4,20},{5,21},{6,22},{7,23},{8,24},{9,... | collective-permute-start | bytes 393224 | tf_op jit(solution)/shard_map/ppermute | solution.py:23
  28.8 13.3 %collective-permute-start.2 = (bf16[32,4096]{1,0:T(8,128)(2,1)}, bf16[32,4096]{1,0:T(8,128)(2,1)S(1)}, u32[]{:S(2)}, u32[]{:S(2)}) collective-permute-start(bf16[32,4096]{1,0:T(8,128)(2,1)} %refs_0_.1), channel_id=1, source_target_pairs={{0,2},{1,3},{2,0},{3,1},{4,6},{5,7},{6,4},{7,5},{8,10},{9,11},{10,... | collective-permute-start | bytes 786440 | tf_op jit(solution)/shard_map/ppermute | solution.py:23
  29.4 5.0 %collective-permute-start.6 = (bf16[16,4096]{1,0:T(8,128)(2,1)S(1)}, bf16[16,4096]{1,0:T(8,128)(2,1)S(1)}, u32[]{:S(2)}, u32[]{:S(2)}) collective-permute-start(bf16[16,4096]{1,0:T(8,128)(2,1)S(1)} %collective-permute-done.refs_1_), channel_id=1, source_target_pairs={{0,4},{1,5},{2,6},{3,7},{4,0},{5,1},{6,2},{7,3},{8,12},{9,13},{10,... | collective-permute-start | bytes 393224 | tf_op jit(solution)/shard_map/ppermute | solution.py:23
  29.4 11.7 %collective-permute-start.5 = (bf16[16,4096]{1,0:T(8,128)(2,1)S(1)}, bf16[16,4096]{1,0:T(8,128)(2,1)S(1)}, u32[]{:S(2)}, u32[]{:S(2)}) collective-permute-start(bf16[16,4096]{1,0:T(8,128)(2,1)S(1)} %collective-permute-done.refs_1_), channel_id=1, source_target_pairs={{0,2},{1,3},{2,0},{3,1},{4,6},{5,7},{6,4},{7,5},{8,10},{9,11},{10,... | collective-permute-start | bytes 393224 | tf_op jit(solution)/shard_map/ppermute | solution.py:23
  32.8 8.8 %collective-permute-start.4 = (bf16[16,4096]{1,0:T(8,128)(2,1)S(1)}, bf16[16,4096]{1,0:T(8,128)(2,1)S(1)}, u32[]{:S(2)}, u32[]{:S(2)}) collective-permute-start(bf16[16,4096]{1,0:T(8,128)(2,1)S(1)} %collective-permute-done.refs_1_), channel_id=1, source_target_pairs={{0,16},{1,17},{2,18},{3,19},{4,20},{5,21},{6,22},{7,23},{8,24},{9,... | collective-permute-start | bytes 393224 | tf_op jit(solution)/shard_map/ppermute | solution.py:23
  34.3 9.3 %collective-permute-start.9 = (bf16[16,4096]{1,0:T(8,128)(2,1)S(1)}, bf16[16,4096]{1,0:T(8,128)(2,1)S(1)}, u32[]{:S(2)}, u32[]{:S(2)}) collective-permute-start(bf16[16,4096]{1,0:T(8,128)(2,1)S(1)} %collective-permute-done.6.refs_7_), channel_id=1, source_target_pairs={{0,2},{1,3},{2,0},{3,1},{4,6},{5,7},{6,4},{7,5},{8,10},{9,11},{10,... | collective-permute-start | bytes 393224 | tf_op jit(solution)/shard_map/ppermute | solution.py:23
  41.1 5.0 %collective-permute-start.8 = (bf16[16,4096]{1,0:T(8,128)(2,1)S(1)}, bf16[16,4096]{1,0:T(8,128)(2,1)S(1)}, u32[]{:S(2)}, u32[]{:S(2)}) collective-permute-start(bf16[16,4096]{1,0:T(8,128)(2,1)S(1)} %collective-permute-done.6.refs_7_), channel_id=1, source_target_pairs={{0,16},{1,17},{2,18},{3,19},{4,20},{5,21},{6,22},{7,23},{8,24},{9,... | collective-permute-start | bytes 393224 | tf_op jit(solution)/shard_map/ppermute | solution.py:23
  41.6 5.8 %collective-permute-start.18 = (bf16[576,128]{1,0:T(8,128)(2,1)S(1)}, bf16[576,128]{1,0:T(8,128)(2,1)S(1)}, u32[]{:S(2)}, u32[]{:S(2)}) collective-permute-start(bf16[576,128]{1,0:T(8,128)(2,1)S(1)} %collective-permute-done.16.refs_14_), channel_id=1, source_target_pairs={{0,2},{1,3},{2,0},{3,1},{4,6},{5,7},{6,4},{7,5},{8,10},{9,11},{10,... | collective-permute-start | bytes 442376 | tf_op jit(solution)/shard_map/ppermute | solution.py:23
  42.1 5.3 %collective-permute-start.10 = (bf16[16,4096]{1,0:T(8,128)(2,1)S(1)}, bf16[16,4096]{1,0:T(8,128)(2,1)S(1)}, u32[]{:S(2)}, u32[]{:S(2)}) collective-permute-start(bf16[16,4096]{1,0:T(8,128)(2,1)S(1)} %collective-permute-done.5.refs_6_), channel_id=1, source_target_pairs={{0,16},{1,17},{2,18},{3,19},{4,20},{5,21},{6,22},{7,23},{8,24},{9,... | collective-permute-start | bytes 393224 | tf_op jit(solution)/shard_map/ppermute | solution.py:23
  43.7 4.3 %collective-permute-start.21 = (bf16[576,128]{1,0:T(8,128)(2,1)S(1)}, bf16[576,128]{1,0:T(8,128)(2,1)S(1)}, u32[]{:S(2)}, u32[]{:S(2)}) collective-permute-start(bf16[576,128]{1,0:T(8,128)(2,1)S(1)} %collective-permute-done.17.refs_15_), channel_id=1, source_target_pairs={{0,1},{1,0},{2,3},{3,2},{4,5},{5,4},{6,7},{7,6},{8,9},{9,8},{10,11... | collective-permute-start | bytes 442376 | tf_op jit(solution)/shard_map/ppermute | solution.py:23
  46.0 7.4 %collective-permute-start.7 = (bf16[32,4096]{1,0:T(8,128)(2,1)S(1)}, bf16[32,4096]{1,0:T(8,128)(2,1)S(1)}, u32[]{:S(2)}, u32[]{:S(2)}) collective-permute-start(bf16[32,4096]{1,0:T(8,128)(2,1)S(1)} %collective-permute-done.2.refs_3_), channel_id=1, source_target_pairs={{0,4},{1,5},{2,6},{3,7},{4,0},{5,1},{6,2},{7,3},{8,12},{9,13},{10,... | collective-permute-start | bytes 786440 | tf_op jit(solution)/shard_map/ppermute | solution.py:23
  47.4 1.7 %collective-permute-start.20 = (bf16[576,128]{1,0:T(8,128)(2,1)S(1)}, bf16[576,128]{1,0:T(8,128)(2,1)S(1)}, u32[]{:S(2)}, u32[]{:S(2)}) collective-permute-start(bf16[576,128]{1,0:T(8,128)(2,1)S(1)} %collective-permute-done.16.refs_14_), channel_id=1, source_target_pairs={{0,1},{1,0},{2,3},{3,2},{4,5},{5,4},{6,7},{7,6},{8,9},{9,8},{10,11... | collective-permute-start | bytes 442376 | tf_op jit(solution)/shard_map/ppermute | solution.py:23
  47.4 6.0 %collective-permute-start.22 = (bf16[576,128]{1,0:T(8,128)(2,1)S(1)}, bf16[576,128]{1,0:T(8,128)(2,1)S(1)}, u32[]{:S(2)}, u32[]{:S(2)}) collective-permute-start(bf16[576,128]{1,0:T(8,128)(2,1)S(1)} %collective-permute-done.18.refs_16_), channel_id=1, source_target_pairs={{0,1},{1,0},{2,3},{3,2},{4,5},{5,4},{6,7},{7,6},{8,9},{9,8},{10,11... | collective-permute-start | bytes 442376 | tf_op jit(solution)/shard_map/ppermute | solution.py:23
  48.0 5.5 %collective-permute-start.11 = (bf16[16,4096]{1,0:T(8,128)(2,1)S(1)}, bf16[16,4096]{1,0:T(8,128)(2,1)S(1)}, u32[]{:S(2)}, u32[]{:S(2)}) collective-permute-start(bf16[16,4096]{1,0:T(8,128)(2,1)S(1)} %collective-permute-done.9.refs_10_), channel_id=1, source_target_pairs={{0,16},{1,17},{2,18},{3,19},{4,20},{5,21},{6,22},{7,23},{8,24},{9,... | collective-permute-start | bytes 393224 | tf_op jit(solution)/shard_map/ppermute | solution.py:23
  (6 other events, 9.9 us)

commit v2 on v0

v2 whole, which is shorter than its diff:
```python
import functools

import jax
import jax.numpy as jnp
from jax import lax
from jax.experimental import pallas as pl
from jax.experimental.pallas import tpu as pltpu
from jax.sharding import PartitionSpec as P

step_size = 0.5
AXES = ("rep", "fsdp")
NT = (((1,), (1,)), ((), ()))
NN = (((1,), (0,)), ((), ()))
VMEM_LIMIT = 16 * 1024 * 1024
WIDE_LIMIT = 58 * 1024 * 1024
S_FLOPS = 4e9
U_FLOPS = 4e9
W_FLOPS = 1
M_FLOPS = 1


def dot(a, b, dims):
    return lax.dot_general(a, b, dims, preferred_element_type=jnp.float32)


def general(hidden, weight, adapter_a, adapter_b, grad_a, grad_b):
    replicas = lax.axis_size("rep")
    summed = lax.psum((grad_a[0], grad_b[0]), "rep")
    new_a = adapter_a - step_size * (summed[0] / replicas)
    new_b = adapter_b - step_size * (summed[1] / replicas)
    full_a = lax.all_gather(new_a, "fsdp", axis=0, tiled=True)
    delta = lax.dot_general(new_b, full_a, NT, precision=lax.Precision.HIGHEST, preferred_element_type=jnp.float32)
    own_rows = (weight.astype(jnp.float32) + delta).astype(jnp.bfloat16)
    output = dot(hidden, lax.all_gather(own_rows, "fsdp", axis=0, tiled=True), NT)
    return output.astype(jnp.bfloat16), own_rows


CORE, Y, Z1, Z2 = (0, 1), (0, 2), (0, 4), (0, 8)
REPLICA, X = (1, 0), (1, 1)


def send(rows, group, move, other_move=None, name="sent"):
    reps, shards = group
    pairs = []
    for r in range(reps):
        for f in range(shards):
            dr, df = move if (f & 1) == r or other_move is None else other_move
            pairs.append((r * shards + f, (r ^ dr) * shards + (f ^ df)))
    with jax.named_scope(name):
        return lax.ppermute(rows, AXES, pairs)


HELD = (
    ((0, 0, 0), (0, 0, 1)),
    ((2, 0, 0), (1, 0, 1)),
    ((0, 1, 0), (0, 1, 1)),
    ((2, 0, 1), (1, 0, 0)),
    ((2, 1, 0), (1, 1, 1)),
    ((3, 0, 0), (3, 0, 1)),
    ((2, 1, 1), (1, 1, 0)),
    ((3, 1, 0), (3, 1, 1)),
)
SHARDS = (((0, 0), (2, 0)), ((1, 0), (3, 0)), ((0, 1), (2, 1)), ((1, 1), (3, 1)))


def position():
    x, f = lax.axis_index("rep"), lax.axis_index("fsdp")
    return x, f >> 1, f & 1


def flips_of(i, kind):
    first, second = HELD[i]
    return [a + kind * (b - a) for a, b in zip(first, second)]


def shard_of(flips):
    x, place, _ = position()
    return (place ^ (flips[0] * 2 + flips[1])) * 2 + (x ^ flips[2])


def update_kernel(replicas, old_ref, own_ref, oa_ref, ob_ref, ab_ref):
    rows_a = oa_ref.shape[1]
    ab_ref[:rows_a] = (old_ref[:rows_a] - step_size * ((own_ref[:rows_a] + oa_ref[0]) / replicas)).astype(jnp.bfloat16)
    ab_ref[rows_a:] = (old_ref[rows_a:] - step_size * ((own_ref[rows_a:] + ob_ref[0]) / replicas)).astype(jnp.bfloat16)


def weight_kernel(h_ref, hs_ref, *refs):
    *shard_refs, own_ref, other_ref, w_all = refs
    rows = shard_refs[0].shape[0]
    for i, ref in enumerate(shard_refs):
        w_all[i * rows : (i + 1) * rows] = ref[...]
    other_ref[...] = dot(hs_ref[...], w_all[...], NT)
    own_ref[...] = dot(h_ref[...], w_all[...], NT)


def placing(rows, n, m, kind):
    source = lax.broadcasted_iota(jnp.int32, (n, m), 0)
    target = lax.broadcasted_iota(jnp.int32, (n, m), 1)
    column = jnp.zeros((n, m), jnp.int32)
    for i in range(len(HELD)):
        shard = shard_of(flips_of(i, kind))
        column = jnp.where(source // rows == i, shard * rows, column)
    return (target == column + source % rows).astype(jnp.bfloat16)


def split_bf16(v):
    high = v.astype(jnp.bfloat16)
    return high, (v - high.astype(jnp.float32)).astype(jnp.bfloat16)


def add_blocks(h_ref, w_ref, b_own, merged_ref, b_all, blocks, t):
    x, place, core = position()
    rows_b = w_ref.shape[0]
    rows_a = h_ref.shape[1] * rows_b // b_all.shape[0]
    for ref, other, at in blocks:
        for j, (dz, dy) in enumerate(SHARDS[at]):
            shard = (place ^ (dz * 2 + dy)) * 2 + (core ^ other)
            row = j * (rows_a + rows_b)
            columns = pl.ds(pl.multiple_of(shard * rows_a, rows_a), rows_a)
            part = ref[row : row + rows_a]
            b_all[pl.ds(pl.multiple_of(shard * rows_b, rows_b), rows_b)] = ref[row + rows_a : row + rows_a + rows_b]
            t = t + dot(h_ref[:, columns], part, NN)
            merged_ref[:, columns] = (w_ref[:, columns].astype(jnp.float32) + dot(b_own, part, NT)).astype(jnp.bfloat16)
    return t


def middle_kernel(at, h_ref, w_ref, *refs):
    *ab_refs, t_ref, merged_ref, b_all = refs
    rows_b = w_ref.shape[0]
    rows_a = h_ref.shape[1] * rows_b // b_all.shape[0]
    b_own = ab_refs[0][rows_a : rows_a + rows_b]
    blocks = [(ref, i // len(at), at[i % len(at)]) for i, ref in enumerate(ab_refs)]
    t_ref[...] = add_blocks(h_ref, w_ref, b_own, merged_ref, b_all, blocks, jnp.zeros(t_ref.shape, jnp.float32))


def last_kernel(at, h_ref, w_ref, own_ref, received_ref, t_ref, m_ref, b_ref, first_ref, *refs):
    *ab_refs, out_ref, merged_ref, b_all = refs
    x, place, core = position()
    kind = core ^ x
    n, m = own_ref.shape[1], out_ref.shape[1]
    rows_b = w_ref.shape[0]
    rows_a = h_ref.shape[1] * rows_b // b_all.shape[0]
    b_own = first_ref[rows_a : rows_a + rows_b]
    merged_ref[...] = m_ref[...]
    b_all[...] = b_ref[...]
    blocks = [(ref, i // len(at), at[i % len(at)]) for i, ref in enumerate(ab_refs)]
    t = add_blocks(h_ref, w_ref, b_own, merged_ref, b_all, blocks, t_ref[...])
    out = jnp.zeros(out_ref.shape, jnp.float32)
    for part in split_bf16(t):
        out = out + dot(part, b_all[...], NT)
    for ref, which in ((own_ref, kind), (received_ref, 1 - kind)):
        columns = placing(rows_b, n, m, which)
        for part in split_bf16(ref[...]):
            out = out + dot(part, columns, NN)
    out_ref[...] = out.astype(jnp.bfloat16)


def cost(flops, number_of_bytes):
    return pl.CostEstimate(flops=int(flops), bytes_accessed=int(number_of_bytes), transcendentals=0)


def paired(hidden, weight, adapter_a, adapter_b, grad_a, grad_b):
    group = (lax.axis_size("rep"), lax.axis_size("fsdp"))
    tokens, depth = hidden.shape
    rank = adapter_a.shape[1]
    rows_a, rows_b = adapter_a.shape[0], weight.shape[0]
    outputs = rows_b * group[1]

    any_space = pl.BlockSpec(memory_space=pltpu.HBM)
    vmem = pl.BlockSpec(memory_space=pltpu.VMEM)
    params = pltpu.CompilerParams(vmem_limit_bytes=VMEM_LIMIT)
    wide = pltpu.CompilerParams(vmem_limit_bytes=WIDE_LIMIT)
    bf16, f32 = jnp.bfloat16, jnp.float32

    w0 = weight
    other_a = send(grad_a, group, REPLICA, name="other_a")
    other_b = send(grad_b, group, REPLICA, name="other_b")
    w1 = send(w0, group, Z2, Z1, name="w1")
    w2 = send(w0, group, Y, name="w2")
    w1, w2 = lax.optimization_barrier((w1, w2))
    other_hidden = send(hidden, group, CORE, name="other_hidden")
    old, mine = lax.optimization_barrier((jnp.concatenate([adapter_a, adapter_b]), jnp.concatenate([grad_a[0], grad_b[0]])))
    h_here, w_here = hidden, weight
    ab = pl.pallas_call(
        functools.partial(update_kernel, group[0]),
        out_shape=jax.ShapeDtypeStruct((rows_a + rows_b, rank), bf16),
        in_specs=[vmem] * 4,
        out_specs=vmem,
        compiler_params=params,
        cost_estimate=cost(U_FLOPS, 8 * rank * rows_a),
        name="update",
    )(old, mine, other_a, other_b)
    ab_far = send(ab, group, Z2, name="ab_far")
    w1, _ = lax.optimization_barrier((w1, ab))
    w3 = send(w1, group, X, name="w3")
    w4 = send(w1, group, Y, name="w4")
    w5 = send(w1, group, Z1, Z2, name="w5")
    ab_0 = jnp.concatenate([ab, ab_far])
    ab_1 = send(ab_0, group, Z1, name="ab_1")
    ab_2 = send(ab_0, group, Y, name="ab_2")
    w3, w4, w5 = lax.optimization_barrier((w3, w4, w5))
    w6 = send(w4, group, X, name="w6")
    w7 = send(w4, group, Z1, Z2, name="w7")
    ab_3 = send(ab_1, group, Y, name="ab_3")
    held = [w0, w1, w2, w3, w4, w5, w6, w7]
    other_0 = send(ab_0, group, CORE, name="other_0")
    other_1 = send(ab_1, group, CORE, name="other_1")
    other_2 = send(ab_2, group, CORE, name="other_2")
    other_3 = send(ab_3, group, CORE, name="other_3")
    held, other_0, other_1, other_2 = lax.optimization_barrier((held, other_0, other_1, other_2))

    columns = outputs // 2
    held[0] = w_here
    own, other = pl.pallas_call(
        weight_kernel,
        out_shape=[jax.ShapeDtypeStruct((tokens, columns), f32)] * 2,
        in_specs=[vmem] * (2 + len(held)),
        out_specs=[vmem] * 2,
        scratch_shapes=[pltpu.VMEM((columns, depth), bf16)],
        compiler_params=params,
        cost_estimate=cost(W_FLOPS * 2 * tokens * outputs * depth, 2 * depth * (2 * tokens + columns)),
        name="weight_product",
    )(h_here, other_hidden, *held)
    received = send(other, group, CORE, name="received")
    middle = (0, 1, 2)
    t, merged, b_all = pl.pallas_call(
        functools.partial(middle_kernel, middle),
        out_shape=[
            jax.ShapeDtypeStruct((tokens, rank), f32),
            jax.ShapeDtypeStruct(weight.shape, bf16),
            jax.ShapeDtypeStruct((outputs, rank), bf16),
        ],
        in_specs=[vmem] * (2 + 2 * len(middle)),
        out_specs=[vmem] * 3,
        compiler_params=params,
        cost_estimate=cost(M_FLOPS * 2 * tokens * rank * depth, 2 * depth * (tokens + rank)),
        name="middle",
    )(h_here, w_here, ab_0, ab_1, ab_2, other_0, other_1, other_2)
    return tuple(pl.pallas_call(
        functools.partial(last_kernel, (3,)),
        out_shape=[
            jax.ShapeDtypeStruct((tokens, outputs), bf16),
            jax.ShapeDtypeStruct(weight.shape, bf16),
        ],
        in_specs=[vmem] * 10,
        out_specs=[vmem] * 2,
        scratch_shapes=[pltpu.VMEM((outputs, rank), bf16)],
        compiler_params=params,
        cost_estimate=cost(2 * tokens * rank * outputs, 2 * outputs * tokens),
        name="last",
    )(h_here, w_here, own, received, t, merged, b_all, ab_0, ab_3, other_3))


def solution(mesh):
    paired_fits = mesh.shape["rep"] == 2 and mesh.shape["fsdp"] == 16
    return jax.shard_map(
        paired if paired_fits else general,
        mesh=mesh,
        in_specs=(
            P(("rep", "fsdp"), None),
            P("fsdp", None),
            P("fsdp", None),
            P("fsdp", None),
            P("rep", "fsdp", None),
            P("rep", "fsdp", None),
        ),
        out_specs=(P(("rep", "fsdp"), None), P("fsdp", None)),
        check_vma=False,
    )
```

time: 144 us -> 40.9 us (0.28)
  waiting for transfers between devices: 112 us -> 17.9 us
  starting transfers between devices: 0.12 us -> 16.1 us
  between operations: 13.8 us -> 0.71 us
  matrix products: 7.93 us -> 0 us
  blocking collectives: 7.48 us -> 0 us
  Pallas kernels: 0 us -> 3.58 us
    all_gather x2 -> x0, waiting for transfers between devices: 84.6 us -> none  [the longest x1 49.6 us: shards(): lax.all_gather(own_rows, 'fsdp', axis=0, tiled=True)]
    psum x1 -> x0, waiting for transfers between devices: 26.5 us -> none  [shards(): summed = lax.psum((grad_a[0], grad_b[0]), 'rep')]
    ppermute x0 -> x19, waiting for transfers between devices: none -> 17.9 us  [send(): return lax.ppermute(rows, AXES, pairs)]
    ppermute x0 -> x19, starting transfers between devices: none -> 16.1 us  [send(): return lax.ppermute(rows, AXES, pairs)]
    dot_general x2 -> x0, matrix products: 7.93 us -> none  [the longest x1 4.46 us: low_rank(): lax.dot_general(b_rows, full_a, (((1,), (1,)), ((), ())), precision=lax.P...]
    psum x1 -> x0, blocking collectives: 7.48 us -> none  [shards(): summed = lax.psum((grad_a[0], grad_b[0]), 'rep')]
    pallas_call x0 -> x4, Pallas kernels: none -> 3.58 us  [the longest x1 1.58 us: paired(): pl.pallas_call(functools.partial(last_kernel, (3,)), out_shape=[jax.Shape...]
    concatenate x0 -> x3, other arithmetic: none -> 1.88 us  [the longest x1 0.93 us: paired(): jnp.concatenate([grad_a[0], grad_b[0]])]
  transfers between devices with their start and end apart: 3 -> 19, of which waited for: 3 -> 10; matrix products, arithmetic and copies ran while one was open for 0% -> 5% of each run, Pallas kernels for 0% -> 5%
where the time goes in v2:
time: 40.9 us; the launch traced here: 40.2 us
  waiting for transfers between devices  17.9 us (44%)
  starting transfers between devices  16.1 us (39%)
  Pallas kernels  3.58 us (9%)
  other arithmetic  1.88 us (5%)
  between operations  0.71 us (2%)
    ppermute x19, waiting for transfers between devices, send(): return lax.ppermute(rows, AXES, pairs)  17.9 us
    ppermute x19, starting transfers between devices, send(): return lax.ppermute(rows, AXES, pairs)  16.1 us
    pallas_call x1, Pallas kernels, paired(): pl.pallas_call(functools.partial(last_kernel, (3,)), out_shape=[jax.Shape...  1.58 us
    pallas_call x1, Pallas kernels, paired(): pl.pallas_call(weight_kernel, out_shape=[jax.ShapeDtypeStruct((tokens, co...  1.28 us
    concatenate x1, other arithmetic, paired(): jnp.concatenate([grad_a[0], grad_b[0]])  0.93 us
    concatenate x1, other arithmetic, paired(): jnp.concatenate([adapter_a, adapter_b])  0.93 us
  transfers between devices with their start and end apart: 19, of which 10 were waited for; matrix products, arithmetic and copies ran while one was open for 5% of the time, Pallas kernels for 5%

profile of v2, /device:TPU:0, one launch (start us, length us, event | category | flops | bytes accessed | tf_op | source)
XLA Modules:
  0.0 40.2 jit_solution(6509392535884565233)
XLA Ops:
  0.6 0.5 %collective-permute-start = (bf16[256,4096]{1,0:T(8,128)(2,1)}, bf16[256,4096]{1,0:T(8,128)(2,1)S(1)}, u32[]{:S(2)}, u32[]{:S(2)}) collective-permute-start(bf16[256,4096]{1,0:T(8,128)(2,1)} %h_ref.5), channel_id=1, source_target_pairs={{0,1},{1,0},{2,3},{3,2},{4,5},{5,4},{6,7},{7,6},{8,9},{9,8},{10,11... | collective-permute-start | bytes 6291464 | tf_op jit(solution)/shard_map/other_hidden/ppermute | solution.py:50
  1.1 3.7 %collective-permute-start.1 = (bf16[32,4096]{1,0:T(8,128)(2,1)}, bf16[32,4096]{1,0:T(8,128)(2,1)S(1)}, u32[]{:S(2)}, u32[]{:S(2)}) collective-permute-start(bf16[32,4096]{1,0:T(8,128)(2,1)} %w_ref.3), channel_id=1, source_target_pairs={{0,8},{1,5},{2,10},{3,7},{4,12},{5,1},{6,14},{7,3},{8,0},{9,13},{1... | collective-permute-start | bytes 786440 | tf_op jit(solution)/shard_map/w1/ppermute | solution.py:50
  4.8 1.5 %collective-permute-start.2 = (bf16[32,4096]{1,0:T(8,128)(2,1)}, bf16[32,4096]{1,0:T(8,128)(2,1)S(1)}, u32[]{:S(2)}, u32[]{:S(2)}) collective-permute-start(bf16[32,4096]{1,0:T(8,128)(2,1)} %w_ref.3), channel_id=1, source_target_pairs={{0,2},{1,3},{2,0},{3,1},{4,6},{5,7},{6,4},{7,5},{8,10},{9,11},{10,... | collective-permute-start | bytes 786440 | tf_op jit(solution)/shard_map/w2/ppermute | solution.py:50
  6.8 1.5 %collective-permute-start.4 = (f32[1,32,128]{2,1,0:T(8,128)}, f32[1,32,128]{2,1,0:T(8,128)S(1)}, u32[]{:S(2)}, u32[]{:S(2)}) collective-permute-start(f32[1,32,128]{2,1,0:T(8,128)} %param.11), channel_id=1, source_target_pairs={{0,16},{1,17},{2,18},{3,19},{4,20},{5,21},{6,22},{7,23},{8,24},{9,... | collective-permute-start | bytes 49160 | tf_op jit(solution)/shard_map/other_b/ppermute | solution.py:50
  8.4 0.9 %pad_maximum_fusion.old_ref = f32[288,128]{1,0:T(8,128)S(1)} fusion(f32[32,128]{1,0:T(8,128)} %param.9, f32[256,128]{1,0:T(8,128)} %param.8), kind=kLoop, calls=%fused_computation | loop fusion | flops 36864 | bytes 294912 | tf_op jit(solution)/shard_map/concatenate | solution.py:182
  9.3 0.9 %pad_maximum_fusion.1.own_ref = f32[288,128]{1,0:T(8,128)S(1)} fusion(f32[32,128]{1,0:T(8,128)} %bitcast.3, f32[256,128]{1,0:T(8,128)} %bitcast.2), kind=kLoop, calls=%fused_computation.1 | loop fusion | flops 36864 | bytes 294912 | tf_op jit(solution)/shard_map/concatenate | solution.py:182
  10.3 1.7 %collective-permute-done.4.ob_ref = f32[1,32,128]{2,1,0:T(8,128)S(1)} collective-permute-done((f32[1,32,128]{2,1,0:T(8,128)}, f32[1,32,128]{2,1,0:T(8,128)S(1)}, u32[]{:S(2)}, u32[]{:S(2)}) %collective-permute-start.4) | collective-permute-done | bytes 16416 | tf_op jit(solution)/shard_map/other_b/ppermute | solution.py:50
  11.9 1.9 %collective-permute-start.10 = (bf16[288,128]{1,0:T(8,128)(2,1)S(1)}, bf16[288,128]{1,0:T(8,128)(2,1)S(1)}, u32[]{:S(2)}, u32[]{:S(2)}) collective-permute-start(bf16[288,128]{1,0:T(8,128)(2,1)S(1)} %update.1), channel_id=1, source_target_pairs={{0,8},{1,9},{2,10},{3,11},{4,12},{5,13},{6,14},{7,15},{8,0},{9,1},... | collective-permute-start | bytes 221192 | tf_op jit(solution)/shard_map/ab_far/ppermute | solution.py:50
  14.2 1.5 %collective-permute-start.6 = (bf16[32,4096]{1,0:T(8,128)(2,1)S(1)}, bf16[32,4096]{1,0:T(8,128)(2,1)S(1)}, u32[]{:S(2)}, u32[]{:S(2)}) collective-permute-start(bf16[32,4096]{1,0:T(8,128)(2,1)S(1)} %collective-permute-done.1.refs_1_), channel_id=1, source_target_pairs={{0,2},{1,3},{2,0},{3,1},{4,6},{5,7},{6,4},{7,5},{8,10},{9,11},{10,... | collective-permute-start | bytes 786440 | tf_op jit(solution)/shard_map/w4/ppermute | solution.py:50
  16.1 1.2 %collective-permute-done.10 = bf16[288,128]{1,0:T(8,128)(2,1)S(1)} collective-permute-done((bf16[288,128]{1,0:T(8,128)(2,1)S(1)}, bf16[288,128]{1,0:T(8,128)(2,1)S(1)}, u32[]{:S(2)}, u32[]{:S(2)}) %collective-permute-start.10) | collective-permute-done | bytes 73760 | tf_op jit(solution)/shard_map/ab_far/ppermute | solution.py:50
  17.3 1.6 %collective-permute-start.12 = (bf16[576,128]{1,0:T(8,128)(2,1)S(1)}, bf16[576,128]{1,0:T(8,128)(2,1)S(1)}, u32[]{:S(2)}, u32[]{:S(2)}) collective-permute-start(bf16[576,128]{1,0:T(8,128)(2,1)S(1)} %pad_maximum_fusion.2.refs_0_.first_ref), channel_id=1, source_target_pairs={{0,4},{1,5},{2,6},{3,7},{4,0},{5,1},{6,2},{7,3},{8,12},{9,13},{10,... | collective-permute-start | bytes 442376 | tf_op jit(solution)/shard_map/ab_1/ppermute | solution.py:50
  18.9 3.1 %collective-permute-done.5.refs_3_ = bf16[32,4096]{1,0:T(8,128)(2,1)S(1)} collective-permute-done((bf16[32,4096]{1,0:T(8,128)(2,1)S(1)}, bf16[32,4096]{1,0:T(8,128)(2,1)S(1)}, u32[]{:S(2)}, u32[]{:S(2)}) %collective-permute-start.5) | collective-permute-done | bytes 262176 | tf_op jit(solution)/shard_map/w3/ppermute | solution.py:50
  22.0 0.7 %collective-permute-start.14 = (bf16[576,128]{1,0:T(8,128)(2,1)S(1)}, bf16[576,128]{1,0:T(8,128)(2,1)S(1)}, u32[]{:S(2)}, u32[]{:S(2)}) collective-permute-start(bf16[576,128]{1,0:T(8,128)(2,1)S(1)} %pad_maximum_fusion.2.refs_0_.first_ref), channel_id=1, source_target_pairs={{0,2},{1,3},{2,0},{3,1},{4,6},{5,7},{6,4},{7,5},{8,10},{9,11},{10,... | collective-permute-start | bytes 442376 | tf_op jit(solution)/shard_map/ab_2/ppermute | solution.py:50
  23.2 3.3 %collective-permute-done.7.refs_5_ = bf16[32,4096]{1,0:T(8,128)(2,1)S(1)} collective-permute-done((bf16[32,4096]{1,0:T(8,128)(2,1)S(1)}, bf16[32,4096]{1,0:T(8,128)(2,1)S(1)}, u32[]{:S(2)}, u32[]{:S(2)}) %collective-permute-start.7) | collective-permute-done | bytes 262176 | tf_op jit(solution)/shard_map/w5/ppermute | solution.py:50
  26.5 1.6 %collective-permute-done.12.refs_1_ = bf16[576,128]{1,0:T(8,128)(2,1)S(1)} collective-permute-done((bf16[576,128]{1,0:T(8,128)(2,1)S(1)}, bf16[576,128]{1,0:T(8,128)(2,1)S(1)}, u32[]{:S(2)}, u32[]{:S(2)}) %collective-permute-start.12) | collective-permute-done | bytes 147488 | tf_op jit(solution)/shard_map/ab_1/ppermute | solution.py:50
  28.4 0.5 %collective-permute-start.15 = (bf16[576,128]{1,0:T(8,128)(2,1)S(1)}, bf16[576,128]{1,0:T(8,128)(2,1)S(1)}, u32[]{:S(2)}, u32[]{:S(2)}) collective-permute-start(bf16[576,128]{1,0:T(8,128)(2,1)S(1)} %collective-permute-done.14.refs_2_), channel_id=1, source_target_pairs={{0,1},{1,0},{2,3},{3,2},{4,5},{5,4},{6,7},{7,6},{8,9},{9,8},{10,11... | collective-permute-start | bytes 442376 | tf_op jit(solution)/shard_map/other_2/ppermute | solution.py:50
  28.9 0.9 %collective-permute-done.13.refs_4_ = bf16[576,128]{1,0:T(8,128)(2,1)S(1)} collective-permute-done((bf16[576,128]{1,0:T(8,128)(2,1)S(1)}, bf16[576,128]{1,0:T(8,128)(2,1)S(1)}, u32[]{:S(2)}, u32[]{:S(2)}) %collective-permute-start.13) | collective-permute-done | bytes 147488 | tf_op jit(solution)/shard_map/other_1/ppermute | solution.py:50
  30.2 3.1 %collective-permute-done.8.refs_6_ = bf16[32,4096]{1,0:T(8,128)(2,1)S(1)} collective-permute-done((bf16[32,4096]{1,0:T(8,128)(2,1)S(1)}, bf16[32,4096]{1,0:T(8,128)(2,1)S(1)}, u32[]{:S(2)}, u32[]{:S(2)}) %collective-permute-start.8) | collective-permute-done | bytes 262176 | tf_op jit(solution)/shard_map/w6/ppermute | solution.py:50
  33.3 2.2 %collective-permute-done.9.refs_7_ = bf16[32,4096]{1,0:T(8,128)(2,1)S(1)} collective-permute-done((bf16[32,4096]{1,0:T(8,128)(2,1)S(1)}, bf16[32,4096]{1,0:T(8,128)(2,1)S(1)}, u32[]{:S(2)}, u32[]{:S(2)}) %collective-permute-start.9) | collective-permute-done | bytes 262176 | tf_op jit(solution)/shard_map/w7/ppermute | solution.py:50
  35.5 1.3 %weight_product.1 = (f32[256,256]{1,0:T(8,128)S(1)}, f32[256,256]{1,0:T(8,128)S(1)}) custom-call(bf16[256,4096]{1,0:T(8,128)(2,1)S(1)} %copy-done, bf16[256,4096]{1,0:T(8,128)(2,1)S(1)} %collective-permute-done.hs_ref, bf16[32,4096]{1,0:T(8,128)(2,1)S(1)} %copy-done.1, bf16[32,4096]{1,0:T(8,128)(2,1)S(1)} %collective-permute-done.1.refs_1_, ...), custom_call_target="tpu_custom_call" | custom-call | flops 1073741824 | bytes 6291456 | tf_op jit(solution)/shard_map/weight_product/pallas_call | solution.py:214
  36.9 0.5 %collective-permute-start.18 = (bf16[576,128]{1,0:T(8,128)(2,1)S(1)}, bf16[576,128]{1,0:T(8,128)(2,1)S(1)}, u32[]{:S(2)}, u32[]{:S(2)}) collective-permute-start(bf16[576,128]{1,0:T(8,128)(2,1)S(1)} %collective-permute-done.17.refs_0_), channel_id=1, source_target_pairs={{0,1},{1,0},{2,3},{3,2},{4,5},{5,4},{6,7},{7,6},{8,9},{9,8},{10,11... | collective-permute-start | bytes 442376 | tf_op jit(solution)/shard_map/other_3/ppermute | solution.py:50
  37.4 0.7 %middle.1 = (f32[256,128]{1,0:T(8,128)S(1)}, bf16[32,4096]{1,0:T(8,128)(2,1)S(1)}, bf16[512,128]{1,0:T(8,128)(2,1)S(1)}) custom-call(bf16[256,4096]{1,0:T(8,128)(2,1)S(1)} %copy-done, bf16[32,4096]{1,0:T(8,128)(2,1)S(1)} %copy-done.1, bf16[576,128]{1,0:T(8,128)(2,1)S(1)} %pad_maximum_fusion.2.refs_0_.first_ref, ...), custom_call_target="tpu_custom_call" | custom-call | flops 268435456 | bytes 3145728 | tf_op jit(solution)/shard_map/middle/pallas_call | solution.py:226
  38.1 0.5 %collective-permute-done.18.refs_1_ = bf16[576,128]{1,0:T(8,128)(2,1)S(1)} collective-permute-done((bf16[576,128]{1,0:T(8,128)(2,1)S(1)}, bf16[576,128]{1,0:T(8,128)(2,1)S(1)}, u32[]{:S(2)}, u32[]{:S(2)}) %collective-permute-start.18) | collective-permute-done | bytes 147488 | tf_op jit(solution)/shard_map/other_3/ppermute | solution.py:50
  38.6 1.6 %last.1 = (bf16[256,512]{1,0:T(8,128)(2,1)}, bf16[32,4096]{1,0:T(8,128)(2,1)}) custom-call(bf16[256,4096]{1,0:T(8,128)(2,1)S(1)} %copy-done, bf16[32,4096]{1,0:T(8,128)(2,1)S(1)} %copy-done.1, f32[256,256]{1,0:T(8,128)S(1)} %get-tuple-element.40.own_ref, f32[256,256]{1,0:T(8,128)S(1)} %collective-permute-done.16.received_ref, ...), custom_call_target="tpu_custom_call" | custom-call | flops 33554432 | bytes 262144 | tf_op jit(solution)/shard_map/last/pallas_call | solution.py:239
  (25 shorter events, 2.5 us)
Async XLA Ops:
  0.6 34.9 %collective-permute-start = (bf16[256,4096]{1,0:T(8,128)(2,1)}, bf16[256,4096]{1,0:T(8,128)(2,1)S(1)}, u32[]{:S(2)}, u32[]{:S(2)}) collective-permute-start(bf16[256,4096]{1,0:T(8,128)(2,1)} %h_ref.5), channel_id=1, source_target_pairs={{0,1},{1,0},{2,3},{3,2},{4,5},{5,4},{6,7},{7,6},{8,9},{9,8},{10,11... | collective-permute-start | bytes 6291464 | tf_op jit(solution)/shard_map/other_hidden/ppermute | solution.py:50
  1.1 12.7 %collective-permute-start.1 = (bf16[32,4096]{1,0:T(8,128)(2,1)}, bf16[32,4096]{1,0:T(8,128)(2,1)S(1)}, u32[]{:S(2)}, u32[]{:S(2)}) collective-permute-start(bf16[32,4096]{1,0:T(8,128)(2,1)} %w_ref.3), channel_id=1, source_target_pairs={{0,8},{1,5},{2,10},{3,7},{4,12},{5,1},{6,14},{7,3},{8,0},{9,13},{1... | collective-permute-start | bytes 786440 | tf_op jit(solution)/shard_map/w1/ppermute | solution.py:50
  4.8 9.0 %collective-permute-start.2 = (bf16[32,4096]{1,0:T(8,128)(2,1)}, bf16[32,4096]{1,0:T(8,128)(2,1)S(1)}, u32[]{:S(2)}, u32[]{:S(2)}) collective-permute-start(bf16[32,4096]{1,0:T(8,128)(2,1)} %w_ref.3), channel_id=1, source_target_pairs={{0,2},{1,3},{2,0},{3,1},{4,6},{5,7},{6,4},{7,5},{8,10},{9,11},{10,... | collective-permute-start | bytes 786440 | tf_op jit(solution)/shard_map/w2/ppermute | solution.py:50
  6.3 5.6 %collective-permute-start.3 = (f32[1,256,128]{2,1,0:T(8,128)}, f32[1,256,128]{2,1,0:T(8,128)S(1)}, u32[]{:S(2)}, u32[]{:S(2)}) collective-permute-start(f32[1,256,128]{2,1,0:T(8,128)} %param.10), channel_id=1, source_target_pairs={{0,16},{1,17},{2,18},{3,19},{4,20},{5,21},{6,22},{7,23},{8,24},{9,... | collective-permute-start | bytes 393224 | tf_op jit(solution)/shard_map/other_a/ppermute | solution.py:50
  6.8 5.1 %collective-permute-start.4 = (f32[1,32,128]{2,1,0:T(8,128)}, f32[1,32,128]{2,1,0:T(8,128)S(1)}, u32[]{:S(2)}, u32[]{:S(2)}) collective-permute-start(f32[1,32,128]{2,1,0:T(8,128)} %param.11), channel_id=1, source_target_pairs={{0,16},{1,17},{2,18},{3,19},{4,20},{5,21},{6,22},{7,23},{8,24},{9,... | collective-permute-start | bytes 49160 | tf_op jit(solution)/shard_map/other_b/ppermute | solution.py:50
  10.2 25.3 %copy-start = (bf16[256,4096]{1,0:T(8,128)(2,1)S(1)}, bf16[256,4096]{1,0:T(8,128)(2,1)}, u32[]{:S(2)}) copy-start(bf16[256,4096]{1,0:T(8,128)(2,1)} %h_ref.5) | copy-start | bytes 6291460
  10.2 25.3 %copy-start.1 = (bf16[32,4096]{1,0:T(8,128)(2,1)S(1)}, bf16[32,4096]{1,0:T(8,128)(2,1)}, u32[]{:S(2)}) copy-start(bf16[32,4096]{1,0:T(8,128)(2,1)} %w_ref.3) | copy-start | bytes 786436
  11.9 5.3 %collective-permute-start.10 = (bf16[288,128]{1,0:T(8,128)(2,1)S(1)}, bf16[288,128]{1,0:T(8,128)(2,1)S(1)}, u32[]{:S(2)}, u32[]{:S(2)}) collective-permute-start(bf16[288,128]{1,0:T(8,128)(2,1)S(1)} %update.1), channel_id=1, source_target_pairs={{0,8},{1,9},{2,10},{3,11},{4,12},{5,13},{6,14},{7,15},{8,0},{9,1},... | collective-permute-start | bytes 221192 | tf_op jit(solution)/shard_map/ab_far/ppermute | solution.py:50
  13.8 8.2 %collective-permute-start.5 = (bf16[32,4096]{1,0:T(8,128)(2,1)S(1)}, bf16[32,4096]{1,0:T(8,128)(2,1)S(1)}, u32[]{:S(2)}, u32[]{:S(2)}) collective-permute-start(bf16[32,4096]{1,0:T(8,128)(2,1)S(1)} %collective-permute-done.1.refs_1_), channel_id=1, source_target_pairs={{0,17},{1,16},{2,19},{3,18},{4,21},{5,20},{6,23},{7,22},{8,25},{9,... | collective-permute-start | bytes 786440 | tf_op jit(solution)/shard_map/w3/ppermute | solution.py:50
  14.2 9.0 %collective-permute-start.6 = (bf16[32,4096]{1,0:T(8,128)(2,1)S(1)}, bf16[32,4096]{1,0:T(8,128)(2,1)S(1)}, u32[]{:S(2)}, u32[]{:S(2)}) collective-permute-start(bf16[32,4096]{1,0:T(8,128)(2,1)S(1)} %collective-permute-done.1.refs_1_), channel_id=1, source_target_pairs={{0,2},{1,3},{2,0},{3,1},{4,6},{5,7},{6,4},{7,5},{8,10},{9,11},{10,... | collective-permute-start | bytes 786440 | tf_op jit(solution)/shard_map/w4/ppermute | solution.py:50
  15.7 10.8 %collective-permute-start.7 = (bf16[32,4096]{1,0:T(8,128)(2,1)S(1)}, bf16[32,4096]{1,0:T(8,128)(2,1)S(1)}, u32[]{:S(2)}, u32[]{:S(2)}) collective-permute-start(bf16[32,4096]{1,0:T(8,128)(2,1)S(1)} %collective-permute-done.1.refs_1_), channel_id=1, source_target_pairs={{0,4},{1,9},{2,6},{3,11},{4,0},{5,13},{6,2},{7,15},{8,12},{9,1},{1... | collective-permute-start | bytes 786440 | tf_op jit(solution)/shard_map/w5/ppermute | solution.py:50
  17.3 10.8 %collective-permute-start.12 = (bf16[576,128]{1,0:T(8,128)(2,1)S(1)}, bf16[576,128]{1,0:T(8,128)(2,1)S(1)}, u32[]{:S(2)}, u32[]{:S(2)}) collective-permute-start(bf16[576,128]{1,0:T(8,128)(2,1)S(1)} %pad_maximum_fusion.2.refs_0_.first_ref), channel_id=1, source_target_pairs={{0,4},{1,5},{2,6},{3,7},{4,0},{5,1},{6,2},{7,3},{8,12},{9,13},{10,... | collective-permute-start | bytes 442376 | tf_op jit(solution)/shard_map/ab_1/ppermute | solution.py:50
  22.0 6.4 %collective-permute-start.14 = (bf16[576,128]{1,0:T(8,128)(2,1)S(1)}, bf16[576,128]{1,0:T(8,128)(2,1)S(1)}, u32[]{:S(2)}, u32[]{:S(2)}) collective-permute-start(bf16[576,128]{1,0:T(8,128)(2,1)S(1)} %pad_maximum_fusion.2.refs_0_.first_ref), channel_id=1, source_target_pairs={{0,2},{1,3},{2,0},{3,1},{4,6},{5,7},{6,4},{7,5},{8,10},{9,11},{10,... | collective-permute-start | bytes 442376 | tf_op jit(solution)/shard_map/ab_2/ppermute | solution.py:50
  23.2 5.2 %collective-permute-start.11 = (bf16[576,128]{1,0:T(8,128)(2,1)S(1)}, bf16[576,128]{1,0:T(8,128)(2,1)S(1)}, u32[]{:S(2)}, u32[]{:S(2)}) collective-permute-start(bf16[576,128]{1,0:T(8,128)(2,1)S(1)} %pad_maximum_fusion.2.refs_0_.first_ref), channel_id=1, source_target_pairs={{0,1},{1,0},{2,3},{3,2},{4,5},{5,4},{6,7},{7,6},{8,9},{9,8},{10,11... | collective-permute-start | bytes 442376 | tf_op jit(solution)/shard_map/other_0/ppermute | solution.py:50
  26.5 6.8 %collective-permute-start.8 = (bf16[32,4096]{1,0:T(8,128)(2,1)S(1)}, bf16[32,4096]{1,0:T(8,128)(2,1)S(1)}, u32[]{:S(2)}, u32[]{:S(2)}) collective-permute-start(bf16[32,4096]{1,0:T(8,128)(2,1)S(1)} %collective-permute-done.6.refs_4_), channel_id=1, source_target_pairs={{0,17},{1,16},{2,19},{3,18},{4,21},{5,20},{6,23},{7,22},{8,25},{9,... | collective-permute-start | bytes 786440 | tf_op jit(solution)/shard_map/w6/ppermute | solution.py:50
  28.1 7.4 %collective-permute-start.9 = (bf16[32,4096]{1,0:T(8,128)(2,1)S(1)}, bf16[32,4096]{1,0:T(8,128)(2,1)S(1)}, u32[]{:S(2)}, u32[]{:S(2)}) collective-permute-start(bf16[32,4096]{1,0:T(8,128)(2,1)S(1)} %collective-permute-done.6.refs_4_), channel_id=1, source_target_pairs={{0,4},{1,9},{2,6},{3,11},{4,0},{5,13},{6,2},{7,15},{8,12},{9,1},{1... | collective-permute-start | bytes 786440 | tf_op jit(solution)/shard_map/w7/ppermute | solution.py:50
  28.4 1.4 %collective-permute-start.13 = (bf16[576,128]{1,0:T(8,128)(2,1)S(1)}, bf16[576,128]{1,0:T(8,128)(2,1)S(1)}, u32[]{:S(2)}, u32[]{:S(2)}) collective-permute-start(bf16[576,128]{1,0:T(8,128)(2,1)S(1)} %collective-permute-done.12.refs_1_), channel_id=1, source_target_pairs={{0,1},{1,0},{2,3},{3,2},{4,5},{5,4},{6,7},{7,6},{8,9},{9,8},{10,11... | collective-permute-start | bytes 442376 | tf_op jit(solution)/shard_map/other_1/ppermute | solution.py:50
  28.4 1.8 %collective-permute-start.15 = (bf16[576,128]{1,0:T(8,128)(2,1)S(1)}, bf16[576,128]{1,0:T(8,128)(2,1)S(1)}, u32[]{:S(2)}, u32[]{:S(2)}) collective-permute-start(bf16[576,128]{1,0:T(8,128)(2,1)S(1)} %collective-permute-done.14.refs_2_), channel_id=1, source_target_pairs={{0,1},{1,0},{2,3},{3,2},{4,5},{5,4},{6,7},{7,6},{8,9},{9,8},{10,11... | collective-permute-start | bytes 442376 | tf_op jit(solution)/shard_map/other_2/ppermute | solution.py:50
  29.8 7.1 %collective-permute-start.17 = (bf16[576,128]{1,0:T(8,128)(2,1)S(1)}, bf16[576,128]{1,0:T(8,128)(2,1)S(1)}, u32[]{:S(2)}, u32[]{:S(2)}) collective-permute-start(bf16[576,128]{1,0:T(8,128)(2,1)S(1)} %collective-permute-done.12.refs_1_), channel_id=1, source_target_pairs={{0,2},{1,3},{2,0},{3,1},{4,6},{5,7},{6,4},{7,5},{8,10},{9,11},{10,... | collective-permute-start | bytes 442376 | tf_op jit(solution)/shard_map/ab_3/ppermute | solution.py:50
  36.8 1.8 %collective-permute-start.16 = (f32[256,256]{1,0:T(8,128)S(1)}, f32[256,256]{1,0:T(8,128)S(1)}, u32[]{:S(2)}, u32[]{:S(2)}) collective-permute-start(f32[256,256]{1,0:T(8,128)S(1)} %get-tuple-element.41), channel_id=1, source_target_pairs={{0,1},{1,0},{2,3},{3,2},{4,5},{5,4},{6,7},{7,6},{8,9},{9,8},{10,11... | collective-permute-start | bytes 786440 | tf_op jit(solution)/shard_map/received/ppermute | solution.py:50
  36.9 1.7 %collective-permute-start.18 = (bf16[576,128]{1,0:T(8,128)(2,1)S(1)}, bf16[576,128]{1,0:T(8,128)(2,1)S(1)}, u32[]{:S(2)}, u32[]{:S(2)}) collective-permute-start(bf16[576,128]{1,0:T(8,128)(2,1)S(1)} %collective-permute-done.17.refs_0_), channel_id=1, source_target_pairs={{0,1},{1,0},{2,3},{3,2},{4,5},{5,4},{6,7},{7,6},{8,9},{9,8},{10,11... | collective-permute-start | bytes 442376 | tf_op jit(solution)/shard_map/other_3/ppermute | solution.py:50

commit v3 on v2

--- a/solution.py
+++ b/solution.py
@@ -13,8 +13,10 @@
 NN = (((1,), (0,)), ((), ()))
 VMEM_LIMIT = 16 * 1024 * 1024
 WIDE_LIMIT = 58 * 1024 * 1024
-S_FLOPS = 4e9
+EARLY = 6
 U_FLOPS = 4e9
+L_FLOPS = 1e6
+P_FLOPS = 0
 W_FLOPS = 1
 M_FLOPS = 1
 
@@ -37,6 +39,7 @@
 
 CORE, Y, Z1, Z2 = (0, 1), (0, 2), (0, 4), (0, 8)
 REPLICA, X = (1, 0), (1, 1)
+ZY1, ZY2 = (0, 6), (0, 10)
 
 
 def send(rows, group, move, other_move=None, name="sent"):
@@ -93,14 +96,17 @@
     own_ref[...] = dot(h_ref[...], w_all[...], NT)
 
 
-def placing(rows, n, m, kind):
+def place(block_of, rows, products, out):
+    n, m = products.shape[1], out.shape[1]
     source = lax.broadcasted_iota(jnp.int32, (n, m), 0)
     target = lax.broadcasted_iota(jnp.int32, (n, m), 1)
     column = jnp.zeros((n, m), jnp.int32)
-    for i in range(len(HELD)):
-        shard = shard_of(flips_of(i, kind))
-        column = jnp.where(source // rows == i, shard * rows, column)
-    return (target == column + source % rows).astype(jnp.bfloat16)
+    for i, (held, kind) in enumerate(block_of):
+        column = jnp.where(source // rows == i, shard_of(flips_of(held, kind)) * rows, column)
+    columns = (target == column + source % rows).astype(jnp.bfloat16)
+    for part in split_bf16(products):
+        out = out + dot(part, columns, NN)
+    return out
 
 
 def split_bf16(v):
@@ -112,8 +118,8 @@
     x, place, core = position()
     rows_b = w_ref.shape[0]
     rows_a = h_ref.shape[1] * rows_b // b_all.shape[0]
-    for ref, other, at in blocks:
-        for j, (dz, dy) in enumerate(SHARDS[at]):
+    for ref, other, at, first in blocks:
+        for j, (dz, dy) in enumerate(SHARDS[at], first):
             shard = (place ^ (dz * 2 + dy)) * 2 + (core ^ other)
             row = j * (rows_a + rows_b)
             columns = pl.ds(pl.multiple_of(shard * rows_a, rows_a), rows_a)
@@ -124,35 +130,58 @@
     return t
 
 
-def middle_kernel(at, h_ref, w_ref, *refs):
-    *ab_refs, t_ref, merged_ref, b_all = refs
+def middle_kernel(at, early, h_ref, w_ref, own_ref, received_ref, *refs):
+    *ab_refs, t_ref, high_ref, merged_ref, b_all = refs
+    x, place_at, core = position()
+    kind = core ^ x
     rows_b = w_ref.shape[0]
     rows_a = h_ref.shape[1] * rows_b // b_all.shape[0]
+    out = jnp.zeros(high_ref.shape, jnp.float32)
+    for ref, which in ((own_ref, kind), (received_ref, 1 - kind)):
+        out = place([(i, which) for i in range(early)], rows_b, ref[...], out)
+    high_ref[...] = out
     b_own = ab_refs[0][rows_a : rows_a + rows_b]
-    blocks = [(ref, i // len(at), at[i % len(at)]) for i, ref in enumerate(ab_refs)]
+    n = len(at)
+    blocks = [(ref, 0, at[i], 0) for i, ref in enumerate(ab_refs[:n])]
+    joined = len(ab_refs) == n + 1
+    blocks += [(ab_refs[n if joined else n + i], 1, k, 2 * i if joined else 0) for i, k in enumerate(at)]
     t_ref[...] = add_blocks(h_ref, w_ref, b_own, merged_ref, b_all, blocks, jnp.zeros(t_ref.shape, jnp.float32))
 
 
-def last_kernel(at, h_ref, w_ref, own_ref, received_ref, t_ref, m_ref, b_ref, first_ref, *refs):
+def late_kernel(late, h_ref, high_ref, *refs):
+    *w_refs, out_ref = refs
+    x, _, core = position()
+    kind = core ^ x
+    held = [(i, which) for which in (kind, 1 - kind) for i in late]
+    products = dot(h_ref[...], jnp.concatenate([ref[...] for ref in w_refs]), NT)
+    out_ref[...] = place(held, w_refs[0].shape[0], products, high_ref[...])
+
+
+def last_kernel(at, h_ref, w_ref, t_ref, high_ref, m_ref, b_ref, first_ref, *refs):
     *ab_refs, out_ref, merged_ref, b_all = refs
-    x, place, core = position()
-    kind = core ^ x
-    n, m = own_ref.shape[1], out_ref.shape[1]
     rows_b = w_ref.shape[0]
     rows_a = h_ref.shape[1] * rows_b // b_all.shape[0]
     b_own = first_ref[rows_a : rows_a + rows_b]
     merged_ref[...] = m_ref[...]
     b_all[...] = b_ref[...]
-    blocks = [(ref, i // len(at), at[i % len(at)]) for i, ref in enumerate(ab_refs)]
+    blocks = [(ref, i // len(at), at[i % len(at)], 0) for i, ref in enumerate(ab_refs)]
     t = add_blocks(h_ref, w_ref, b_own, merged_ref, b_all, blocks, t_ref[...])
-    out = jnp.zeros(out_ref.shape, jnp.float32)
+    out = high_ref[...]
     for part in split_bf16(t):
         out = out + dot(part, b_all[...], NT)
-    for ref, which in ((own_ref, kind), (received_ref, 1 - kind)):
-        columns = placing(rows_b, n, m, which)
-        for part in split_bf16(ref[...]):
-            out = out + dot(part, columns, NN)
     out_ref[...] = out.astype(jnp.bfloat16)
+
+
+def pick_kernel(first_ref, second_ref, out_ref):
+    x, _, core = position()
+
+    @pl.when(core == x)
+    def _():
+        out_ref[...] = first_ref[...]
+
+    @pl.when(core != x)
+    def _():
+        out_ref[...] = second_ref[...]
 
 
 def cost(flops, number_of_bytes):
@@ -172,15 +201,18 @@
     wide = pltpu.CompilerParams(vmem_limit_bytes=WIDE_LIMIT)
     bf16, f32 = jnp.bfloat16, jnp.float32
 
+    hold = lax.optimization_barrier
+    h_here, w_here = hidden, weight
+    old = jnp.concatenate([adapter_a, adapter_b])
+    mine = jnp.concatenate([grad_a[0], grad_b[0]])
+    old, mine = hold((old, mine))
     w0 = weight
     other_a = send(grad_a, group, REPLICA, name="other_a")
     other_b = send(grad_b, group, REPLICA, name="other_b")
     w1 = send(w0, group, Z2, Z1, name="w1")
     w2 = send(w0, group, Y, name="w2")
-    w1, w2 = lax.optimization_barrier((w1, w2))
+    w1, w2 = hold((w1, w2))
     other_hidden = send(hidden, group, CORE, name="other_hidden")
-    old, mine = lax.optimization_barrier((jnp.concatenate([adapter_a, adapter_b]), jnp.concatenate([grad_a[0], grad_b[0]])))
-    h_here, w_here = hidden, weight
     ab = pl.pallas_call(
         functools.partial(update_kernel, group[0]),
         out_shape=jax.ShapeDtypeStruct((rows_a + rows_b, rank), bf16),
@@ -191,64 +223,87 @@
         name="update",
     )(old, mine, other_a, other_b)
     ab_far = send(ab, group, Z2, name="ab_far")
-    w1, _ = lax.optimization_barrier((w1, ab))
     w3 = send(w1, group, X, name="w3")
     w4 = send(w1, group, Y, name="w4")
     w5 = send(w1, group, Z1, Z2, name="w5")
     ab_0 = jnp.concatenate([ab, ab_far])
     ab_1 = send(ab_0, group, Z1, name="ab_1")
     ab_2 = send(ab_0, group, Y, name="ab_2")
-    w3, w4, w5 = lax.optimization_barrier((w3, w4, w5))
+    other_0 = send(ab_0, group, CORE, name="other_0")
+    ab_3 = send(ab_1, group, Y, name="ab_3")
+    w3, w4, w5 = hold((w3, w4, w5))
     w6 = send(w4, group, X, name="w6")
-    w7 = send(w4, group, Z1, Z2, name="w7")
-    ab_3 = send(ab_1, group, Y, name="ab_3")
+    mixed = pl.pallas_call(
+        pick_kernel,
+        out_shape=jax.ShapeDtypeStruct(weight.shape, bf16),
+        in_specs=[vmem] * 2,
+        out_specs=vmem,
+        compiler_params=params,
+        cost_estimate=cost(P_FLOPS, 0),
+        name="pick",
+    )(w4, w5)
+    w7 = send(mixed, group, Z1, Y, name="w7")
     held = [w0, w1, w2, w3, w4, w5, w6, w7]
-    other_0 = send(ab_0, group, CORE, name="other_0")
     other_1 = send(ab_1, group, CORE, name="other_1")
     other_2 = send(ab_2, group, CORE, name="other_2")
     other_3 = send(ab_3, group, CORE, name="other_3")
-    held, other_0, other_1, other_2 = lax.optimization_barrier((held, other_0, other_1, other_2))
-
-    columns = outputs // 2
-    held[0] = w_here
+    ab_early = [ab_0, ab_1, ab_2, other_0, other_1, other_2]
+
+    early = [w_here] + held[1:EARLY]
+    late = held[EARLY:]
+    early, other_0 = lax.optimization_barrier((early, other_0))
+    ab_early = [ab_0, ab_1, ab_2, other_0, other_1, other_2]
+    columns = rows_b * EARLY
     own, other = pl.pallas_call(
         weight_kernel,
         out_shape=[jax.ShapeDtypeStruct((tokens, columns), f32)] * 2,
-        in_specs=[vmem] * (2 + len(held)),
+        in_specs=[vmem] * (2 + EARLY),
         out_specs=[vmem] * 2,
         scratch_shapes=[pltpu.VMEM((columns, depth), bf16)],
         compiler_params=params,
-        cost_estimate=cost(W_FLOPS * 2 * tokens * outputs * depth, 2 * depth * (2 * tokens + columns)),
+        cost_estimate=cost(W_FLOPS * 4 * tokens * columns * depth, 2 * depth * (2 * tokens + columns)),
         name="weight_product",
-    )(h_here, other_hidden, *held)
+    )(h_here, other_hidden, *early)
     received = send(other, group, CORE, name="received")
     middle = (0, 1, 2)
-    t, merged, b_all = pl.pallas_call(
-        functools.partial(middle_kernel, middle),
+    t, high, merged, b_all = pl.pallas_call(
+        functools.partial(middle_kernel, middle, EARLY),
         out_shape=[
             jax.ShapeDtypeStruct((tokens, rank), f32),
+            jax.ShapeDtypeStruct((tokens, outputs), f32),
             jax.ShapeDtypeStruct(weight.shape, bf16),
             jax.ShapeDtypeStruct((outputs, rank), bf16),
         ],
-        in_specs=[vmem] * (2 + 2 * len(middle)),
-        out_specs=[vmem] * 3,
+        in_specs=[vmem] * (4 + len(ab_early)),
+        out_specs=[vmem] * 4,
         compiler_params=params,
         cost_estimate=cost(M_FLOPS * 2 * tokens * rank * depth, 2 * depth * (tokens + rank)),
         name="middle",
-    )(h_here, w_here, ab_0, ab_1, ab_2, other_0, other_1, other_2)
+    )(h_here, w_here, own, received, *ab_early)
+    late, t = lax.optimization_barrier((late, t))
+    other_late = [send(v, group, CORE, name="other_late") for v in late]
+    high = pl.pallas_call(
+        functools.partial(late_kernel, tuple(range(EARLY, len(HELD)))),
+        out_shape=jax.ShapeDtypeStruct((tokens, outputs), f32),
+        in_specs=[vmem] * (2 + 2 * len(late)),
+        out_specs=vmem,
+        compiler_params=params,
+        cost_estimate=cost(L_FLOPS, 2 * outputs * tokens),
+        name="late_product",
+    )(h_here, high, *late, *other_late)
     return tuple(pl.pallas_call(
         functools.partial(last_kernel, (3,)),
         out_shape=[
             jax.ShapeDtypeStruct((tokens, outputs), bf16),
             jax.ShapeDtypeStruct(weight.shape, bf16),
         ],
-        in_specs=[vmem] * 10,
+        in_specs=[vmem] * 9,
         out_specs=[vmem] * 2,
         scratch_shapes=[pltpu.VMEM((outputs, rank), bf16)],
         compiler_params=params,
         cost_estimate=cost(2 * tokens * rank * outputs, 2 * outputs * tokens),
         name="last",
-    )(h_here, w_here, own, received, t, merged, b_all, ab_0, ab_3, other_3))
+    )(h_here, w_here, t, high, merged, b_all, ab_0, ab_3, other_3))
 
 
 def solution(mesh):

time: 40.9 us -> 38.8 us (0.949)
  waiting for transfers between devices: 17.9 us -> 13.6 us
  starting transfers between devices: 16.1 us -> 17.5 us
  Pallas kernels: 3.58 us -> 4.74 us
    ppermute x19 -> x21, waiting for transfers between devices: 17.9 us -> 13.6 us  [send(): return lax.ppermute(rows, AXES, pairs)]
    pallas_call x1 -> x3, Pallas kernels: 0.69 us -> 2.2 us  [the longest x1 1.17 us: paired(): pl.pallas_call(functools.partial(late_kernel, tuple(range(EARLY, len(HELD...]
    ppermute x19 -> x21, starting transfers between devices: 16.1 us -> 17.5 us  [send(): return lax.ppermute(rows, AXES, pairs)]
  transfers between devices with their start and end apart: 19 -> 21, of which waited for: 10 -> 10; matrix products, arithmetic and copies ran while one was open for 5% -> 5% of each run, Pallas kernels for 5% -> 9%
where the time goes in v3:
time: 38.8 us; the launch traced here: 38.4 us
  starting transfers between devices  17.5 us (45%)
  waiting for transfers between devices  13.6 us (35%)
  Pallas kernels  4.74 us (12%)
  other arithmetic  1.88 us (5%)
  between operations  0.73 us (2%)
    ppermute x21, starting transfers between devices, send(): return lax.ppermute(rows, AXES, pairs)  17.5 us
    ppermute x21, waiting for transfers between devices, send(): return lax.ppermute(rows, AXES, pairs)  13.6 us
    pallas_call x1, Pallas kernels, paired(): pl.pallas_call(weight_kernel, out_shape=[jax.ShapeDtypeStruct((tokens, co...  1.26 us
    pallas_call x1, Pallas kernels, paired(): pl.pallas_call(functools.partial(last_kernel, (3,)), out_shape=[jax.Shape...  1.25 us
    pallas_call x1, Pallas kernels, paired(): pl.pallas_call(functools.partial(late_kernel, tuple(range(EARLY, len(HELD...  1.17 us
    pallas_call x1, Pallas kernels, paired(): pl.pallas_call(functools.partial(middle_kernel, middle, EARLY), out_shape...  1.01 us
    concatenate x1, other arithmetic, paired(): mine = jnp.concatenate([grad_a[0], grad_b[0]])  0.93 us
    concatenate x1, other arithmetic, paired(): old = jnp.concatenate([adapter_a, adapter_b])  0.93 us
  transfers between devices with their start and end apart: 21, of which 10 were waited for; matrix products, arithmetic and copies ran while one was open for 5% of the time, Pallas kernels for 9%

profile of v3, /device:TPU:0, one launch (start us, length us, event | category | flops | bytes accessed | tf_op | source)
XLA Modules:
  0.0 38.4 jit_solution(17105300129459121842)
XLA Ops:
  0.6 0.5 %collective-permute-start.7 = (bf16[256,4096]{1,0:T(8,128)(2,1)}, bf16[256,4096]{1,0:T(8,128)(2,1)S(1)}, u32[]{:S(2)}, u32[]{:S(2)}) collective-permute-start(bf16[256,4096]{1,0:T(8,128)(2,1)} %h_ref.7), channel_id=1, source_target_pairs={{0,1},{1,0},{2,3},{3,2},{4,5},{5,4},{6,7},{7,6},{8,9},{9,8},{10,11... | collective-permute-start | bytes 6291464 | tf_op jit(solution)/shard_map/other_hidden/ppermute | solution.py:53
  1.1 3.7 %collective-permute-start = (bf16[32,4096]{1,0:T(8,128)(2,1)}, bf16[32,4096]{1,0:T(8,128)(2,1)S(1)}, u32[]{:S(2)}, u32[]{:S(2)}) collective-permute-start(bf16[32,4096]{1,0:T(8,128)(2,1)} %w_ref.3), channel_id=1, source_target_pairs={{0,8},{1,5},{2,10},{3,7},{4,12},{5,1},{6,14},{7,3},{8,0},{9,13},{1... | collective-permute-start | bytes 786440 | tf_op jit(solution)/shard_map/w1/ppermute | solution.py:53
  4.8 1.5 %collective-permute-start.1 = (bf16[32,4096]{1,0:T(8,128)(2,1)}, bf16[32,4096]{1,0:T(8,128)(2,1)S(1)}, u32[]{:S(2)}, u32[]{:S(2)}) collective-permute-start(bf16[32,4096]{1,0:T(8,128)(2,1)} %w_ref.3), channel_id=1, source_target_pairs={{0,2},{1,3},{2,0},{3,1},{4,6},{5,7},{6,4},{7,5},{8,10},{9,11},{10,... | collective-permute-start | bytes 786440 | tf_op jit(solution)/shard_map/w2/ppermute | solution.py:53
  6.8 1.5 %collective-permute-start.9 = (f32[1,32,128]{2,1,0:T(8,128)}, f32[1,32,128]{2,1,0:T(8,128)S(1)}, u32[]{:S(2)}, u32[]{:S(2)}) collective-permute-start(f32[1,32,128]{2,1,0:T(8,128)} %param.11), channel_id=1, source_target_pairs={{0,16},{1,17},{2,18},{3,19},{4,20},{5,21},{6,22},{7,23},{8,24},{9,... | collective-permute-start | bytes 49160 | tf_op jit(solution)/shard_map/other_b/ppermute | solution.py:53
  8.4 0.9 %pad_maximum_fusion.old_ref = f32[288,128]{1,0:T(8,128)S(1)} fusion(f32[32,128]{1,0:T(8,128)} %param.9, f32[256,128]{1,0:T(8,128)} %param.8), kind=kLoop, calls=%fused_computation | loop fusion | flops 36864 | bytes 294912 | tf_op jit(solution)/shard_map/concatenate | solution.py:206
  9.3 0.9 %pad_maximum_fusion.1.own_ref = f32[288,128]{1,0:T(8,128)S(1)} fusion(f32[32,128]{1,0:T(8,128)} %bitcast.3, f32[256,128]{1,0:T(8,128)} %bitcast.2), kind=kLoop, calls=%fused_computation.1 | loop fusion | flops 36864 | bytes 294912 | tf_op jit(solution)/shard_map/concatenate | solution.py:207
  10.2 1.7 %collective-permute-done.9.ob_ref = f32[1,32,128]{2,1,0:T(8,128)S(1)} collective-permute-done((f32[1,32,128]{2,1,0:T(8,128)}, f32[1,32,128]{2,1,0:T(8,128)S(1)}, u32[]{:S(2)}, u32[]{:S(2)}) %collective-permute-start.9) | collective-permute-done | bytes 16416 | tf_op jit(solution)/shard_map/other_b/ppermute | solution.py:53
  12.0 1.9 %collective-permute-start.10 = (bf16[288,128]{1,0:T(8,128)(2,1)S(1)}, bf16[288,128]{1,0:T(8,128)(2,1)S(1)}, u32[]{:S(2)}, u32[]{:S(2)}) collective-permute-start(bf16[288,128]{1,0:T(8,128)(2,1)S(1)} %update.1), channel_id=1, source_target_pairs={{0,8},{1,9},{2,10},{3,11},{4,12},{5,13},{6,14},{7,15},{8,0},{9,1},... | collective-permute-start | bytes 221192 | tf_op jit(solution)/shard_map/ab_far/ppermute | solution.py:53
  14.2 1.5 %collective-permute-start.3 = (bf16[32,4096]{1,0:T(8,128)(2,1)S(1)}, bf16[32,4096]{1,0:T(8,128)(2,1)S(1)}, u32[]{:S(2)}, u32[]{:S(2)}) collective-permute-start(bf16[32,4096]{1,0:T(8,128)(2,1)S(1)} %collective-permute-done.refs_1_), channel_id=1, source_target_pairs={{0,2},{1,3},{2,0},{3,1},{4,6},{5,7},{6,4},{7,5},{8,10},{9,11},{10,... | collective-permute-start | bytes 786440 | tf_op jit(solution)/shard_map/w4/ppermute | solution.py:53
  16.1 1.2 %collective-permute-done.10 = bf16[288,128]{1,0:T(8,128)(2,1)S(1)} collective-permute-done((bf16[288,128]{1,0:T(8,128)(2,1)S(1)}, bf16[288,128]{1,0:T(8,128)(2,1)S(1)}, u32[]{:S(2)}, u32[]{:S(2)}) %collective-permute-start.10) | collective-permute-done | bytes 73760 | tf_op jit(solution)/shard_map/ab_far/ppermute | solution.py:53
  17.4 4.7 %collective-permute-done.2.refs_3_ = bf16[32,4096]{1,0:T(8,128)(2,1)S(1)} collective-permute-done((bf16[32,4096]{1,0:T(8,128)(2,1)S(1)}, bf16[32,4096]{1,0:T(8,128)(2,1)S(1)}, u32[]{:S(2)}, u32[]{:S(2)}) %collective-permute-start.2) | collective-permute-done | bytes 262176 | tf_op jit(solution)/shard_map/w3/ppermute | solution.py:53
  22.0 0.8 %collective-permute-start.13 = (bf16[576,128]{1,0:T(8,128)(2,1)S(1)}, bf16[576,128]{1,0:T(8,128)(2,1)S(1)}, u32[]{:S(2)}, u32[]{:S(2)}) collective-permute-start(bf16[576,128]{1,0:T(8,128)(2,1)S(1)} %pad_maximum_fusion.2.refs_0_.first_ref), channel_id=1, source_target_pairs={{0,4},{1,5},{2,6},{3,7},{4,0},{5,1},{6,2},{7,3},{8,12},{9,13},{10,... | collective-permute-start | bytes 442376 | tf_op jit(solution)/shard_map/ab_1/ppermute | solution.py:53
  23.2 1.2 %collective-permute-start.14 = (bf16[576,128]{1,0:T(8,128)(2,1)S(1)}, bf16[576,128]{1,0:T(8,128)(2,1)S(1)}, u32[]{:S(2)}, u32[]{:S(2)}) collective-permute-start(bf16[576,128]{1,0:T(8,128)(2,1)S(1)} %pad_maximum_fusion.2.refs_0_.first_ref), channel_id=1, source_target_pairs={{0,2},{1,3},{2,0},{3,1},{4,6},{5,7},{6,4},{7,5},{8,10},{9,11},{10,... | collective-permute-start | bytes 442376 | tf_op jit(solution)/shard_map/ab_2/ppermute | solution.py:53
  24.4 0.7 %collective-permute-done.4.second_ref.refs_5_ = bf16[32,4096]{1,0:T(8,128)(2,1)S(1)} collective-permute-done((bf16[32,4096]{1,0:T(8,128)(2,1)S(1)}, bf16[32,4096]{1,0:T(8,128)(2,1)S(1)}, u32[]{:S(2)}, u32[]{:S(2)}) %collective-permute-start.4) | collective-permute-done | bytes 262176 | tf_op jit(solution)/shard_map/w5/ppermute | solution.py:53
  25.1 0.8 %collective-permute-start.6 = (bf16[32,4096]{1,0:T(8,128)(2,1)S(1)}, bf16[32,4096]{1,0:T(8,128)(2,1)S(1)}, u32[]{:S(2)}, u32[]{:S(2)}) collective-permute-start(bf16[32,4096]{1,0:T(8,128)(2,1)S(1)} %pick.1), channel_id=1, source_target_pairs={{0,4},{1,3},{2,6},{3,1},{4,0},{5,7},{6,2},{7,5},{8,12},{9,11},{10,... | collective-permute-start | bytes 786440 | tf_op jit(solution)/shard_map/w7/ppermute | solution.py:53
  25.9 1.3 %weight_product.1 = (f32[256,192]{1,0:T(8,128)S(1)}, f32[256,192]{1,0:T(8,128)S(1)}) custom-call(bf16[256,4096]{1,0:T(8,128)(2,1)S(1)} %copy-done, bf16[256,4096]{1,0:T(8,128)(2,1)S(1)} %collective-permute-done.7.hs_ref, bf16[32,4096]{1,0:T(8,128)(2,1)S(1)} %copy-done.1, bf16[32,4096]{1,0:T(8,128)(2,1)S(1)} %collective-permute-done.refs_1_, ...), custom_call_target="tpu_custom_call" | custom-call | flops 805306368 | bytes 5767168 | tf_op jit(solution)/shard_map/weight_product/pallas_call | solution.py:257
  27.2 1.1 %collective-permute-start.12 = (f32[256,192]{1,0:T(8,128)S(1)}, f32[256,192]{1,0:T(8,128)S(1)}, u32[]{:S(2)}, u32[]{:S(2)}) collective-permute-start(f32[256,192]{1,0:T(8,128)S(1)} %get-tuple-element.39), channel_id=1, source_target_pairs={{0,1},{1,0},{2,3},{3,2},{4,5},{5,4},{6,7},{7,6},{8,9},{9,8},{10,11... | collective-permute-start | bytes 589832 | tf_op jit(solution)/shard_map/received/ppermute | solution.py:53
  28.9 0.8 %collective-permute-done.15.refs_4_ = bf16[576,128]{1,0:T(8,128)(2,1)S(1)} collective-permute-done((bf16[576,128]{1,0:T(8,128)(2,1)S(1)}, bf16[576,128]{1,0:T(8,128)(2,1)S(1)}, u32[]{:S(2)}, u32[]{:S(2)}) %collective-permute-start.15) | collective-permute-done | bytes 147488 | tf_op jit(solution)/shard_map/other_1/ppermute | solution.py:53
  29.7 1.0 %collective-permute-start.19 = (bf16[576,128]{1,0:T(8,128)(2,1)S(1)}, bf16[576,128]{1,0:T(8,128)(2,1)S(1)}, u32[]{:S(2)}, u32[]{:S(2)}) collective-permute-start(bf16[576,128]{1,0:T(8,128)(2,1)S(1)} %collective-permute-done.13.refs_1_), channel_id=1, source_target_pairs={{0,2},{1,3},{2,0},{3,1},{4,6},{5,7},{6,4},{7,5},{8,10},{9,11},{10,... | collective-permute-start | bytes 442376 | tf_op jit(solution)/shard_map/ab_3/ppermute | solution.py:53
  30.7 1.0 %middle.1 = (f32[256,128]{1,0:T(8,128)S(1)}, f32[256,512]{1,0:T(8,128)S(1)}, bf16[32,4096]{1,0:T(8,128)(2,1)S(1)}, bf16[512,128]{1,0:T(8,128)(2,1)S(1)}) custom-call(bf16[256,4096]{1,0:T(8,128)(2,1)S(1)} %copy-done, bf16[32,4096]{1,0:T(8,128)(2,1)S(1)} %copy-done.1, f32[256,192]{1,0:T(8,128)S(1)} %get-tuple-element.38.own_ref, ...), custom_call_target="tpu_custom_call" | custom-call | flops 268435456 | bytes 3145728 | tf_op jit(solution)/shard_map/middle/pallas_call | solution.py:269
  31.8 1.5 %collective-permute-done.5.refs_0_ = bf16[32,4096]{1,0:T(8,128)(2,1)S(1)} collective-permute-done((bf16[32,4096]{1,0:T(8,128)(2,1)S(1)}, bf16[32,4096]{1,0:T(8,128)(2,1)S(1)}, u32[]{:S(2)}, u32[]{:S(2)}) %collective-permute-start.5) | collective-permute-done | bytes 262176 | tf_op jit(solution)/shard_map/w6/ppermute | solution.py:53
  33.8 2.0 %collective-permute-done.19.refs_0_ = bf16[576,128]{1,0:T(8,128)(2,1)S(1)} collective-permute-done((bf16[576,128]{1,0:T(8,128)(2,1)S(1)}, bf16[576,128]{1,0:T(8,128)(2,1)S(1)}, u32[]{:S(2)}, u32[]{:S(2)}) %collective-permute-start.19) | collective-permute-done | bytes 147488 | tf_op jit(solution)/shard_map/ab_3/ppermute | solution.py:53
  35.8 1.2 %late_product.1.high_ref = f32[256,512]{1,0:T(8,128)S(1)} custom-call(bf16[256,4096]{1,0:T(8,128)(2,1)S(1)} %copy-done, f32[256,512]{1,0:T(8,128)S(1)} %get-tuple-element.43.high_ref, bf16[32,4096]{1,0:T(8,128)(2,1)S(1)} %collective-permute-done.5.refs_0_, bf16[32,4096]{1,0:T(8,128)(2,1)S(1)} %collective-permute-done.6.refs_1_, ...), custom_call_target="tpu_custom_call" | custom-call | flops 1000000 | bytes 262144 | tf_op jit(solution)/shard_map/late_product/pallas_call | solution.py:285
  37.2 1.3 %last.1 = (bf16[256,512]{1,0:T(8,128)(2,1)}, bf16[32,4096]{1,0:T(8,128)(2,1)}) custom-call(bf16[256,4096]{1,0:T(8,128)(2,1)S(1)} %copy-done, bf16[32,4096]{1,0:T(8,128)(2,1)S(1)} %copy-done.1, f32[256,128]{1,0:T(8,128)S(1)} %get-tuple-element.42.t_ref, f32[256,512]{1,0:T(8,128)S(1)} %late_product.1.high_ref, bf16[32,4096]{1,0:T(8,128)(2,1)S(1)} %get-tuple-element.46.m_ref, ...), custom_call_target="tpu_custom_call" | custom-call | flops 33554432 | bytes 262144 | tf_op jit(solution)/shard_map/last/pallas_call | solution.py:294
  (31 shorter events, 2.9 us)
Async XLA Ops:
  0.6 25.3 %collective-permute-start.7 = (bf16[256,4096]{1,0:T(8,128)(2,1)}, bf16[256,4096]{1,0:T(8,128)(2,1)S(1)}, u32[]{:S(2)}, u32[]{:S(2)}) collective-permute-start(bf16[256,4096]{1,0:T(8,128)(2,1)} %h_ref.7), channel_id=1, source_target_pairs={{0,1},{1,0},{2,3},{3,2},{4,5},{5,4},{6,7},{7,6},{8,9},{9,8},{10,11... | collective-permute-start | bytes 6291464 | tf_op jit(solution)/shard_map/other_hidden/ppermute | solution.py:53
  1.1 12.7 %collective-permute-start = (bf16[32,4096]{1,0:T(8,128)(2,1)}, bf16[32,4096]{1,0:T(8,128)(2,1)S(1)}, u32[]{:S(2)}, u32[]{:S(2)}) collective-permute-start(bf16[32,4096]{1,0:T(8,128)(2,1)} %w_ref.3), channel_id=1, source_target_pairs={{0,8},{1,5},{2,10},{3,7},{4,12},{5,1},{6,14},{7,3},{8,0},{9,13},{1... | collective-permute-start | bytes 786440 | tf_op jit(solution)/shard_map/w1/ppermute | solution.py:53
  4.8 9.0 %collective-permute-start.1 = (bf16[32,4096]{1,0:T(8,128)(2,1)}, bf16[32,4096]{1,0:T(8,128)(2,1)S(1)}, u32[]{:S(2)}, u32[]{:S(2)}) collective-permute-start(bf16[32,4096]{1,0:T(8,128)(2,1)} %w_ref.3), channel_id=1, source_target_pairs={{0,2},{1,3},{2,0},{3,1},{4,6},{5,7},{6,4},{7,5},{8,10},{9,11},{10,... | collective-permute-start | bytes 786440 | tf_op jit(solution)/shard_map/w2/ppermute | solution.py:53
  6.3 5.6 %collective-permute-start.8 = (f32[1,256,128]{2,1,0:T(8,128)}, f32[1,256,128]{2,1,0:T(8,128)S(1)}, u32[]{:S(2)}, u32[]{:S(2)}) collective-permute-start(f32[1,256,128]{2,1,0:T(8,128)} %param.10), channel_id=1, source_target_pairs={{0,16},{1,17},{2,18},{3,19},{4,20},{5,21},{6,22},{7,23},{8,24},{9,... | collective-permute-start | bytes 393224 | tf_op jit(solution)/shard_map/other_a/ppermute | solution.py:53
  6.8 5.1 %collective-permute-start.9 = (f32[1,32,128]{2,1,0:T(8,128)}, f32[1,32,128]{2,1,0:T(8,128)S(1)}, u32[]{:S(2)}, u32[]{:S(2)}) collective-permute-start(f32[1,32,128]{2,1,0:T(8,128)} %param.11), channel_id=1, source_target_pairs={{0,16},{1,17},{2,18},{3,19},{4,20},{5,21},{6,22},{7,23},{8,24},{9,... | collective-permute-start | bytes 49160 | tf_op jit(solution)/shard_map/other_b/ppermute | solution.py:53
  10.2 15.7 %copy-start.1 = (bf16[32,4096]{1,0:T(8,128)(2,1)S(1)}, bf16[32,4096]{1,0:T(8,128)(2,1)}, u32[]{:S(2)}) copy-start(bf16[32,4096]{1,0:T(8,128)(2,1)} %w_ref.3) | copy-start | bytes 786436
  11.9 14.0 %copy-start = (bf16[256,4096]{1,0:T(8,128)(2,1)S(1)}, bf16[256,4096]{1,0:T(8,128)(2,1)}, u32[]{:S(2)}) copy-start(bf16[256,4096]{1,0:T(8,128)(2,1)} %h_ref.7) | copy-start | bytes 6291460
  12.0 5.3 %collective-permute-start.10 = (bf16[288,128]{1,0:T(8,128)(2,1)S(1)}, bf16[288,128]{1,0:T(8,128)(2,1)S(1)}, u32[]{:S(2)}, u32[]{:S(2)}) collective-permute-start(bf16[288,128]{1,0:T(8,128)(2,1)S(1)} %update.1), channel_id=1, source_target_pairs={{0,8},{1,9},{2,10},{3,11},{4,12},{5,13},{6,14},{7,15},{8,0},{9,1},... | collective-permute-start | bytes 221192 | tf_op jit(solution)/shard_map/ab_far/ppermute | solution.py:53
  13.9 8.2 %collective-permute-start.2 = (bf16[32,4096]{1,0:T(8,128)(2,1)S(1)}, bf16[32,4096]{1,0:T(8,128)(2,1)S(1)}, u32[]{:S(2)}, u32[]{:S(2)}) collective-permute-start(bf16[32,4096]{1,0:T(8,128)(2,1)S(1)} %collective-permute-done.refs_1_), channel_id=1, source_target_pairs={{0,17},{1,16},{2,19},{3,18},{4,21},{5,20},{6,23},{7,22},{8,25},{9,... | collective-permute-start | bytes 786440 | tf_op jit(solution)/shard_map/w3/ppermute | solution.py:53
  14.2 9.0 %collective-permute-start.3 = (bf16[32,4096]{1,0:T(8,128)(2,1)S(1)}, bf16[32,4096]{1,0:T(8,128)(2,1)S(1)}, u32[]{:S(2)}, u32[]{:S(2)}) collective-permute-start(bf16[32,4096]{1,0:T(8,128)(2,1)S(1)} %collective-permute-done.refs_1_), channel_id=1, source_target_pairs={{0,2},{1,3},{2,0},{3,1},{4,6},{5,7},{6,4},{7,5},{8,10},{9,11},{10,... | collective-permute-start | bytes 786440 | tf_op jit(solution)/shard_map/w4/ppermute | solution.py:53
  15.7 9.4 %collective-permute-start.4 = (bf16[32,4096]{1,0:T(8,128)(2,1)S(1)}, bf16[32,4096]{1,0:T(8,128)(2,1)S(1)}, u32[]{:S(2)}, u32[]{:S(2)}) collective-permute-start(bf16[32,4096]{1,0:T(8,128)(2,1)S(1)} %collective-permute-done.refs_1_), channel_id=1, source_target_pairs={{0,4},{1,9},{2,6},{3,11},{4,0},{5,13},{6,2},{7,15},{8,12},{9,1},{1... | collective-permute-start | bytes 786440 | tf_op jit(solution)/shard_map/w5/ppermute | solution.py:53
  17.3 7.8 %collective-permute-start.11 = (bf16[576,128]{1,0:T(8,128)(2,1)S(1)}, bf16[576,128]{1,0:T(8,128)(2,1)S(1)}, u32[]{:S(2)}, u32[]{:S(2)}) collective-permute-start(bf16[576,128]{1,0:T(8,128)(2,1)S(1)} %pad_maximum_fusion.2.refs_0_.first_ref), channel_id=1, source_target_pairs={{0,1},{1,0},{2,3},{3,2},{4,5},{5,4},{6,7},{7,6},{8,9},{9,8},{10,11... | collective-permute-start | bytes 442376 | tf_op jit(solution)/shard_map/other_0/ppermute | solution.py:53
  22.0 6.3 %collective-permute-start.13 = (bf16[576,128]{1,0:T(8,128)(2,1)S(1)}, bf16[576,128]{1,0:T(8,128)(2,1)S(1)}, u32[]{:S(2)}, u32[]{:S(2)}) collective-permute-start(bf16[576,128]{1,0:T(8,128)(2,1)S(1)} %pad_maximum_fusion.2.refs_0_.first_ref), channel_id=1, source_target_pairs={{0,4},{1,5},{2,6},{3,7},{4,0},{5,1},{6,2},{7,3},{8,12},{9,13},{10,... | collective-permute-start | bytes 442376 | tf_op jit(solution)/shard_map/ab_1/ppermute | solution.py:53
  23.2 5.7 %collective-permute-start.14 = (bf16[576,128]{1,0:T(8,128)(2,1)S(1)}, bf16[576,128]{1,0:T(8,128)(2,1)S(1)}, u32[]{:S(2)}, u32[]{:S(2)}) collective-permute-start(bf16[576,128]{1,0:T(8,128)(2,1)S(1)} %pad_maximum_fusion.2.refs_0_.first_ref), channel_id=1, source_target_pairs={{0,2},{1,3},{2,0},{3,1},{4,6},{5,7},{6,4},{7,5},{8,10},{9,11},{10,... | collective-permute-start | bytes 442376 | tf_op jit(solution)/shard_map/ab_2/ppermute | solution.py:53
  25.1 8.2 %collective-permute-start.5 = (bf16[32,4096]{1,0:T(8,128)(2,1)S(1)}, bf16[32,4096]{1,0:T(8,128)(2,1)S(1)}, u32[]{:S(2)}, u32[]{:S(2)}) collective-permute-start(bf16[32,4096]{1,0:T(8,128)(2,1)S(1)} %collective-permute-done.3.first_ref.refs_4_), channel_id=1, source_target_pairs={{0,17},{1,16},{2,19},{3,18},{4,21},{5,20},{6,23},{7,22},{8,25},{9,... | collective-permute-start | bytes 786440 | tf_op jit(solution)/shard_map/w6/ppermute | solution.py:53
  25.1 6.6 %collective-permute-start.6 = (bf16[32,4096]{1,0:T(8,128)(2,1)S(1)}, bf16[32,4096]{1,0:T(8,128)(2,1)S(1)}, u32[]{:S(2)}, u32[]{:S(2)}) collective-permute-start(bf16[32,4096]{1,0:T(8,128)(2,1)S(1)} %pick.1), channel_id=1, source_target_pairs={{0,4},{1,3},{2,6},{3,1},{4,0},{5,7},{6,2},{7,5},{8,12},{9,11},{10,... | collective-permute-start | bytes 786440 | tf_op jit(solution)/shard_map/w7/ppermute | solution.py:53
  27.2 3.5 %collective-permute-start.12 = (f32[256,192]{1,0:T(8,128)S(1)}, f32[256,192]{1,0:T(8,128)S(1)}, u32[]{:S(2)}, u32[]{:S(2)}) collective-permute-start(f32[256,192]{1,0:T(8,128)S(1)} %get-tuple-element.39), channel_id=1, source_target_pairs={{0,1},{1,0},{2,3},{3,2},{4,5},{5,4},{6,7},{7,6},{8,9},{9,8},{10,11... | collective-permute-start | bytes 589832 | tf_op jit(solution)/shard_map/received/ppermute | solution.py:53
  28.3 1.4 %collective-permute-start.15 = (bf16[576,128]{1,0:T(8,128)(2,1)S(1)}, bf16[576,128]{1,0:T(8,128)(2,1)S(1)}, u32[]{:S(2)}, u32[]{:S(2)}) collective-permute-start(bf16[576,128]{1,0:T(8,128)(2,1)S(1)} %collective-permute-done.13.refs_1_), channel_id=1, source_target_pairs={{0,1},{1,0},{2,3},{3,2},{4,5},{5,4},{6,7},{7,6},{8,9},{9,8},{10,11... | collective-permute-start | bytes 442376 | tf_op jit(solution)/shard_map/other_1/ppermute | solution.py:53
  28.9 1.9 %collective-permute-start.16 = (bf16[576,128]{1,0:T(8,128)(2,1)S(1)}, bf16[576,128]{1,0:T(8,128)(2,1)S(1)}, u32[]{:S(2)}, u32[]{:S(2)}) collective-permute-start(bf16[576,128]{1,0:T(8,128)(2,1)S(1)} %collective-permute-done.14.refs_2_), channel_id=1, source_target_pairs={{0,1},{1,0},{2,3},{3,2},{4,5},{5,4},{6,7},{7,6},{8,9},{9,8},{10,11... | collective-permute-start | bytes 442376 | tf_op jit(solution)/shard_map/other_2/ppermute | solution.py:53
  29.7 6.1 %collective-permute-start.19 = (bf16[576,128]{1,0:T(8,128)(2,1)S(1)}, bf16[576,128]{1,0:T(8,128)(2,1)S(1)}, u32[]{:S(2)}, u32[]{:S(2)}) collective-permute-start(bf16[576,128]{1,0:T(8,128)(2,1)S(1)} %collective-permute-done.13.refs_1_), channel_id=1, source_target_pairs={{0,2},{1,3},{2,0},{3,1},{4,6},{5,7},{6,4},{7,5},{8,10},{9,11},{10,... | collective-permute-start | bytes 442376 | tf_op jit(solution)/shard_map/ab_3/ppermute | solution.py:53
  33.3 2.5 %collective-permute-start.17 = (bf16[32,4096]{1,0:T(8,128)(2,1)S(1)}, bf16[32,4096]{1,0:T(8,128)(2,1)S(1)}, u32[]{:S(2)}, u32[]{:S(2)}) collective-permute-start(bf16[32,4096]{1,0:T(8,128)(2,1)S(1)} %collective-permute-done.5.refs_0_), channel_id=1, source_target_pairs={{0,1},{1,0},{2,3},{3,2},{4,5},{5,4},{6,7},{7,6},{8,9},{9,8},{10,11... | collective-permute-start | bytes 786440 | tf_op jit(solution)/shard_map/other_late/ppermute | solution.py:53
  33.3 2.5 %collective-permute-start.18 = (bf16[32,4096]{1,0:T(8,128)(2,1)S(1)}, bf16[32,4096]{1,0:T(8,128)(2,1)S(1)}, u32[]{:S(2)}, u32[]{:S(2)}) collective-permute-start(bf16[32,4096]{1,0:T(8,128)(2,1)S(1)} %collective-permute-done.6.refs_1_), channel_id=1, source_target_pairs={{0,1},{1,0},{2,3},{3,2},{4,5},{5,4},{6,7},{7,6},{8,9},{9,8},{10,11... | collective-permute-start | bytes 786440 | tf_op jit(solution)/shard_map/other_late/ppermute | solution.py:53
  35.8 1.4 %collective-permute-start.20 = (bf16[576,128]{1,0:T(8,128)(2,1)S(1)}, bf16[576,128]{1,0:T(8,128)(2,1)S(1)}, u32[]{:S(2)}, u32[]{:S(2)}) collective-permute-start(bf16[576,128]{1,0:T(8,128)(2,1)S(1)} %collective-permute-done.19.refs_0_), channel_id=1, source_target_pairs={{0,1},{1,0},{2,3},{3,2},{4,5},{5,4},{6,7},{7,6},{8,9},{9,8},{10,11... | collective-permute-start | bytes 442376 | tf_op jit(solution)/shard_map/other_3/ppermute | solution.py:53

commit v4 on v3

--- a/solution.py
+++ b/solution.py
@@ -12,12 +12,10 @@
 NT = (((1,), (1,)), ((), ()))
 NN = (((1,), (0,)), ((), ()))
 VMEM_LIMIT = 16 * 1024 * 1024
-WIDE_LIMIT = 58 * 1024 * 1024
 EARLY = 6
 U_FLOPS = 4e9
 L_FLOPS = 1e6
-P_FLOPS = 0
-W_FLOPS = 1
+W_FLOPS = 4
 M_FLOPS = 1
 
 
@@ -39,7 +37,6 @@
 
 CORE, Y, Z1, Z2 = (0, 1), (0, 2), (0, 4), (0, 8)
 REPLICA, X = (1, 0), (1, 1)
-ZY1, ZY2 = (0, 6), (0, 10)
 
 
 def send(rows, group, move, other_move=None, name="sent"):
@@ -143,8 +140,10 @@
     b_own = ab_refs[0][rows_a : rows_a + rows_b]
     n = len(at)
     blocks = [(ref, 0, at[i], 0) for i, ref in enumerate(ab_refs[:n])]
-    joined = len(ab_refs) == n + 1
-    blocks += [(ab_refs[n if joined else n + i], 1, k, 2 * i if joined else 0) for i, k in enumerate(at)]
+    rest = ab_refs[n:]
+    separate = len(rest) if len(rest) == n else len(rest) - 1
+    blocks += [(rest[i], 1, at[i], 0) for i in range(separate)]
+    blocks += [(rest[-1], 1, at[i], 2 * (i - separate)) for i in range(separate, n)]
     t_ref[...] = add_blocks(h_ref, w_ref, b_own, merged_ref, b_all, blocks, jnp.zeros(t_ref.shape, jnp.float32))
 
 
@@ -172,18 +171,6 @@
     out_ref[...] = out.astype(jnp.bfloat16)
 
 
-def pick_kernel(first_ref, second_ref, out_ref):
-    x, _, core = position()
-
-    @pl.when(core == x)
-    def _():
-        out_ref[...] = first_ref[...]
-
-    @pl.when(core != x)
-    def _():
-        out_ref[...] = second_ref[...]
-
-
 def cost(flops, number_of_bytes):
     return pl.CostEstimate(flops=int(flops), bytes_accessed=int(number_of_bytes), transcendentals=0)
 
@@ -195,10 +182,8 @@
     rows_a, rows_b = adapter_a.shape[0], weight.shape[0]
     outputs = rows_b * group[1]
 
-    any_space = pl.BlockSpec(memory_space=pltpu.HBM)
     vmem = pl.BlockSpec(memory_space=pltpu.VMEM)
     params = pltpu.CompilerParams(vmem_limit_bytes=VMEM_LIMIT)
-    wide = pltpu.CompilerParams(vmem_limit_bytes=WIDE_LIMIT)
     bf16, f32 = jnp.bfloat16, jnp.float32
 
     hold = lax.optimization_barrier
@@ -230,19 +215,10 @@
     ab_1 = send(ab_0, group, Z1, name="ab_1")
     ab_2 = send(ab_0, group, Y, name="ab_2")
     other_0 = send(ab_0, group, CORE, name="other_0")
-    ab_3 = send(ab_1, group, Y, name="ab_3")
-    w3, w4, w5 = hold((w3, w4, w5))
+    ab_3 = send(ab_2, group, Z1, name="ab_3")
+    w3, w4 = hold((w3, w4))
     w6 = send(w4, group, X, name="w6")
-    mixed = pl.pallas_call(
-        pick_kernel,
-        out_shape=jax.ShapeDtypeStruct(weight.shape, bf16),
-        in_specs=[vmem] * 2,
-        out_specs=vmem,
-        compiler_params=params,
-        cost_estimate=cost(P_FLOPS, 0),
-        name="pick",
-    )(w4, w5)
-    w7 = send(mixed, group, Z1, Y, name="w7")
+    w7 = send(w5, group, Y, name="w7")
     held = [w0, w1, w2, w3, w4, w5, w6, w7]
     other_1 = send(ab_1, group, CORE, name="other_1")
     other_2 = send(ab_2, group, CORE, name="other_2")

time: 38.8 us -> 38.1 us (0.982)
  starting transfers between devices: 17.5 us -> 15.9 us
  waiting for transfers between devices: 13.6 us -> 14.5 us
    ppermute x21, starting transfers between devices: 17.5 us -> 15.9 us  [send(): return lax.ppermute(rows, AXES, pairs)]
    ppermute x21, waiting for transfers between devices: 13.6 us -> 14.5 us  [send(): return lax.ppermute(rows, AXES, pairs)]
  transfers between devices with their start and end apart: 21 -> 21, of which waited for: 10 -> 13; matrix products, arithmetic and copies ran while one was open for 5% -> 5% of each run, Pallas kernels for 9% -> 9%
where the time goes in v4:
time: 38.1 us; the launch traced here: 37.8 us
  starting transfers between devices  15.9 us (42%)
  waiting for transfers between devices  14.5 us (38%)
  Pallas kernels  4.73 us (12%)
  other arithmetic  1.88 us (5%)
  between operations  0.71 us (2%)
    ppermute x21, starting transfers between devices, send(): return lax.ppermute(rows, AXES, pairs)  15.9 us
    ppermute x21, waiting for transfers between devices, send(): return lax.ppermute(rows, AXES, pairs)  14.5 us
    pallas_call x1, Pallas kernels, paired(): pl.pallas_call(weight_kernel, out_shape=[jax.ShapeDtypeStruct((tokens, co...  1.25 us
    pallas_call x1, Pallas kernels, paired(): pl.pallas_call(functools.partial(last_kernel, (3,)), out_shape=[jax.Shape...  1.25 us
    pallas_call x1, Pallas kernels, paired(): pl.pallas_call(functools.partial(late_kernel, tuple(range(EARLY, len(HELD...  1.17 us
    pallas_call x1, Pallas kernels, paired(): pl.pallas_call(functools.partial(middle_kernel, middle, EARLY), out_shape...  1.01 us
    concatenate x1, other arithmetic, paired(): mine = jnp.concatenate([grad_a[0], grad_b[0]])  0.93 us
    concatenate x1, other arithmetic, paired(): old = jnp.concatenate([adapter_a, adapter_b])  0.93 us
  transfers between devices with their start and end apart: 21, of which 13 were waited for; matrix products, arithmetic and copies ran while one was open for 5% of the time, Pallas kernels for 9%

profile of v4, /device:TPU:0, one launch (start us, length us, event | category | flops | bytes accessed | tf_op | source)
XLA Modules:
  0.0 37.8 jit_solution(2235228056132693158)
XLA Ops:
  1.1 3.7 %collective-permute-start = (bf16[32,4096]{1,0:T(8,128)(2,1)}, bf16[32,4096]{1,0:T(8,128)(2,1)S(1)}, u32[]{:S(2)}, u32[]{:S(2)}) collective-permute-start(bf16[32,4096]{1,0:T(8,128)(2,1)} %w_ref.3), channel_id=1, source_target_pairs={{0,8},{1,5},{2,10},{3,7},{4,12},{5,1},{6,14},{7,3},{8,0},{9,13},{1... | collective-permute-start | bytes 786440 | tf_op jit(solution)/shard_map/w1/ppermute | solution.py:50
  4.8 1.5 %collective-permute-start.1 = (bf16[32,4096]{1,0:T(8,128)(2,1)}, bf16[32,4096]{1,0:T(8,128)(2,1)S(1)}, u32[]{:S(2)}, u32[]{:S(2)}) collective-permute-start(bf16[32,4096]{1,0:T(8,128)(2,1)} %w_ref.3), channel_id=1, source_target_pairs={{0,2},{1,3},{2,0},{3,1},{4,6},{5,7},{6,4},{7,5},{8,10},{9,11},{10,... | collective-permute-start | bytes 786440 | tf_op jit(solution)/shard_map/w2/ppermute | solution.py:50
  6.8 1.5 %collective-permute-start.9 = (f32[1,32,128]{2,1,0:T(8,128)}, f32[1,32,128]{2,1,0:T(8,128)S(1)}, u32[]{:S(2)}, u32[]{:S(2)}) collective-permute-start(f32[1,32,128]{2,1,0:T(8,128)} %param.11), channel_id=1, source_target_pairs={{0,16},{1,17},{2,18},{3,19},{4,20},{5,21},{6,22},{7,23},{8,24},{9,... | collective-permute-start | bytes 49160 | tf_op jit(solution)/shard_map/other_b/ppermute | solution.py:50
  8.4 0.9 %pad_maximum_fusion.old_ref = f32[288,128]{1,0:T(8,128)S(1)} fusion(f32[32,128]{1,0:T(8,128)} %param.9, f32[256,128]{1,0:T(8,128)} %param.8), kind=kLoop, calls=%fused_computation | loop fusion | flops 36864 | bytes 294912 | tf_op jit(solution)/shard_map/concatenate | solution.py:191
  9.3 0.9 %pad_maximum_fusion.1.own_ref = f32[288,128]{1,0:T(8,128)S(1)} fusion(f32[32,128]{1,0:T(8,128)} %bitcast.3, f32[256,128]{1,0:T(8,128)} %bitcast.2), kind=kLoop, calls=%fused_computation.1 | loop fusion | flops 36864 | bytes 294912 | tf_op jit(solution)/shard_map/concatenate | solution.py:192
  10.3 1.7 %collective-permute-done.9.ob_ref = f32[1,32,128]{2,1,0:T(8,128)S(1)} collective-permute-done((f32[1,32,128]{2,1,0:T(8,128)}, f32[1,32,128]{2,1,0:T(8,128)S(1)}, u32[]{:S(2)}, u32[]{:S(2)}) %collective-permute-start.9) | collective-permute-done | bytes 16416 | tf_op jit(solution)/shard_map/other_b/ppermute | solution.py:50
  12.0 1.9 %collective-permute-start.10 = (bf16[288,128]{1,0:T(8,128)(2,1)S(1)}, bf16[288,128]{1,0:T(8,128)(2,1)S(1)}, u32[]{:S(2)}, u32[]{:S(2)}) collective-permute-start(bf16[288,128]{1,0:T(8,128)(2,1)S(1)} %update.1), channel_id=1, source_target_pairs={{0,8},{1,9},{2,10},{3,11},{4,12},{5,13},{6,14},{7,15},{8,0},{9,1},... | collective-permute-start | bytes 221192 | tf_op jit(solution)/shard_map/ab_far/ppermute | solution.py:50
  14.2 1.5 %collective-permute-start.3 = (bf16[32,4096]{1,0:T(8,128)(2,1)S(1)}, bf16[32,4096]{1,0:T(8,128)(2,1)S(1)}, u32[]{:S(2)}, u32[]{:S(2)}) collective-permute-start(bf16[32,4096]{1,0:T(8,128)(2,1)S(1)} %collective-permute-done.refs_1_), channel_id=1, source_target_pairs={{0,2},{1,3},{2,0},{3,1},{4,6},{5,7},{6,4},{7,5},{8,10},{9,11},{10,... | collective-permute-start | bytes 786440 | tf_op jit(solution)/shard_map/w4/ppermute | solution.py:50
  16.1 1.2 %collective-permute-done.10 = bf16[288,128]{1,0:T(8,128)(2,1)S(1)} collective-permute-done((bf16[288,128]{1,0:T(8,128)(2,1)S(1)}, bf16[288,128]{1,0:T(8,128)(2,1)S(1)}, u32[]{:S(2)}, u32[]{:S(2)}) %collective-permute-start.10) | collective-permute-done | bytes 73760 | tf_op jit(solution)/shard_map/ab_far/ppermute | solution.py:50
  17.4 4.7 %collective-permute-done.2.refs_3_ = bf16[32,4096]{1,0:T(8,128)(2,1)S(1)} collective-permute-done((bf16[32,4096]{1,0:T(8,128)(2,1)S(1)}, bf16[32,4096]{1,0:T(8,128)(2,1)S(1)}, u32[]{:S(2)}, u32[]{:S(2)}) %collective-permute-start.2) | collective-permute-done | bytes 262176 | tf_op jit(solution)/shard_map/w3/ppermute | solution.py:50
  22.0 0.8 %collective-permute-start.14 = (bf16[576,128]{1,0:T(8,128)(2,1)S(1)}, bf16[576,128]{1,0:T(8,128)(2,1)S(1)}, u32[]{:S(2)}, u32[]{:S(2)}) collective-permute-start(bf16[576,128]{1,0:T(8,128)(2,1)S(1)} %pad_maximum_fusion.2.refs_0_.first_ref), channel_id=1, source_target_pairs={{0,2},{1,3},{2,0},{3,1},{4,6},{5,7},{6,4},{7,5},{8,10},{9,11},{10,... | collective-permute-start | bytes 442376 | tf_op jit(solution)/shard_map/ab_2/ppermute | solution.py:50
  23.5 0.7 %collective-permute-start.4 = (bf16[32,4096]{1,0:T(8,128)(2,1)S(1)}, bf16[32,4096]{1,0:T(8,128)(2,1)S(1)}, u32[]{:S(2)}, u32[]{:S(2)}) collective-permute-start(bf16[32,4096]{1,0:T(8,128)(2,1)S(1)} %collective-permute-done.3.refs_4_), channel_id=1, source_target_pairs={{0,17},{1,16},{2,19},{3,18},{4,21},{5,20},{6,23},{7,22},{8,25},{9,... | collective-permute-start | bytes 786440 | tf_op jit(solution)/shard_map/w6/ppermute | solution.py:50
  24.1 0.8 %collective-permute-done.5.refs_5_ = bf16[32,4096]{1,0:T(8,128)(2,1)S(1)} collective-permute-done((bf16[32,4096]{1,0:T(8,128)(2,1)S(1)}, bf16[32,4096]{1,0:T(8,128)(2,1)S(1)}, u32[]{:S(2)}, u32[]{:S(2)}) %collective-permute-start.5) | collective-permute-done | bytes 262176 | tf_op jit(solution)/shard_map/w5/ppermute | solution.py:50
  25.0 1.3 %weight_product.1 = (f32[256,192]{1,0:T(8,128)S(1)}, f32[256,192]{1,0:T(8,128)S(1)}) custom-call(bf16[256,4096]{1,0:T(8,128)(2,1)S(1)} %copy-done, bf16[256,4096]{1,0:T(8,128)(2,1)S(1)} %collective-permute-done.7.hs_ref, bf16[32,4096]{1,0:T(8,128)(2,1)S(1)} %copy-done.1, bf16[32,4096]{1,0:T(8,128)(2,1)S(1)} %collective-permute-done.refs_1_, ...), custom_call_target="tpu_custom_call" | custom-call | flops 3221225472 | bytes 5767168 | tf_op jit(solution)/shard_map/weight_product/pallas_call | solution.py:233
  26.2 0.7 %collective-permute-start.12 = (f32[256,192]{1,0:T(8,128)S(1)}, f32[256,192]{1,0:T(8,128)S(1)}, u32[]{:S(2)}, u32[]{:S(2)}) collective-permute-start(f32[256,192]{1,0:T(8,128)S(1)} %get-tuple-element.37), channel_id=1, source_target_pairs={{0,1},{1,0},{2,3},{3,2},{4,5},{5,4},{6,7},{7,6},{8,9},{9,8},{10,11... | collective-permute-start | bytes 589832 | tf_op jit(solution)/shard_map/received/ppermute | solution.py:50
  27.0 0.7 %collective-permute-done.14.refs_2_ = bf16[576,128]{1,0:T(8,128)(2,1)S(1)} collective-permute-done((bf16[576,128]{1,0:T(8,128)(2,1)S(1)}, bf16[576,128]{1,0:T(8,128)(2,1)S(1)}, u32[]{:S(2)}, u32[]{:S(2)}) %collective-permute-start.14) | collective-permute-done | bytes 147488 | tf_op jit(solution)/shard_map/ab_2/ppermute | solution.py:50
  27.6 1.2 %collective-permute-done.13.refs_1_ = bf16[576,128]{1,0:T(8,128)(2,1)S(1)} collective-permute-done((bf16[576,128]{1,0:T(8,128)(2,1)S(1)}, bf16[576,128]{1,0:T(8,128)(2,1)S(1)}, u32[]{:S(2)}, u32[]{:S(2)}) %collective-permute-start.13) | collective-permute-done | bytes 147488 | tf_op jit(solution)/shard_map/ab_1/ppermute | solution.py:50
  29.0 1.0 %collective-permute-start.19 = (bf16[576,128]{1,0:T(8,128)(2,1)S(1)}, bf16[576,128]{1,0:T(8,128)(2,1)S(1)}, u32[]{:S(2)}, u32[]{:S(2)}) collective-permute-start(bf16[576,128]{1,0:T(8,128)(2,1)S(1)} %collective-permute-done.14.refs_2_), channel_id=1, source_target_pairs={{0,4},{1,5},{2,6},{3,7},{4,0},{5,1},{6,2},{7,3},{8,12},{9,13},{10,... | collective-permute-start | bytes 442376 | tf_op jit(solution)/shard_map/ab_3/ppermute | solution.py:50
  30.3 1.0 %middle.1 = (f32[256,128]{1,0:T(8,128)S(1)}, f32[256,512]{1,0:T(8,128)S(1)}, bf16[32,4096]{1,0:T(8,128)(2,1)S(1)}, bf16[512,128]{1,0:T(8,128)(2,1)S(1)}) custom-call(bf16[256,4096]{1,0:T(8,128)(2,1)S(1)} %copy-done, bf16[32,4096]{1,0:T(8,128)(2,1)S(1)} %copy-done.1, f32[256,192]{1,0:T(8,128)S(1)} %get-tuple-element.36.own_ref, ...), custom_call_target="tpu_custom_call" | custom-call | flops 268435456 | bytes 3145728 | tf_op jit(solution)/shard_map/middle/pallas_call | solution.py:245
  31.3 0.6 %collective-permute-done.4.refs_0_ = bf16[32,4096]{1,0:T(8,128)(2,1)S(1)} collective-permute-done((bf16[32,4096]{1,0:T(8,128)(2,1)S(1)}, bf16[32,4096]{1,0:T(8,128)(2,1)S(1)}, u32[]{:S(2)}, u32[]{:S(2)}) %collective-permute-start.4) | collective-permute-done | bytes 262176 | tf_op jit(solution)/shard_map/w6/ppermute | solution.py:50
  31.8 1.3 %collective-permute-done.6.refs_1_ = bf16[32,4096]{1,0:T(8,128)(2,1)S(1)} collective-permute-done((bf16[32,4096]{1,0:T(8,128)(2,1)S(1)}, bf16[32,4096]{1,0:T(8,128)(2,1)S(1)}, u32[]{:S(2)}, u32[]{:S(2)}) %collective-permute-start.6) | collective-permute-done | bytes 262176 | tf_op jit(solution)/shard_map/w7/ppermute | solution.py:50
  33.7 1.5 %collective-permute-done.19.refs_0_ = bf16[576,128]{1,0:T(8,128)(2,1)S(1)} collective-permute-done((bf16[576,128]{1,0:T(8,128)(2,1)S(1)}, bf16[576,128]{1,0:T(8,128)(2,1)S(1)}, u32[]{:S(2)}, u32[]{:S(2)}) %collective-permute-start.19) | collective-permute-done | bytes 147488 | tf_op jit(solution)/shard_map/ab_3/ppermute | solution.py:50
  35.2 1.2 %late_product.1.high_ref = f32[256,512]{1,0:T(8,128)S(1)} custom-call(bf16[256,4096]{1,0:T(8,128)(2,1)S(1)} %copy-done, f32[256,512]{1,0:T(8,128)S(1)} %get-tuple-element.41.high_ref, bf16[32,4096]{1,0:T(8,128)(2,1)S(1)} %collective-permute-done.4.refs_0_, bf16[32,4096]{1,0:T(8,128)(2,1)S(1)} %collective-permute-done.6.refs_1_, ...), custom_call_target="tpu_custom_call" | custom-call | flops 1000000 | bytes 262144 | tf_op jit(solution)/shard_map/late_product/pallas_call | solution.py:261
  36.5 1.3 %last.1 = (bf16[256,512]{1,0:T(8,128)(2,1)}, bf16[32,4096]{1,0:T(8,128)(2,1)}) custom-call(bf16[256,4096]{1,0:T(8,128)(2,1)S(1)} %copy-done, bf16[32,4096]{1,0:T(8,128)(2,1)S(1)} %copy-done.1, f32[256,128]{1,0:T(8,128)S(1)} %get-tuple-element.40.t_ref, f32[256,512]{1,0:T(8,128)S(1)} %late_product.1.high_ref, bf16[32,4096]{1,0:T(8,128)(2,1)S(1)} %get-tuple-element.44.m_ref, ...), custom_call_target="tpu_custom_call" | custom-call | flops 33554432 | bytes 262144 | tf_op jit(solution)/shard_map/last/pallas_call | solution.py:270
  (30 shorter events, 3.7 us)
Async XLA Ops:
  0.6 24.3 %collective-permute-start.7 = (bf16[256,4096]{1,0:T(8,128)(2,1)}, bf16[256,4096]{1,0:T(8,128)(2,1)S(1)}, u32[]{:S(2)}, u32[]{:S(2)}) collective-permute-start(bf16[256,4096]{1,0:T(8,128)(2,1)} %h_ref.7), channel_id=1, source_target_pairs={{0,1},{1,0},{2,3},{3,2},{4,5},{5,4},{6,7},{7,6},{8,9},{9,8},{10,11... | collective-permute-start | bytes 6291464 | tf_op jit(solution)/shard_map/other_hidden/ppermute | solution.py:50
  1.1 12.7 %collective-permute-start = (bf16[32,4096]{1,0:T(8,128)(2,1)}, bf16[32,4096]{1,0:T(8,128)(2,1)S(1)}, u32[]{:S(2)}, u32[]{:S(2)}) collective-permute-start(bf16[32,4096]{1,0:T(8,128)(2,1)} %w_ref.3), channel_id=1, source_target_pairs={{0,8},{1,5},{2,10},{3,7},{4,12},{5,1},{6,14},{7,3},{8,0},{9,13},{1... | collective-permute-start | bytes 786440 | tf_op jit(solution)/shard_map/w1/ppermute | solution.py:50
  4.8 9.0 %collective-permute-start.1 = (bf16[32,4096]{1,0:T(8,128)(2,1)}, bf16[32,4096]{1,0:T(8,128)(2,1)S(1)}, u32[]{:S(2)}, u32[]{:S(2)}) collective-permute-start(bf16[32,4096]{1,0:T(8,128)(2,1)} %w_ref.3), channel_id=1, source_target_pairs={{0,2},{1,3},{2,0},{3,1},{4,6},{5,7},{6,4},{7,5},{8,10},{9,11},{10,... | collective-permute-start | bytes 786440 | tf_op jit(solution)/shard_map/w2/ppermute | solution.py:50
  6.3 5.6 %collective-permute-start.8 = (f32[1,256,128]{2,1,0:T(8,128)}, f32[1,256,128]{2,1,0:T(8,128)S(1)}, u32[]{:S(2)}, u32[]{:S(2)}) collective-permute-start(f32[1,256,128]{2,1,0:T(8,128)} %param.10), channel_id=1, source_target_pairs={{0,16},{1,17},{2,18},{3,19},{4,20},{5,21},{6,22},{7,23},{8,24},{9,... | collective-permute-start | bytes 393224 | tf_op jit(solution)/shard_map/other_a/ppermute | solution.py:50
  6.8 5.1 %collective-permute-start.9 = (f32[1,32,128]{2,1,0:T(8,128)}, f32[1,32,128]{2,1,0:T(8,128)S(1)}, u32[]{:S(2)}, u32[]{:S(2)}) collective-permute-start(f32[1,32,128]{2,1,0:T(8,128)} %param.11), channel_id=1, source_target_pairs={{0,16},{1,17},{2,18},{3,19},{4,20},{5,21},{6,22},{7,23},{8,24},{9,... | collective-permute-start | bytes 49160 | tf_op jit(solution)/shard_map/other_b/ppermute | solution.py:50
  10.2 14.7 %copy-start = (bf16[256,4096]{1,0:T(8,128)(2,1)S(1)}, bf16[256,4096]{1,0:T(8,128)(2,1)}, u32[]{:S(2)}) copy-start(bf16[256,4096]{1,0:T(8,128)(2,1)} %h_ref.7) | copy-start | bytes 6291460
  10.2 14.7 %copy-start.1 = (bf16[32,4096]{1,0:T(8,128)(2,1)S(1)}, bf16[32,4096]{1,0:T(8,128)(2,1)}, u32[]{:S(2)}) copy-start(bf16[32,4096]{1,0:T(8,128)(2,1)} %w_ref.3) | copy-start | bytes 786436
  12.0 5.3 %collective-permute-start.10 = (bf16[288,128]{1,0:T(8,128)(2,1)S(1)}, bf16[288,128]{1,0:T(8,128)(2,1)S(1)}, u32[]{:S(2)}, u32[]{:S(2)}) collective-permute-start(bf16[288,128]{1,0:T(8,128)(2,1)S(1)} %update.1), channel_id=1, source_target_pairs={{0,8},{1,9},{2,10},{3,11},{4,12},{5,13},{6,14},{7,15},{8,0},{9,1},... | collective-permute-start | bytes 221192 | tf_op jit(solution)/shard_map/ab_far/ppermute | solution.py:50
  13.9 8.2 %collective-permute-start.2 = (bf16[32,4096]{1,0:T(8,128)(2,1)S(1)}, bf16[32,4096]{1,0:T(8,128)(2,1)S(1)}, u32[]{:S(2)}, u32[]{:S(2)}) collective-permute-start(bf16[32,4096]{1,0:T(8,128)(2,1)S(1)} %collective-permute-done.refs_1_), channel_id=1, source_target_pairs={{0,17},{1,16},{2,19},{3,18},{4,21},{5,20},{6,23},{7,22},{8,25},{9,... | collective-permute-start | bytes 786440 | tf_op jit(solution)/shard_map/w3/ppermute | solution.py:50
  14.2 9.0 %collective-permute-start.3 = (bf16[32,4096]{1,0:T(8,128)(2,1)S(1)}, bf16[32,4096]{1,0:T(8,128)(2,1)S(1)}, u32[]{:S(2)}, u32[]{:S(2)}) collective-permute-start(bf16[32,4096]{1,0:T(8,128)(2,1)S(1)} %collective-permute-done.refs_1_), channel_id=1, source_target_pairs={{0,2},{1,3},{2,0},{3,1},{4,6},{5,7},{6,4},{7,5},{8,10},{9,11},{10,... | collective-permute-start | bytes 786440 | tf_op jit(solution)/shard_map/w4/ppermute | solution.py:50
  15.7 9.2 %collective-permute-start.5 = (bf16[32,4096]{1,0:T(8,128)(2,1)S(1)}, bf16[32,4096]{1,0:T(8,128)(2,1)S(1)}, u32[]{:S(2)}, u32[]{:S(2)}) collective-permute-start(bf16[32,4096]{1,0:T(8,128)(2,1)S(1)} %collective-permute-done.refs_1_), channel_id=1, source_target_pairs={{0,4},{1,9},{2,6},{3,11},{4,0},{5,13},{6,2},{7,15},{8,12},{9,1},{1... | collective-permute-start | bytes 786440 | tf_op jit(solution)/shard_map/w5/ppermute | solution.py:50
  17.3 6.2 %collective-permute-start.11 = (bf16[576,128]{1,0:T(8,128)(2,1)S(1)}, bf16[576,128]{1,0:T(8,128)(2,1)S(1)}, u32[]{:S(2)}, u32[]{:S(2)}) collective-permute-start(bf16[576,128]{1,0:T(8,128)(2,1)S(1)} %pad_maximum_fusion.2.refs_0_.first_ref), channel_id=1, source_target_pairs={{0,1},{1,0},{2,3},{3,2},{4,5},{5,4},{6,7},{7,6},{8,9},{9,8},{10,11... | collective-permute-start | bytes 442376 | tf_op jit(solution)/shard_map/other_0/ppermute | solution.py:50
  22.0 5.6 %collective-permute-start.14 = (bf16[576,128]{1,0:T(8,128)(2,1)S(1)}, bf16[576,128]{1,0:T(8,128)(2,1)S(1)}, u32[]{:S(2)}, u32[]{:S(2)}) collective-permute-start(bf16[576,128]{1,0:T(8,128)(2,1)S(1)} %pad_maximum_fusion.2.refs_0_.first_ref), channel_id=1, source_target_pairs={{0,2},{1,3},{2,0},{3,1},{4,6},{5,7},{6,4},{7,5},{8,10},{9,11},{10,... | collective-permute-start | bytes 442376 | tf_op jit(solution)/shard_map/ab_2/ppermute | solution.py:50
  23.2 5.7 %collective-permute-start.13 = (bf16[576,128]{1,0:T(8,128)(2,1)S(1)}, bf16[576,128]{1,0:T(8,128)(2,1)S(1)}, u32[]{:S(2)}, u32[]{:S(2)}) collective-permute-start(bf16[576,128]{1,0:T(8,128)(2,1)S(1)} %pad_maximum_fusion.2.refs_0_.first_ref), channel_id=1, source_target_pairs={{0,4},{1,5},{2,6},{3,7},{4,0},{5,1},{6,2},{7,3},{8,12},{9,13},{10,... | collective-permute-start | bytes 442376 | tf_op jit(solution)/shard_map/ab_1/ppermute | solution.py:50
  23.5 8.3 %collective-permute-start.4 = (bf16[32,4096]{1,0:T(8,128)(2,1)S(1)}, bf16[32,4096]{1,0:T(8,128)(2,1)S(1)}, u32[]{:S(2)}, u32[]{:S(2)}) collective-permute-start(bf16[32,4096]{1,0:T(8,128)(2,1)S(1)} %collective-permute-done.3.refs_4_), channel_id=1, source_target_pairs={{0,17},{1,16},{2,19},{3,18},{4,21},{5,20},{6,23},{7,22},{8,25},{9,... | collective-permute-start | bytes 786440 | tf_op jit(solution)/shard_map/w6/ppermute | solution.py:50
  24.9 8.3 %collective-permute-start.6 = (bf16[32,4096]{1,0:T(8,128)(2,1)S(1)}, bf16[32,4096]{1,0:T(8,128)(2,1)S(1)}, u32[]{:S(2)}, u32[]{:S(2)}) collective-permute-start(bf16[32,4096]{1,0:T(8,128)(2,1)S(1)} %collective-permute-done.5.refs_5_), channel_id=1, source_target_pairs={{0,2},{1,3},{2,0},{3,1},{4,6},{5,7},{6,4},{7,5},{8,10},{9,11},{10,... | collective-permute-start | bytes 786440 | tf_op jit(solution)/shard_map/w7/ppermute | solution.py:50
  26.2 4.0 %collective-permute-start.12 = (f32[256,192]{1,0:T(8,128)S(1)}, f32[256,192]{1,0:T(8,128)S(1)}, u32[]{:S(2)}, u32[]{:S(2)}) collective-permute-start(f32[256,192]{1,0:T(8,128)S(1)} %get-tuple-element.37), channel_id=1, source_target_pairs={{0,1},{1,0},{2,3},{3,2},{4,5},{5,4},{6,7},{7,6},{8,9},{9,8},{10,11... | collective-permute-start | bytes 589832 | tf_op jit(solution)/shard_map/received/ppermute | solution.py:50
  27.6 1.4 %collective-permute-start.16 = (bf16[576,128]{1,0:T(8,128)(2,1)S(1)}, bf16[576,128]{1,0:T(8,128)(2,1)S(1)}, u32[]{:S(2)}, u32[]{:S(2)}) collective-permute-start(bf16[576,128]{1,0:T(8,128)(2,1)S(1)} %collective-permute-done.14.refs_2_), channel_id=1, source_target_pairs={{0,1},{1,0},{2,3},{3,2},{4,5},{5,4},{6,7},{7,6},{8,9},{9,8},{10,11... | collective-permute-start | bytes 442376 | tf_op jit(solution)/shard_map/other_2/ppermute | solution.py:50
  28.9 1.4 %collective-permute-start.15 = (bf16[576,128]{1,0:T(8,128)(2,1)S(1)}, bf16[576,128]{1,0:T(8,128)(2,1)S(1)}, u32[]{:S(2)}, u32[]{:S(2)}) collective-permute-start(bf16[576,128]{1,0:T(8,128)(2,1)S(1)} %collective-permute-done.13.refs_1_), channel_id=1, source_target_pairs={{0,1},{1,0},{2,3},{3,2},{4,5},{5,4},{6,7},{7,6},{8,9},{9,8},{10,11... | collective-permute-start | bytes 442376 | tf_op jit(solution)/shard_map/other_1/ppermute | solution.py:50
  29.0 6.1 %collective-permute-start.19 = (bf16[576,128]{1,0:T(8,128)(2,1)S(1)}, bf16[576,128]{1,0:T(8,128)(2,1)S(1)}, u32[]{:S(2)}, u32[]{:S(2)}) collective-permute-start(bf16[576,128]{1,0:T(8,128)(2,1)S(1)} %collective-permute-done.14.refs_2_), channel_id=1, source_target_pairs={{0,4},{1,5},{2,6},{3,7},{4,0},{5,1},{6,2},{7,3},{8,12},{9,13},{10,... | collective-permute-start | bytes 442376 | tf_op jit(solution)/shard_map/ab_3/ppermute | solution.py:50
  33.2 2.0 %collective-permute-start.17 = (bf16[32,4096]{1,0:T(8,128)(2,1)S(1)}, bf16[32,4096]{1,0:T(8,128)(2,1)S(1)}, u32[]{:S(2)}, u32[]{:S(2)}) collective-permute-start(bf16[32,4096]{1,0:T(8,128)(2,1)S(1)} %collective-permute-done.4.refs_0_), channel_id=1, source_target_pairs={{0,1},{1,0},{2,3},{3,2},{4,5},{5,4},{6,7},{7,6},{8,9},{9,8},{10,11... | collective-permute-start | bytes 786440 | tf_op jit(solution)/shard_map/other_late/ppermute | solution.py:50
  33.2 2.0 %collective-permute-start.18 = (bf16[32,4096]{1,0:T(8,128)(2,1)S(1)}, bf16[32,4096]{1,0:T(8,128)(2,1)S(1)}, u32[]{:S(2)}, u32[]{:S(2)}) collective-permute-start(bf16[32,4096]{1,0:T(8,128)(2,1)S(1)} %collective-permute-done.6.refs_1_), channel_id=1, source_target_pairs={{0,1},{1,0},{2,3},{3,2},{4,5},{5,4},{6,7},{7,6},{8,9},{9,8},{10,11... | collective-permute-start | bytes 786440 | tf_op jit(solution)/shard_map/other_late/ppermute | solution.py:50
  35.1 1.4 %collective-permute-start.20 = (bf16[576,128]{1,0:T(8,128)(2,1)S(1)}, bf16[576,128]{1,0:T(8,128)(2,1)S(1)}, u32[]{:S(2)}, u32[]{:S(2)}) collective-permute-start(bf16[576,128]{1,0:T(8,128)(2,1)S(1)} %collective-permute-done.19.refs_0_), channel_id=1, source_target_pairs={{0,1},{1,0},{2,3},{3,2},{4,5},{5,4},{6,7},{7,6},{8,9},{9,8},{10,11... | collective-permute-start | bytes 442376 | tf_op jit(solution)/shard_map/other_3/ppermute | solution.py:50

commit v5 on v4

--- a/solution.py
+++ b/solution.py
@@ -11,10 +11,10 @@
 AXES = ("rep", "fsdp")
 NT = (((1,), (1,)), ((), ()))
 NN = (((1,), (0,)), ((), ()))
-VMEM_LIMIT = 16 * 1024 * 1024
+VMEM_LIMIT = 8 * 1024 * 1024
 EARLY = 6
 U_FLOPS = 4e9
-L_FLOPS = 1e6
+L_FLOPS = 1e9
 W_FLOPS = 4
 M_FLOPS = 1
 
@@ -127,7 +127,7 @@
     return t
 
 
-def middle_kernel(at, early, h_ref, w_ref, own_ref, received_ref, *refs):
+def middle_kernel(at, others, early, h_ref, w_ref, own_ref, received_ref, *refs):
     *ab_refs, t_ref, high_ref, merged_ref, b_all = refs
     x, place_at, core = position()
     kind = core ^ x
@@ -140,10 +140,7 @@
     b_own = ab_refs[0][rows_a : rows_a + rows_b]
     n = len(at)
     blocks = [(ref, 0, at[i], 0) for i, ref in enumerate(ab_refs[:n])]
-    rest = ab_refs[n:]
-    separate = len(rest) if len(rest) == n else len(rest) - 1
-    blocks += [(rest[i], 1, at[i], 0) for i in range(separate)]
-    blocks += [(rest[-1], 1, at[i], 2 * (i - separate)) for i in range(separate, n)]
+    blocks += [(ref, 1, k, 0) for ref, k in zip(ab_refs[n:], others)]
     t_ref[...] = add_blocks(h_ref, w_ref, b_own, merged_ref, b_all, blocks, jnp.zeros(t_ref.shape, jnp.float32))
 
 
@@ -163,7 +160,8 @@
     b_own = first_ref[rows_a : rows_a + rows_b]
     merged_ref[...] = m_ref[...]
     b_all[...] = b_ref[...]
-    blocks = [(ref, i // len(at), at[i % len(at)], 0) for i, ref in enumerate(ab_refs)]
+    own, joined = ab_refs
+    blocks = [(own, 0, at[-1], 0)] + [(joined, 1, k, 2 * i) for i, k in enumerate(at)]
     t = add_blocks(h_ref, w_ref, b_own, merged_ref, b_all, blocks, t_ref[...])
     out = high_ref[...]
     for part in split_bf16(t):
@@ -220,15 +218,15 @@
     w6 = send(w4, group, X, name="w6")
     w7 = send(w5, group, Y, name="w7")
     held = [w0, w1, w2, w3, w4, w5, w6, w7]
-    other_1 = send(ab_1, group, CORE, name="other_1")
     other_2 = send(ab_2, group, CORE, name="other_2")
-    other_3 = send(ab_3, group, CORE, name="other_3")
-    ab_early = [ab_0, ab_1, ab_2, other_0, other_1, other_2]
+    joined = jnp.concatenate([ab_1, ab_3])
+    other_3 = send(joined, group, CORE, name="other_3")
+    ab_early = [ab_0, ab_1, ab_2, other_0, other_2]
 
     early = [w_here] + held[1:EARLY]
     late = held[EARLY:]
     early, other_0 = lax.optimization_barrier((early, other_0))
-    ab_early = [ab_0, ab_1, ab_2, other_0, other_1, other_2]
+    ab_early = [ab_0, ab_1, ab_2, other_0, other_2]
     columns = rows_b * EARLY
     own, other = pl.pallas_call(
         weight_kernel,
@@ -243,7 +241,7 @@
     received = send(other, group, CORE, name="received")
     middle = (0, 1, 2)
     t, high, merged, b_all = pl.pallas_call(
-        functools.partial(middle_kernel, middle, EARLY),
+        functools.partial(middle_kernel, middle, (0, 2), EARLY),
         out_shape=[
             jax.ShapeDtypeStruct((tokens, rank), f32),
             jax.ShapeDtypeStruct((tokens, outputs), f32),
@@ -268,7 +266,7 @@
         name="late_product",
     )(h_here, high, *late, *other_late)
     return tuple(pl.pallas_call(
-        functools.partial(last_kernel, (3,)),
+        functools.partial(last_kernel, (1, 3)),
         out_shape=[
             jax.ShapeDtypeStruct((tokens, outputs), bf16),
             jax.ShapeDtypeStruct(weight.shape, bf16),

time: 38.1 us -> 37.9 us (level)
    ppermute x21 -> x20, starting transfers between devices: 15.9 us -> 15.7 us  [send(): return lax.ppermute(rows, AXES, pairs)]
    ppermute x21 -> x20, waiting for transfers between devices: 14.5 us -> 14.5 us  [send(): return lax.ppermute(rows, AXES, pairs)]
  transfers between devices with their start and end apart: 21 -> 20, of which waited for: 13 -> 12; matrix products, arithmetic and copies ran while one was open for 5% -> 5% of each run, Pallas kernels for 9% -> 9%
where the time goes in v5:
time: 37.9 us; the launch traced here: 37.6 us
  starting transfers between devices  15.7 us (41%)
  waiting for transfers between devices  14.5 us (38%)
  Pallas kernels  4.75 us (13%)
  other arithmetic  1.9 us (5%)
  between operations  0.73 us (2%)
    ppermute x20, starting transfers between devices, send(): return lax.ppermute(rows, AXES, pairs)  15.7 us
    ppermute x20, waiting for transfers between devices, send(): return lax.ppermute(rows, AXES, pairs)  14.5 us
    pallas_call x1, Pallas kernels, paired(): pl.pallas_call(functools.partial(last_kernel, (1, 3)), out_shape=[jax.Sha...  1.36 us
    pallas_call x1, Pallas kernels, paired(): pl.pallas_call(weight_kernel, out_shape=[jax.ShapeDtypeStruct((tokens, co...  1.27 us
    pallas_call x1, Pallas kernels, paired(): pl.pallas_call(functools.partial(late_kernel, tuple(range(EARLY, len(HELD...  1.17 us
    concatenate x1, other arithmetic, paired(): mine = jnp.concatenate([grad_a[0], grad_b[0]])  0.93 us
    concatenate x1, other arithmetic, paired(): old = jnp.concatenate([adapter_a, adapter_b])  0.93 us
    pallas_call x1, Pallas kernels, paired(): pl.pallas_call(functools.partial(middle_kernel, middle, (0, 2), EARLY), o...  0.93 us
  transfers between devices with their start and end apart: 20, of which 12 were waited for; matrix products, arithmetic and copies ran while one was open for 5% of the time, Pallas kernels for 9%

profile of v5, /device:TPU:0, one launch (start us, length us, event | category | flops | bytes accessed | tf_op | source)
XLA Modules:
  0.0 37.6 jit_solution(5303034951969828515)
XLA Ops:
  1.1 3.7 %collective-permute-start = (bf16[32,4096]{1,0:T(8,128)(2,1)}, bf16[32,4096]{1,0:T(8,128)(2,1)S(1)}, u32[]{:S(2)}, u32[]{:S(2)}) collective-permute-start(bf16[32,4096]{1,0:T(8,128)(2,1)} %w_ref.3), channel_id=1, source_target_pairs={{0,8},{1,5},{2,10},{3,7},{4,12},{5,1},{6,14},{7,3},{8,0},{9,13},{1... | collective-permute-start | bytes 786440 | tf_op jit(solution)/shard_map/w1/ppermute | solution.py:50
  4.8 1.5 %collective-permute-start.1 = (bf16[32,4096]{1,0:T(8,128)(2,1)}, bf16[32,4096]{1,0:T(8,128)(2,1)S(1)}, u32[]{:S(2)}, u32[]{:S(2)}) collective-permute-start(bf16[32,4096]{1,0:T(8,128)(2,1)} %w_ref.3), channel_id=1, source_target_pairs={{0,2},{1,3},{2,0},{3,1},{4,6},{5,7},{6,4},{7,5},{8,10},{9,11},{10,... | collective-permute-start | bytes 786440 | tf_op jit(solution)/shard_map/w2/ppermute | solution.py:50
  6.8 1.5 %collective-permute-start.9 = (f32[1,32,128]{2,1,0:T(8,128)}, f32[1,32,128]{2,1,0:T(8,128)S(1)}, u32[]{:S(2)}, u32[]{:S(2)}) collective-permute-start(f32[1,32,128]{2,1,0:T(8,128)} %param.11), channel_id=1, source_target_pairs={{0,16},{1,17},{2,18},{3,19},{4,20},{5,21},{6,22},{7,23},{8,24},{9,... | collective-permute-start | bytes 49160 | tf_op jit(solution)/shard_map/other_b/ppermute | solution.py:50
  8.4 0.9 %pad_maximum_fusion.1.old_ref = f32[288,128]{1,0:T(8,128)S(1)} fusion(f32[32,128]{1,0:T(8,128)} %param.9, f32[256,128]{1,0:T(8,128)} %param.8), kind=kLoop, calls=%fused_computation.1 | loop fusion | flops 36864 | bytes 294912 | tf_op jit(solution)/shard_map/concatenate | solution.py:189
  9.3 0.9 %pad_maximum_fusion.2.own_ref = f32[288,128]{1,0:T(8,128)S(1)} fusion(f32[32,128]{1,0:T(8,128)} %bitcast.3, f32[256,128]{1,0:T(8,128)} %bitcast.2), kind=kLoop, calls=%fused_computation.2 | loop fusion | flops 36864 | bytes 294912 | tf_op jit(solution)/shard_map/concatenate | solution.py:190
  10.3 1.7 %collective-permute-done.9.ob_ref = f32[1,32,128]{2,1,0:T(8,128)S(1)} collective-permute-done((f32[1,32,128]{2,1,0:T(8,128)}, f32[1,32,128]{2,1,0:T(8,128)S(1)}, u32[]{:S(2)}, u32[]{:S(2)}) %collective-permute-start.9) | collective-permute-done | bytes 16416 | tf_op jit(solution)/shard_map/other_b/ppermute | solution.py:50
  12.0 1.9 %collective-permute-start.10 = (bf16[288,128]{1,0:T(8,128)(2,1)S(1)}, bf16[288,128]{1,0:T(8,128)(2,1)S(1)}, u32[]{:S(2)}, u32[]{:S(2)}) collective-permute-start(bf16[288,128]{1,0:T(8,128)(2,1)S(1)} %update.1), channel_id=1, source_target_pairs={{0,8},{1,9},{2,10},{3,11},{4,12},{5,13},{6,14},{7,15},{8,0},{9,1},... | collective-permute-start | bytes 221192 | tf_op jit(solution)/shard_map/ab_far/ppermute | solution.py:50
  14.2 1.5 %collective-permute-start.3 = (bf16[32,4096]{1,0:T(8,128)(2,1)S(1)}, bf16[32,4096]{1,0:T(8,128)(2,1)S(1)}, u32[]{:S(2)}, u32[]{:S(2)}) collective-permute-start(bf16[32,4096]{1,0:T(8,128)(2,1)S(1)} %collective-permute-done.refs_1_), channel_id=1, source_target_pairs={{0,2},{1,3},{2,0},{3,1},{4,6},{5,7},{6,4},{7,5},{8,10},{9,11},{10,... | collective-permute-start | bytes 786440 | tf_op jit(solution)/shard_map/w4/ppermute | solution.py:50
  16.1 1.2 %collective-permute-done.10 = bf16[288,128]{1,0:T(8,128)(2,1)S(1)} collective-permute-done((bf16[288,128]{1,0:T(8,128)(2,1)S(1)}, bf16[288,128]{1,0:T(8,128)(2,1)S(1)}, u32[]{:S(2)}, u32[]{:S(2)}) %collective-permute-start.10) | collective-permute-done | bytes 73760 | tf_op jit(solution)/shard_map/ab_far/ppermute | solution.py:50
  17.4 4.7 %collective-permute-done.2.refs_3_ = bf16[32,4096]{1,0:T(8,128)(2,1)S(1)} collective-permute-done((bf16[32,4096]{1,0:T(8,128)(2,1)S(1)}, bf16[32,4096]{1,0:T(8,128)(2,1)S(1)}, u32[]{:S(2)}, u32[]{:S(2)}) %collective-permute-start.2) | collective-permute-done | bytes 262176 | tf_op jit(solution)/shard_map/w3/ppermute | solution.py:50
  22.0 0.7 %collective-permute-start.14 = (bf16[576,128]{1,0:T(8,128)(2,1)S(1)}, bf16[576,128]{1,0:T(8,128)(2,1)S(1)}, u32[]{:S(2)}, u32[]{:S(2)}) collective-permute-start(bf16[576,128]{1,0:T(8,128)(2,1)S(1)} %pad_maximum_fusion.3.refs_0_.first_ref), channel_id=1, source_target_pairs={{0,2},{1,3},{2,0},{3,1},{4,6},{5,7},{6,4},{7,5},{8,10},{9,11},{10,... | collective-permute-start | bytes 442376 | tf_op jit(solution)/shard_map/ab_2/ppermute | solution.py:50
  23.5 0.7 %collective-permute-start.4 = (bf16[32,4096]{1,0:T(8,128)(2,1)S(1)}, bf16[32,4096]{1,0:T(8,128)(2,1)S(1)}, u32[]{:S(2)}, u32[]{:S(2)}) collective-permute-start(bf16[32,4096]{1,0:T(8,128)(2,1)S(1)} %collective-permute-done.3.refs_4_), channel_id=1, source_target_pairs={{0,17},{1,16},{2,19},{3,18},{4,21},{5,20},{6,23},{7,22},{8,25},{9,... | collective-permute-start | bytes 786440 | tf_op jit(solution)/shard_map/w6/ppermute | solution.py:50
  24.1 0.8 %collective-permute-done.5.refs_5_ = bf16[32,4096]{1,0:T(8,128)(2,1)S(1)} collective-permute-done((bf16[32,4096]{1,0:T(8,128)(2,1)S(1)}, bf16[32,4096]{1,0:T(8,128)(2,1)S(1)}, u32[]{:S(2)}, u32[]{:S(2)}) %collective-permute-start.5) | collective-permute-done | bytes 262176 | tf_op jit(solution)/shard_map/w5/ppermute | solution.py:50
  25.0 1.3 %weight_product.1 = (f32[256,192]{1,0:T(8,128)S(1)}, f32[256,192]{1,0:T(8,128)S(1)}) custom-call(bf16[256,4096]{1,0:T(8,128)(2,1)S(1)} %copy-done, bf16[256,4096]{1,0:T(8,128)(2,1)S(1)} %collective-permute-done.7.hs_ref, bf16[32,4096]{1,0:T(8,128)(2,1)S(1)} %copy-done.1, bf16[32,4096]{1,0:T(8,128)(2,1)S(1)} %collective-permute-done.refs_1_, ...), custom_call_target="tpu_custom_call" | custom-call | flops 3221225472 | bytes 5767168 | tf_op jit(solution)/shard_map/weight_product/pallas_call | solution.py:231
  26.2 0.7 %collective-permute-start.12 = (f32[256,192]{1,0:T(8,128)S(1)}, f32[256,192]{1,0:T(8,128)S(1)}, u32[]{:S(2)}, u32[]{:S(2)}) collective-permute-start(f32[256,192]{1,0:T(8,128)S(1)} %get-tuple-element.37), channel_id=1, source_target_pairs={{0,1},{1,0},{2,3},{3,2},{4,5},{5,4},{6,7},{7,6},{8,9},{9,8},{10,11... | collective-permute-start | bytes 589832 | tf_op jit(solution)/shard_map/received/ppermute | solution.py:50
  27.0 0.7 %collective-permute-done.14.refs_2_ = bf16[576,128]{1,0:T(8,128)(2,1)S(1)} collective-permute-done((bf16[576,128]{1,0:T(8,128)(2,1)S(1)}, bf16[576,128]{1,0:T(8,128)(2,1)S(1)}, u32[]{:S(2)}, u32[]{:S(2)}) %collective-permute-start.14) | collective-permute-done | bytes 147488 | tf_op jit(solution)/shard_map/ab_2/ppermute | solution.py:50
  27.6 1.2 %collective-permute-done.13.refs_1_ = bf16[576,128]{1,0:T(8,128)(2,1)S(1)} collective-permute-done((bf16[576,128]{1,0:T(8,128)(2,1)S(1)}, bf16[576,128]{1,0:T(8,128)(2,1)S(1)}, u32[]{:S(2)}, u32[]{:S(2)}) %collective-permute-start.13) | collective-permute-done | bytes 147488 | tf_op jit(solution)/shard_map/ab_1/ppermute | solution.py:50
  28.9 0.7 %collective-permute-start.18 = (bf16[576,128]{1,0:T(8,128)(2,1)S(1)}, bf16[576,128]{1,0:T(8,128)(2,1)S(1)}, u32[]{:S(2)}, u32[]{:S(2)}) collective-permute-start(bf16[576,128]{1,0:T(8,128)(2,1)S(1)} %collective-permute-done.14.refs_2_), channel_id=1, source_target_pairs={{0,4},{1,5},{2,6},{3,7},{4,0},{5,1},{6,2},{7,3},{8,12},{9,13},{10,... | collective-permute-start | bytes 442376 | tf_op jit(solution)/shard_map/ab_3/ppermute | solution.py:50
  29.6 0.9 %middle.1 = (f32[256,128]{1,0:T(8,128)S(1)}, f32[256,512]{1,0:T(8,128)S(1)}, bf16[32,4096]{1,0:T(8,128)(2,1)S(1)}, bf16[512,128]{1,0:T(8,128)(2,1)S(1)}) custom-call(bf16[256,4096]{1,0:T(8,128)(2,1)S(1)} %copy-done, bf16[32,4096]{1,0:T(8,128)(2,1)S(1)} %copy-done.1, f32[256,192]{1,0:T(8,128)S(1)} %get-tuple-element.36.own_ref, ...), custom_call_target="tpu_custom_call" | custom-call | flops 268435456 | bytes 3145728 | tf_op jit(solution)/shard_map/middle/pallas_call | solution.py:243
  30.6 1.3 %collective-permute-done.4.refs_0_ = bf16[32,4096]{1,0:T(8,128)(2,1)S(1)} collective-permute-done((bf16[32,4096]{1,0:T(8,128)(2,1)S(1)}, bf16[32,4096]{1,0:T(8,128)(2,1)S(1)}, u32[]{:S(2)}, u32[]{:S(2)}) %collective-permute-start.4) | collective-permute-done | bytes 262176 | tf_op jit(solution)/shard_map/w6/ppermute | solution.py:50
  31.8 1.3 %collective-permute-done.6.refs_1_ = bf16[32,4096]{1,0:T(8,128)(2,1)S(1)} collective-permute-done((bf16[32,4096]{1,0:T(8,128)(2,1)S(1)}, bf16[32,4096]{1,0:T(8,128)(2,1)S(1)}, u32[]{:S(2)}, u32[]{:S(2)}) %collective-permute-start.6) | collective-permute-done | bytes 262176 | tf_op jit(solution)/shard_map/w7/ppermute | solution.py:50
  34.1 0.6 %collective-permute-done.16.refs_2_ = bf16[32,4096]{1,0:T(8,128)(2,1)S(1)} collective-permute-done((bf16[32,4096]{1,0:T(8,128)(2,1)S(1)}, bf16[32,4096]{1,0:T(8,128)(2,1)S(1)}, u32[]{:S(2)}, u32[]{:S(2)}) %collective-permute-start.16) | collective-permute-done | bytes 262176 | tf_op jit(solution)/shard_map/other_late/ppermute | solution.py:50
  35.1 1.2 %late_product.1.high_ref = f32[256,512]{1,0:T(8,128)S(1)} custom-call(bf16[256,4096]{1,0:T(8,128)(2,1)S(1)} %copy-done, f32[256,512]{1,0:T(8,128)S(1)} %get-tuple-element.41.high_ref, bf16[32,4096]{1,0:T(8,128)(2,1)S(1)} %collective-permute-done.4.refs_0_, bf16[32,4096]{1,0:T(8,128)(2,1)S(1)} %collective-permute-done.6.refs_1_, ...), custom_call_target="tpu_custom_call" | custom-call | flops 1000000000 | bytes 262144 | tf_op jit(solution)/shard_map/late_product/pallas_call | solution.py:259
  36.3 1.4 %last.1 = (bf16[256,512]{1,0:T(8,128)(2,1)}, bf16[32,4096]{1,0:T(8,128)(2,1)}) custom-call(bf16[256,4096]{1,0:T(8,128)(2,1)S(1)} %copy-done, bf16[32,4096]{1,0:T(8,128)(2,1)S(1)} %copy-done.1, f32[256,128]{1,0:T(8,128)S(1)} %get-tuple-element.40.t_ref, f32[256,512]{1,0:T(8,128)S(1)} %late_product.1.high_ref, bf16[32,4096]{1,0:T(8,128)(2,1)S(1)} %get-tuple-element.44.m_ref, ...), custom_call_target="tpu_custom_call" | custom-call | flops 33554432 | bytes 262144 | tf_op jit(solution)/shard_map/last/pallas_call | solution.py:268
  (29 shorter events, 3.9 us)
Async XLA Ops:
  0.6 24.3 %collective-permute-start.7 = (bf16[256,4096]{1,0:T(8,128)(2,1)}, bf16[256,4096]{1,0:T(8,128)(2,1)S(1)}, u32[]{:S(2)}, u32[]{:S(2)}) collective-permute-start(bf16[256,4096]{1,0:T(8,128)(2,1)} %h_ref.7), channel_id=1, source_target_pairs={{0,1},{1,0},{2,3},{3,2},{4,5},{5,4},{6,7},{7,6},{8,9},{9,8},{10,11... | collective-permute-start | bytes 6291464 | tf_op jit(solution)/shard_map/other_hidden/ppermute | solution.py:50
  1.1 12.7 %collective-permute-start = (bf16[32,4096]{1,0:T(8,128)(2,1)}, bf16[32,4096]{1,0:T(8,128)(2,1)S(1)}, u32[]{:S(2)}, u32[]{:S(2)}) collective-permute-start(bf16[32,4096]{1,0:T(8,128)(2,1)} %w_ref.3), channel_id=1, source_target_pairs={{0,8},{1,5},{2,10},{3,7},{4,12},{5,1},{6,14},{7,3},{8,0},{9,13},{1... | collective-permute-start | bytes 786440 | tf_op jit(solution)/shard_map/w1/ppermute | solution.py:50
  4.8 9.0 %collective-permute-start.1 = (bf16[32,4096]{1,0:T(8,128)(2,1)}, bf16[32,4096]{1,0:T(8,128)(2,1)S(1)}, u32[]{:S(2)}, u32[]{:S(2)}) collective-permute-start(bf16[32,4096]{1,0:T(8,128)(2,1)} %w_ref.3), channel_id=1, source_target_pairs={{0,2},{1,3},{2,0},{3,1},{4,6},{5,7},{6,4},{7,5},{8,10},{9,11},{10,... | collective-permute-start | bytes 786440 | tf_op jit(solution)/shard_map/w2/ppermute | solution.py:50
  6.3 5.6 %collective-permute-start.8 = (f32[1,256,128]{2,1,0:T(8,128)}, f32[1,256,128]{2,1,0:T(8,128)S(1)}, u32[]{:S(2)}, u32[]{:S(2)}) collective-permute-start(f32[1,256,128]{2,1,0:T(8,128)} %param.10), channel_id=1, source_target_pairs={{0,16},{1,17},{2,18},{3,19},{4,20},{5,21},{6,22},{7,23},{8,24},{9,... | collective-permute-start | bytes 393224 | tf_op jit(solution)/shard_map/other_a/ppermute | solution.py:50
  6.8 5.1 %collective-permute-start.9 = (f32[1,32,128]{2,1,0:T(8,128)}, f32[1,32,128]{2,1,0:T(8,128)S(1)}, u32[]{:S(2)}, u32[]{:S(2)}) collective-permute-start(f32[1,32,128]{2,1,0:T(8,128)} %param.11), channel_id=1, source_target_pairs={{0,16},{1,17},{2,18},{3,19},{4,20},{5,21},{6,22},{7,23},{8,24},{9,... | collective-permute-start | bytes 49160 | tf_op jit(solution)/shard_map/other_b/ppermute | solution.py:50
  10.2 14.7 %copy-start = (bf16[256,4096]{1,0:T(8,128)(2,1)S(1)}, bf16[256,4096]{1,0:T(8,128)(2,1)}, u32[]{:S(2)}) copy-start(bf16[256,4096]{1,0:T(8,128)(2,1)} %h_ref.7) | copy-start | bytes 6291460
  10.2 14.7 %copy-start.1 = (bf16[32,4096]{1,0:T(8,128)(2,1)S(1)}, bf16[32,4096]{1,0:T(8,128)(2,1)}, u32[]{:S(2)}) copy-start(bf16[32,4096]{1,0:T(8,128)(2,1)} %w_ref.3) | copy-start | bytes 786436
  12.0 5.3 %collective-permute-start.10 = (bf16[288,128]{1,0:T(8,128)(2,1)S(1)}, bf16[288,128]{1,0:T(8,128)(2,1)S(1)}, u32[]{:S(2)}, u32[]{:S(2)}) collective-permute-start(bf16[288,128]{1,0:T(8,128)(2,1)S(1)} %update.1), channel_id=1, source_target_pairs={{0,8},{1,9},{2,10},{3,11},{4,12},{5,13},{6,14},{7,15},{8,0},{9,1},... | collective-permute-start | bytes 221192 | tf_op jit(solution)/shard_map/ab_far/ppermute | solution.py:50
  13.9 8.2 %collective-permute-start.2 = (bf16[32,4096]{1,0:T(8,128)(2,1)S(1)}, bf16[32,4096]{1,0:T(8,128)(2,1)S(1)}, u32[]{:S(2)}, u32[]{:S(2)}) collective-permute-start(bf16[32,4096]{1,0:T(8,128)(2,1)S(1)} %collective-permute-done.refs_1_), channel_id=1, source_target_pairs={{0,17},{1,16},{2,19},{3,18},{4,21},{5,20},{6,23},{7,22},{8,25},{9,... | collective-permute-start | bytes 786440 | tf_op jit(solution)/shard_map/w3/ppermute | solution.py:50
  14.2 9.0 %collective-permute-start.3 = (bf16[32,4096]{1,0:T(8,128)(2,1)S(1)}, bf16[32,4096]{1,0:T(8,128)(2,1)S(1)}, u32[]{:S(2)}, u32[]{:S(2)}) collective-permute-start(bf16[32,4096]{1,0:T(8,128)(2,1)S(1)} %collective-permute-done.refs_1_), channel_id=1, source_target_pairs={{0,2},{1,3},{2,0},{3,1},{4,6},{5,7},{6,4},{7,5},{8,10},{9,11},{10,... | collective-permute-start | bytes 786440 | tf_op jit(solution)/shard_map/w4/ppermute | solution.py:50
  15.7 9.2 %collective-permute-start.5 = (bf16[32,4096]{1,0:T(8,128)(2,1)S(1)}, bf16[32,4096]{1,0:T(8,128)(2,1)S(1)}, u32[]{:S(2)}, u32[]{:S(2)}) collective-permute-start(bf16[32,4096]{1,0:T(8,128)(2,1)S(1)} %collective-permute-done.refs_1_), channel_id=1, source_target_pairs={{0,4},{1,9},{2,6},{3,11},{4,0},{5,13},{6,2},{7,15},{8,12},{9,1},{1... | collective-permute-start | bytes 786440 | tf_op jit(solution)/shard_map/w5/ppermute | solution.py:50
  17.3 6.2 %collective-permute-start.11 = (bf16[576,128]{1,0:T(8,128)(2,1)S(1)}, bf16[576,128]{1,0:T(8,128)(2,1)S(1)}, u32[]{:S(2)}, u32[]{:S(2)}) collective-permute-start(bf16[576,128]{1,0:T(8,128)(2,1)S(1)} %pad_maximum_fusion.3.refs_0_.first_ref), channel_id=1, source_target_pairs={{0,1},{1,0},{2,3},{3,2},{4,5},{5,4},{6,7},{7,6},{8,9},{9,8},{10,11... | collective-permute-start | bytes 442376 | tf_op jit(solution)/shard_map/other_0/ppermute | solution.py:50
  22.0 5.6 %collective-permute-start.14 = (bf16[576,128]{1,0:T(8,128)(2,1)S(1)}, bf16[576,128]{1,0:T(8,128)(2,1)S(1)}, u32[]{:S(2)}, u32[]{:S(2)}) collective-permute-start(bf16[576,128]{1,0:T(8,128)(2,1)S(1)} %pad_maximum_fusion.3.refs_0_.first_ref), channel_id=1, source_target_pairs={{0,2},{1,3},{2,0},{3,1},{4,6},{5,7},{6,4},{7,5},{8,10},{9,11},{10,... | collective-permute-start | bytes 442376 | tf_op jit(solution)/shard_map/ab_2/ppermute | solution.py:50
  23.2 5.7 %collective-permute-start.13 = (bf16[576,128]{1,0:T(8,128)(2,1)S(1)}, bf16[576,128]{1,0:T(8,128)(2,1)S(1)}, u32[]{:S(2)}, u32[]{:S(2)}) collective-permute-start(bf16[576,128]{1,0:T(8,128)(2,1)S(1)} %pad_maximum_fusion.3.refs_0_.first_ref), channel_id=1, source_target_pairs={{0,4},{1,5},{2,6},{3,7},{4,0},{5,1},{6,2},{7,3},{8,12},{9,13},{10,... | collective-permute-start | bytes 442376 | tf_op jit(solution)/shard_map/ab_1/ppermute | solution.py:50
  23.5 8.3 %collective-permute-start.4 = (bf16[32,4096]{1,0:T(8,128)(2,1)S(1)}, bf16[32,4096]{1,0:T(8,128)(2,1)S(1)}, u32[]{:S(2)}, u32[]{:S(2)}) collective-permute-start(bf16[32,4096]{1,0:T(8,128)(2,1)S(1)} %collective-permute-done.3.refs_4_), channel_id=1, source_target_pairs={{0,17},{1,16},{2,19},{3,18},{4,21},{5,20},{6,23},{7,22},{8,25},{9,... | collective-permute-start | bytes 786440 | tf_op jit(solution)/shard_map/w6/ppermute | solution.py:50
  24.9 8.2 %collective-permute-start.6 = (bf16[32,4096]{1,0:T(8,128)(2,1)S(1)}, bf16[32,4096]{1,0:T(8,128)(2,1)S(1)}, u32[]{:S(2)}, u32[]{:S(2)}) collective-permute-start(bf16[32,4096]{1,0:T(8,128)(2,1)S(1)} %collective-permute-done.5.refs_5_), channel_id=1, source_target_pairs={{0,2},{1,3},{2,0},{3,1},{4,6},{5,7},{6,4},{7,5},{8,10},{9,11},{10,... | collective-permute-start | bytes 786440 | tf_op jit(solution)/shard_map/w7/ppermute | solution.py:50
  26.2 3.4 %collective-permute-start.12 = (f32[256,192]{1,0:T(8,128)S(1)}, f32[256,192]{1,0:T(8,128)S(1)}, u32[]{:S(2)}, u32[]{:S(2)}) collective-permute-start(f32[256,192]{1,0:T(8,128)S(1)} %get-tuple-element.37), channel_id=1, source_target_pairs={{0,1},{1,0},{2,3},{3,2},{4,5},{5,4},{6,7},{7,6},{8,9},{9,8},{10,11... | collective-permute-start | bytes 589832 | tf_op jit(solution)/shard_map/received/ppermute | solution.py:50
  27.6 2.0 %collective-permute-start.15 = (bf16[576,128]{1,0:T(8,128)(2,1)S(1)}, bf16[576,128]{1,0:T(8,128)(2,1)S(1)}, u32[]{:S(2)}, u32[]{:S(2)}) collective-permute-start(bf16[576,128]{1,0:T(8,128)(2,1)S(1)} %collective-permute-done.14.refs_2_), channel_id=1, source_target_pairs={{0,1},{1,0},{2,3},{3,2},{4,5},{5,4},{6,7},{7,6},{8,9},{9,8},{10,11... | collective-permute-start | bytes 442376 | tf_op jit(solution)/shard_map/other_2/ppermute | solution.py:50
  28.9 5.1 %collective-permute-start.18 = (bf16[576,128]{1,0:T(8,128)(2,1)S(1)}, bf16[576,128]{1,0:T(8,128)(2,1)S(1)}, u32[]{:S(2)}, u32[]{:S(2)}) collective-permute-start(bf16[576,128]{1,0:T(8,128)(2,1)S(1)} %collective-permute-done.14.refs_2_), channel_id=1, source_target_pairs={{0,4},{1,5},{2,6},{3,7},{4,0},{5,1},{6,2},{7,3},{8,12},{9,13},{10,... | collective-permute-start | bytes 442376 | tf_op jit(solution)/shard_map/ab_3/ppermute | solution.py:50
  33.2 1.5 %collective-permute-start.16 = (bf16[32,4096]{1,0:T(8,128)(2,1)S(1)}, bf16[32,4096]{1,0:T(8,128)(2,1)S(1)}, u32[]{:S(2)}, u32[]{:S(2)}) collective-permute-start(bf16[32,4096]{1,0:T(8,128)(2,1)S(1)} %collective-permute-done.4.refs_0_), channel_id=1, source_target_pairs={{0,1},{1,0},{2,3},{3,2},{4,5},{5,4},{6,7},{7,6},{8,9},{9,8},{10,11... | collective-permute-start | bytes 786440 | tf_op jit(solution)/shard_map/other_late/ppermute | solution.py:50
  33.2 1.9 %collective-permute-start.17 = (bf16[32,4096]{1,0:T(8,128)(2,1)S(1)}, bf16[32,4096]{1,0:T(8,128)(2,1)S(1)}, u32[]{:S(2)}, u32[]{:S(2)}) collective-permute-start(bf16[32,4096]{1,0:T(8,128)(2,1)S(1)} %collective-permute-done.6.refs_1_), channel_id=1, source_target_pairs={{0,1},{1,0},{2,3},{3,2},{4,5},{5,4},{6,7},{7,6},{8,9},{9,8},{10,11... | collective-permute-start | bytes 786440 | tf_op jit(solution)/shard_map/other_late/ppermute | solution.py:50
  34.0 2.2 %collective-permute-start.19 = (bf16[1152,128]{1,0:T(8,128)(2,1)S(1)}, bf16[1152,128]{1,0:T(8,128)(2,1)S(1)}, u32[]{:S(2)}, u32[]{:S(2)}) collective-permute-start(bf16[1152,128]{1,0:T(8,128)(2,1)S(1)} %pad_maximum_fusion), channel_id=1, source_target_pairs={{0,1},{1,0},{2,3},{3,2},{4,5},{5,4},{6,7},{7,6},{8,9},{9,8},{10,11... | collective-permute-start | bytes 884744 | tf_op jit(solution)/shard_map/other_3/ppermute | solution.py:50

commit v6 on v5

--- a/solution.py
+++ b/solution.py
@@ -206,6 +206,7 @@
         name="update",
     )(old, mine, other_a, other_b)
     ab_far = send(ab, group, Z2, name="ab_far")
+    w1, ab = hold((w1, ab))
     w3 = send(w1, group, X, name="w3")
     w4 = send(w1, group, Y, name="w4")
     w5 = send(w1, group, Z1, Z2, name="w5")

time: 37.9 us -> 37.9 us (level)
  no operation moved by 1% of the time
where the time goes in v6:
time: 37.9 us; the launch traced here: 37.6 us
  starting transfers between devices  15.7 us (41%)
  waiting for transfers between devices  14.5 us (38%)
  Pallas kernels  4.75 us (13%)
  other arithmetic  1.89 us (5%)
  between operations  0.73 us (2%)
    ppermute x20, starting transfers between devices, send(): return lax.ppermute(rows, AXES, pairs)  15.7 us
    ppermute x20, waiting for transfers between devices, send(): return lax.ppermute(rows, AXES, pairs)  14.5 us
    pallas_call x1, Pallas kernels, paired(): pl.pallas_call(functools.partial(last_kernel, (1, 3)), out_shape=[jax.Sha...  1.36 us
    pallas_call x1, Pallas kernels, paired(): pl.pallas_call(weight_kernel, out_shape=[jax.ShapeDtypeStruct((tokens, co...  1.26 us
    pallas_call x1, Pallas kernels, paired(): pl.pallas_call(functools.partial(late_kernel, tuple(range(EARLY, len(HELD...  1.16 us
    concatenate x1, other arithmetic, paired(): mine = jnp.concatenate([grad_a[0], grad_b[0]])  0.93 us
    concatenate x1, other arithmetic, paired(): old = jnp.concatenate([adapter_a, adapter_b])  0.93 us
    pallas_call x1, Pallas kernels, paired(): pl.pallas_call(functools.partial(middle_kernel, middle, (0, 2), EARLY), o...  0.93 us
  transfers between devices with their start and end apart: 20, of which 12 were waited for; matrix products, arithmetic and copies ran while one was open for 5% of the time, Pallas kernels for 9%

profile of v6, /device:TPU:0, one launch (start us, length us, event | category | flops | bytes accessed | tf_op | source)
XLA Modules:
  0.0 37.6 jit_solution(18353044569467201733)
XLA Ops:
  1.1 3.7 %collective-permute-start = (bf16[32,4096]{1,0:T(8,128)(2,1)}, bf16[32,4096]{1,0:T(8,128)(2,1)S(1)}, u32[]{:S(2)}, u32[]{:S(2)}) collective-permute-start(bf16[32,4096]{1,0:T(8,128)(2,1)} %w_ref.3), channel_id=1, source_target_pairs={{0,8},{1,5},{2,10},{3,7},{4,12},{5,1},{6,14},{7,3},{8,0},{9,13},{1... | collective-permute-start | bytes 786440 | tf_op jit(solution)/shard_map/w1/ppermute | solution.py:50
  4.8 1.5 %collective-permute-start.1 = (bf16[32,4096]{1,0:T(8,128)(2,1)}, bf16[32,4096]{1,0:T(8,128)(2,1)S(1)}, u32[]{:S(2)}, u32[]{:S(2)}) collective-permute-start(bf16[32,4096]{1,0:T(8,128)(2,1)} %w_ref.3), channel_id=1, source_target_pairs={{0,2},{1,3},{2,0},{3,1},{4,6},{5,7},{6,4},{7,5},{8,10},{9,11},{10,... | collective-permute-start | bytes 786440 | tf_op jit(solution)/shard_map/w2/ppermute | solution.py:50
  6.8 1.5 %collective-permute-start.3 = (f32[1,32,128]{2,1,0:T(8,128)}, f32[1,32,128]{2,1,0:T(8,128)S(1)}, u32[]{:S(2)}, u32[]{:S(2)}) collective-permute-start(f32[1,32,128]{2,1,0:T(8,128)} %param.11), channel_id=1, source_target_pairs={{0,16},{1,17},{2,18},{3,19},{4,20},{5,21},{6,22},{7,23},{8,24},{9,... | collective-permute-start | bytes 49160 | tf_op jit(solution)/shard_map/other_b/ppermute | solution.py:50
  8.4 0.9 %pad_maximum_fusion.1.old_ref = f32[288,128]{1,0:T(8,128)S(1)} fusion(f32[32,128]{1,0:T(8,128)} %param.9, f32[256,128]{1,0:T(8,128)} %param.8), kind=kLoop, calls=%fused_computation.1 | loop fusion | flops 36864 | bytes 294912 | tf_op jit(solution)/shard_map/concatenate | solution.py:189
  9.3 0.9 %pad_maximum_fusion.2.own_ref = f32[288,128]{1,0:T(8,128)S(1)} fusion(f32[32,128]{1,0:T(8,128)} %bitcast.3, f32[256,128]{1,0:T(8,128)} %bitcast.2), kind=kLoop, calls=%fused_computation.2 | loop fusion | flops 36864 | bytes 294912 | tf_op jit(solution)/shard_map/concatenate | solution.py:190
  10.3 1.7 %collective-permute-done.3.ob_ref = f32[1,32,128]{2,1,0:T(8,128)S(1)} collective-permute-done((f32[1,32,128]{2,1,0:T(8,128)}, f32[1,32,128]{2,1,0:T(8,128)S(1)}, u32[]{:S(2)}, u32[]{:S(2)}) %collective-permute-start.3) | collective-permute-done | bytes 16416 | tf_op jit(solution)/shard_map/other_b/ppermute | solution.py:50
  12.0 1.9 %collective-permute-start.10 = (bf16[288,128]{1,0:T(8,128)(2,1)S(1)}, bf16[288,128]{1,0:T(8,128)(2,1)S(1)}, u32[]{:S(2)}, u32[]{:S(2)}) collective-permute-start(bf16[288,128]{1,0:T(8,128)(2,1)S(1)} %update.1), channel_id=1, source_target_pairs={{0,8},{1,9},{2,10},{3,11},{4,12},{5,13},{6,14},{7,15},{8,0},{9,1},... | collective-permute-start | bytes 221192 | tf_op jit(solution)/shard_map/ab_far/ppermute | solution.py:50
  14.2 1.5 %collective-permute-start.5 = (bf16[32,4096]{1,0:T(8,128)(2,1)S(1)}, bf16[32,4096]{1,0:T(8,128)(2,1)S(1)}, u32[]{:S(2)}, u32[]{:S(2)}) collective-permute-start(bf16[32,4096]{1,0:T(8,128)(2,1)S(1)} %collective-permute-done.refs_1_), channel_id=1, source_target_pairs={{0,2},{1,3},{2,0},{3,1},{4,6},{5,7},{6,4},{7,5},{8,10},{9,11},{10,... | collective-permute-start | bytes 786440 | tf_op jit(solution)/shard_map/w4/ppermute | solution.py:50
  16.1 1.2 %collective-permute-done.10 = bf16[288,128]{1,0:T(8,128)(2,1)S(1)} collective-permute-done((bf16[288,128]{1,0:T(8,128)(2,1)S(1)}, bf16[288,128]{1,0:T(8,128)(2,1)S(1)}, u32[]{:S(2)}, u32[]{:S(2)}) %collective-permute-start.10) | collective-permute-done | bytes 73760 | tf_op jit(solution)/shard_map/ab_far/ppermute | solution.py:50
  17.4 4.7 %collective-permute-done.4.refs_3_ = bf16[32,4096]{1,0:T(8,128)(2,1)S(1)} collective-permute-done((bf16[32,4096]{1,0:T(8,128)(2,1)S(1)}, bf16[32,4096]{1,0:T(8,128)(2,1)S(1)}, u32[]{:S(2)}, u32[]{:S(2)}) %collective-permute-start.4) | collective-permute-done | bytes 262176 | tf_op jit(solution)/shard_map/w3/ppermute | solution.py:50
  22.0 0.7 %collective-permute-start.14 = (bf16[576,128]{1,0:T(8,128)(2,1)S(1)}, bf16[576,128]{1,0:T(8,128)(2,1)S(1)}, u32[]{:S(2)}, u32[]{:S(2)}) collective-permute-start(bf16[576,128]{1,0:T(8,128)(2,1)S(1)} %constant_dynamic-update-slice_fusion.refs_0_.first_ref), channel_id=1, source_target_pairs={{0,2},{1,3},{2,0},{3,1},{4,6},{5,7},{6,4},{7,5},{8,10},{9,11},{10,... | collective-permute-start | bytes 442376 | tf_op jit(solution)/shard_map/ab_2/ppermute | solution.py:50
  23.5 0.7 %collective-permute-start.6 = (bf16[32,4096]{1,0:T(8,128)(2,1)S(1)}, bf16[32,4096]{1,0:T(8,128)(2,1)S(1)}, u32[]{:S(2)}, u32[]{:S(2)}) collective-permute-start(bf16[32,4096]{1,0:T(8,128)(2,1)S(1)} %collective-permute-done.5.refs_4_), channel_id=1, source_target_pairs={{0,17},{1,16},{2,19},{3,18},{4,21},{5,20},{6,23},{7,22},{8,25},{9,... | collective-permute-start | bytes 786440 | tf_op jit(solution)/shard_map/w6/ppermute | solution.py:50
  24.1 0.8 %collective-permute-done.7.refs_5_ = bf16[32,4096]{1,0:T(8,128)(2,1)S(1)} collective-permute-done((bf16[32,4096]{1,0:T(8,128)(2,1)S(1)}, bf16[32,4096]{1,0:T(8,128)(2,1)S(1)}, u32[]{:S(2)}, u32[]{:S(2)}) %collective-permute-start.7) | collective-permute-done | bytes 262176 | tf_op jit(solution)/shard_map/w5/ppermute | solution.py:50
  25.0 1.3 %weight_product.1 = (f32[256,192]{1,0:T(8,128)S(1)}, f32[256,192]{1,0:T(8,128)S(1)}) custom-call(bf16[256,4096]{1,0:T(8,128)(2,1)S(1)} %copy-done, bf16[256,4096]{1,0:T(8,128)(2,1)S(1)} %collective-permute-done.9.hs_ref, bf16[32,4096]{1,0:T(8,128)(2,1)S(1)} %copy-done.1, bf16[32,4096]{1,0:T(8,128)(2,1)S(1)} %collective-permute-done.refs_1_, ...), custom_call_target="tpu_custom_call" | custom-call | flops 3221225472 | bytes 5767168 | tf_op jit(solution)/shard_map/weight_product/pallas_call | solution.py:232
  26.2 0.7 %collective-permute-start.12 = (f32[256,192]{1,0:T(8,128)S(1)}, f32[256,192]{1,0:T(8,128)S(1)}, u32[]{:S(2)}, u32[]{:S(2)}) collective-permute-start(f32[256,192]{1,0:T(8,128)S(1)} %get-tuple-element.41), channel_id=1, source_target_pairs={{0,1},{1,0},{2,3},{3,2},{4,5},{5,4},{6,7},{7,6},{8,9},{9,8},{10,11... | collective-permute-start | bytes 589832 | tf_op jit(solution)/shard_map/received/ppermute | solution.py:50
  27.0 0.7 %collective-permute-done.14.refs_2_ = bf16[576,128]{1,0:T(8,128)(2,1)S(1)} collective-permute-done((bf16[576,128]{1,0:T(8,128)(2,1)S(1)}, bf16[576,128]{1,0:T(8,128)(2,1)S(1)}, u32[]{:S(2)}, u32[]{:S(2)}) %collective-permute-start.14) | collective-permute-done | bytes 147488 | tf_op jit(solution)/shard_map/ab_2/ppermute | solution.py:50
  27.6 1.2 %collective-permute-done.13.refs_1_ = bf16[576,128]{1,0:T(8,128)(2,1)S(1)} collective-permute-done((bf16[576,128]{1,0:T(8,128)(2,1)S(1)}, bf16[576,128]{1,0:T(8,128)(2,1)S(1)}, u32[]{:S(2)}, u32[]{:S(2)}) %collective-permute-start.13) | collective-permute-done | bytes 147488 | tf_op jit(solution)/shard_map/ab_1/ppermute | solution.py:50
  28.9 0.7 %collective-permute-start.18 = (bf16[576,128]{1,0:T(8,128)(2,1)S(1)}, bf16[576,128]{1,0:T(8,128)(2,1)S(1)}, u32[]{:S(2)}, u32[]{:S(2)}) collective-permute-start(bf16[576,128]{1,0:T(8,128)(2,1)S(1)} %collective-permute-done.14.refs_2_), channel_id=1, source_target_pairs={{0,4},{1,5},{2,6},{3,7},{4,0},{5,1},{6,2},{7,3},{8,12},{9,13},{10,... | collective-permute-start | bytes 442376 | tf_op jit(solution)/shard_map/ab_3/ppermute | solution.py:50
  29.6 0.9 %middle.1 = (f32[256,128]{1,0:T(8,128)S(1)}, f32[256,512]{1,0:T(8,128)S(1)}, bf16[32,4096]{1,0:T(8,128)(2,1)S(1)}, bf16[512,128]{1,0:T(8,128)(2,1)S(1)}) custom-call(bf16[256,4096]{1,0:T(8,128)(2,1)S(1)} %copy-done, bf16[32,4096]{1,0:T(8,128)(2,1)S(1)} %copy-done.1, f32[256,192]{1,0:T(8,128)S(1)} %get-tuple-element.40.own_ref, ...), custom_call_target="tpu_custom_call" | custom-call | flops 268435456 | bytes 3145728 | tf_op jit(solution)/shard_map/middle/pallas_call | solution.py:244
  30.6 1.3 %collective-permute-done.6.refs_0_ = bf16[32,4096]{1,0:T(8,128)(2,1)S(1)} collective-permute-done((bf16[32,4096]{1,0:T(8,128)(2,1)S(1)}, bf16[32,4096]{1,0:T(8,128)(2,1)S(1)}, u32[]{:S(2)}, u32[]{:S(2)}) %collective-permute-start.6) | collective-permute-done | bytes 262176 | tf_op jit(solution)/shard_map/w6/ppermute | solution.py:50
  31.8 1.3 %collective-permute-done.8.refs_1_ = bf16[32,4096]{1,0:T(8,128)(2,1)S(1)} collective-permute-done((bf16[32,4096]{1,0:T(8,128)(2,1)S(1)}, bf16[32,4096]{1,0:T(8,128)(2,1)S(1)}, u32[]{:S(2)}, u32[]{:S(2)}) %collective-permute-start.8) | collective-permute-done | bytes 262176 | tf_op jit(solution)/shard_map/w7/ppermute | solution.py:50
  34.1 0.6 %collective-permute-done.16.refs_2_ = bf16[32,4096]{1,0:T(8,128)(2,1)S(1)} collective-permute-done((bf16[32,4096]{1,0:T(8,128)(2,1)S(1)}, bf16[32,4096]{1,0:T(8,128)(2,1)S(1)}, u32[]{:S(2)}, u32[]{:S(2)}) %collective-permute-start.16) | collective-permute-done | bytes 262176 | tf_op jit(solution)/shard_map/other_late/ppermute | solution.py:50
  35.1 1.2 %late_product.1.high_ref = f32[256,512]{1,0:T(8,128)S(1)} custom-call(bf16[256,4096]{1,0:T(8,128)(2,1)S(1)} %copy-done, f32[256,512]{1,0:T(8,128)S(1)} %get-tuple-element.45.high_ref, bf16[32,4096]{1,0:T(8,128)(2,1)S(1)} %collective-permute-done.6.refs_0_, bf16[32,4096]{1,0:T(8,128)(2,1)S(1)} %collective-permute-done.8.refs_1_, ...), custom_call_target="tpu_custom_call" | custom-call | flops 1000000000 | bytes 262144 | tf_op jit(solution)/shard_map/late_product/pallas_call | solution.py:260
  36.3 1.4 %last.1 = (bf16[256,512]{1,0:T(8,128)(2,1)}, bf16[32,4096]{1,0:T(8,128)(2,1)}) custom-call(bf16[256,4096]{1,0:T(8,128)(2,1)S(1)} %copy-done, bf16[32,4096]{1,0:T(8,128)(2,1)S(1)} %copy-done.1, f32[256,128]{1,0:T(8,128)S(1)} %get-tuple-element.44.t_ref, f32[256,512]{1,0:T(8,128)S(1)} %late_product.1.high_ref, bf16[32,4096]{1,0:T(8,128)(2,1)S(1)} %get-tuple-element.48.m_ref, ...), custom_call_target="tpu_custom_call" | custom-call | flops 33554432 | bytes 262144 | tf_op jit(solution)/shard_map/last/pallas_call | solution.py:269
  (30 shorter events, 3.9 us)
Async XLA Ops:
  0.6 24.3 %collective-permute-start.9 = (bf16[256,4096]{1,0:T(8,128)(2,1)}, bf16[256,4096]{1,0:T(8,128)(2,1)S(1)}, u32[]{:S(2)}, u32[]{:S(2)}) collective-permute-start(bf16[256,4096]{1,0:T(8,128)(2,1)} %h_ref.7), channel_id=1, source_target_pairs={{0,1},{1,0},{2,3},{3,2},{4,5},{5,4},{6,7},{7,6},{8,9},{9,8},{10,11... | collective-permute-start | bytes 6291464 | tf_op jit(solution)/shard_map/other_hidden/ppermute | solution.py:50
  1.1 12.7 %collective-permute-start = (bf16[32,4096]{1,0:T(8,128)(2,1)}, bf16[32,4096]{1,0:T(8,128)(2,1)S(1)}, u32[]{:S(2)}, u32[]{:S(2)}) collective-permute-start(bf16[32,4096]{1,0:T(8,128)(2,1)} %w_ref.3), channel_id=1, source_target_pairs={{0,8},{1,5},{2,10},{3,7},{4,12},{5,1},{6,14},{7,3},{8,0},{9,13},{1... | collective-permute-start | bytes 786440 | tf_op jit(solution)/shard_map/w1/ppermute | solution.py:50
  4.8 9.0 %collective-permute-start.1 = (bf16[32,4096]{1,0:T(8,128)(2,1)}, bf16[32,4096]{1,0:T(8,128)(2,1)S(1)}, u32[]{:S(2)}, u32[]{:S(2)}) collective-permute-start(bf16[32,4096]{1,0:T(8,128)(2,1)} %w_ref.3), channel_id=1, source_target_pairs={{0,2},{1,3},{2,0},{3,1},{4,6},{5,7},{6,4},{7,5},{8,10},{9,11},{10,... | collective-permute-start | bytes 786440 | tf_op jit(solution)/shard_map/w2/ppermute | solution.py:50
  6.3 5.6 %collective-permute-start.2 = (f32[1,256,128]{2,1,0:T(8,128)}, f32[1,256,128]{2,1,0:T(8,128)S(1)}, u32[]{:S(2)}, u32[]{:S(2)}) collective-permute-start(f32[1,256,128]{2,1,0:T(8,128)} %param.10), channel_id=1, source_target_pairs={{0,16},{1,17},{2,18},{3,19},{4,20},{5,21},{6,22},{7,23},{8,24},{9,... | collective-permute-start | bytes 393224 | tf_op jit(solution)/shard_map/other_a/ppermute | solution.py:50
  6.8 5.1 %collective-permute-start.3 = (f32[1,32,128]{2,1,0:T(8,128)}, f32[1,32,128]{2,1,0:T(8,128)S(1)}, u32[]{:S(2)}, u32[]{:S(2)}) collective-permute-start(f32[1,32,128]{2,1,0:T(8,128)} %param.11), channel_id=1, source_target_pairs={{0,16},{1,17},{2,18},{3,19},{4,20},{5,21},{6,22},{7,23},{8,24},{9,... | collective-permute-start | bytes 49160 | tf_op jit(solution)/shard_map/other_b/ppermute | solution.py:50
  10.2 14.7 %copy-start = (bf16[256,4096]{1,0:T(8,128)(2,1)S(1)}, bf16[256,4096]{1,0:T(8,128)(2,1)}, u32[]{:S(2)}) copy-start(bf16[256,4096]{1,0:T(8,128)(2,1)} %h_ref.7) | copy-start | bytes 6291460
  10.2 14.7 %copy-start.1 = (bf16[32,4096]{1,0:T(8,128)(2,1)S(1)}, bf16[32,4096]{1,0:T(8,128)(2,1)}, u32[]{:S(2)}) copy-start(bf16[32,4096]{1,0:T(8,128)(2,1)} %w_ref.3) | copy-start | bytes 786436
  12.0 5.3 %collective-permute-start.10 = (bf16[288,128]{1,0:T(8,128)(2,1)S(1)}, bf16[288,128]{1,0:T(8,128)(2,1)S(1)}, u32[]{:S(2)}, u32[]{:S(2)}) collective-permute-start(bf16[288,128]{1,0:T(8,128)(2,1)S(1)} %update.1), channel_id=1, source_target_pairs={{0,8},{1,9},{2,10},{3,11},{4,12},{5,13},{6,14},{7,15},{8,0},{9,1},... | collective-permute-start | bytes 221192 | tf_op jit(solution)/shard_map/ab_far/ppermute | solution.py:50
  13.9 8.2 %collective-permute-start.4 = (bf16[32,4096]{1,0:T(8,128)(2,1)S(1)}, bf16[32,4096]{1,0:T(8,128)(2,1)S(1)}, u32[]{:S(2)}, u32[]{:S(2)}) collective-permute-start(bf16[32,4096]{1,0:T(8,128)(2,1)S(1)} %collective-permute-done.refs_1_), channel_id=1, source_target_pairs={{0,17},{1,16},{2,19},{3,18},{4,21},{5,20},{6,23},{7,22},{8,25},{9,... | collective-permute-start | bytes 786440 | tf_op jit(solution)/shard_map/w3/ppermute | solution.py:50
  14.2 9.0 %collective-permute-start.5 = (bf16[32,4096]{1,0:T(8,128)(2,1)S(1)}, bf16[32,4096]{1,0:T(8,128)(2,1)S(1)}, u32[]{:S(2)}, u32[]{:S(2)}) collective-permute-start(bf16[32,4096]{1,0:T(8,128)(2,1)S(1)} %collective-permute-done.refs_1_), channel_id=1, source_target_pairs={{0,2},{1,3},{2,0},{3,1},{4,6},{5,7},{6,4},{7,5},{8,10},{9,11},{10,... | collective-permute-start | bytes 786440 | tf_op jit(solution)/shard_map/w4/ppermute | solution.py:50
  15.7 9.2 %collective-permute-start.7 = (bf16[32,4096]{1,0:T(8,128)(2,1)S(1)}, bf16[32,4096]{1,0:T(8,128)(2,1)S(1)}, u32[]{:S(2)}, u32[]{:S(2)}) collective-permute-start(bf16[32,4096]{1,0:T(8,128)(2,1)S(1)} %collective-permute-done.refs_1_), channel_id=1, source_target_pairs={{0,4},{1,9},{2,6},{3,11},{4,0},{5,13},{6,2},{7,15},{8,12},{9,1},{1... | collective-permute-start | bytes 786440 | tf_op jit(solution)/shard_map/w5/ppermute | solution.py:50
  17.3 6.2 %collective-permute-start.11 = (bf16[576,128]{1,0:T(8,128)(2,1)S(1)}, bf16[576,128]{1,0:T(8,128)(2,1)S(1)}, u32[]{:S(2)}, u32[]{:S(2)}) collective-permute-start(bf16[576,128]{1,0:T(8,128)(2,1)S(1)} %constant_dynamic-update-slice_fusion.refs_0_.first_ref), channel_id=1, source_target_pairs={{0,1},{1,0},{2,3},{3,2},{4,5},{5,4},{6,7},{7,6},{8,9},{9,8},{10,11... | collective-permute-start | bytes 442376 | tf_op jit(solution)/shard_map/other_0/ppermute | solution.py:50
  22.0 5.6 %collective-permute-start.14 = (bf16[576,128]{1,0:T(8,128)(2,1)S(1)}, bf16[576,128]{1,0:T(8,128)(2,1)S(1)}, u32[]{:S(2)}, u32[]{:S(2)}) collective-permute-start(bf16[576,128]{1,0:T(8,128)(2,1)S(1)} %constant_dynamic-update-slice_fusion.refs_0_.first_ref), channel_id=1, source_target_pairs={{0,2},{1,3},{2,0},{3,1},{4,6},{5,7},{6,4},{7,5},{8,10},{9,11},{10,... | collective-permute-start | bytes 442376 | tf_op jit(solution)/shard_map/ab_2/ppermute | solution.py:50
  23.2 5.7 %collective-permute-start.13 = (bf16[576,128]{1,0:T(8,128)(2,1)S(1)}, bf16[576,128]{1,0:T(8,128)(2,1)S(1)}, u32[]{:S(2)}, u32[]{:S(2)}) collective-permute-start(bf16[576,128]{1,0:T(8,128)(2,1)S(1)} %constant_dynamic-update-slice_fusion.refs_0_.first_ref), channel_id=1, source_target_pairs={{0,4},{1,5},{2,6},{3,7},{4,0},{5,1},{6,2},{7,3},{8,12},{9,13},{10,... | collective-permute-start | bytes 442376 | tf_op jit(solution)/shard_map/ab_1/ppermute | solution.py:50
  23.5 8.3 %collective-permute-start.6 = (bf16[32,4096]{1,0:T(8,128)(2,1)S(1)}, bf16[32,4096]{1,0:T(8,128)(2,1)S(1)}, u32[]{:S(2)}, u32[]{:S(2)}) collective-permute-start(bf16[32,4096]{1,0:T(8,128)(2,1)S(1)} %collective-permute-done.5.refs_4_), channel_id=1, source_target_pairs={{0,17},{1,16},{2,19},{3,18},{4,21},{5,20},{6,23},{7,22},{8,25},{9,... | collective-permute-start | bytes 786440 | tf_op jit(solution)/shard_map/w6/ppermute | solution.py:50
  24.9 8.2 %collective-permute-start.8 = (bf16[32,4096]{1,0:T(8,128)(2,1)S(1)}, bf16[32,4096]{1,0:T(8,128)(2,1)S(1)}, u32[]{:S(2)}, u32[]{:S(2)}) collective-permute-start(bf16[32,4096]{1,0:T(8,128)(2,1)S(1)} %collective-permute-done.7.refs_5_), channel_id=1, source_target_pairs={{0,2},{1,3},{2,0},{3,1},{4,6},{5,7},{6,4},{7,5},{8,10},{9,11},{10,... | collective-permute-start | bytes 786440 | tf_op jit(solution)/shard_map/w7/ppermute | solution.py:50
  26.2 3.4 %collective-permute-start.12 = (f32[256,192]{1,0:T(8,128)S(1)}, f32[256,192]{1,0:T(8,128)S(1)}, u32[]{:S(2)}, u32[]{:S(2)}) collective-permute-start(f32[256,192]{1,0:T(8,128)S(1)} %get-tuple-element.41), channel_id=1, source_target_pairs={{0,1},{1,0},{2,3},{3,2},{4,5},{5,4},{6,7},{7,6},{8,9},{9,8},{10,11... | collective-permute-start | bytes 589832 | tf_op jit(solution)/shard_map/received/ppermute | solution.py:50
  27.6 2.0 %collective-permute-start.15 = (bf16[576,128]{1,0:T(8,128)(2,1)S(1)}, bf16[576,128]{1,0:T(8,128)(2,1)S(1)}, u32[]{:S(2)}, u32[]{:S(2)}) collective-permute-start(bf16[576,128]{1,0:T(8,128)(2,1)S(1)} %collective-permute-done.14.refs_2_), channel_id=1, source_target_pairs={{0,1},{1,0},{2,3},{3,2},{4,5},{5,4},{6,7},{7,6},{8,9},{9,8},{10,11... | collective-permute-start | bytes 442376 | tf_op jit(solution)/shard_map/other_2/ppermute | solution.py:50
  28.9 5.1 %collective-permute-start.18 = (bf16[576,128]{1,0:T(8,128)(2,1)S(1)}, bf16[576,128]{1,0:T(8,128)(2,1)S(1)}, u32[]{:S(2)}, u32[]{:S(2)}) collective-permute-start(bf16[576,128]{1,0:T(8,128)(2,1)S(1)} %collective-permute-done.14.refs_2_), channel_id=1, source_target_pairs={{0,4},{1,5},{2,6},{3,7},{4,0},{5,1},{6,2},{7,3},{8,12},{9,13},{10,... | collective-permute-start | bytes 442376 | tf_op jit(solution)/shard_map/ab_3/ppermute | solution.py:50
  33.2 1.5 %collective-permute-start.16 = (bf16[32,4096]{1,0:T(8,128)(2,1)S(1)}, bf16[32,4096]{1,0:T(8,128)(2,1)S(1)}, u32[]{:S(2)}, u32[]{:S(2)}) collective-permute-start(bf16[32,4096]{1,0:T(8,128)(2,1)S(1)} %collective-permute-done.6.refs_0_), channel_id=1, source_target_pairs={{0,1},{1,0},{2,3},{3,2},{4,5},{5,4},{6,7},{7,6},{8,9},{9,8},{10,11... | collective-permute-start | bytes 786440 | tf_op jit(solution)/shard_map/other_late/ppermute | solution.py:50
  33.2 1.9 %collective-permute-start.17 = (bf16[32,4096]{1,0:T(8,128)(2,1)S(1)}, bf16[32,4096]{1,0:T(8,128)(2,1)S(1)}, u32[]{:S(2)}, u32[]{:S(2)}) collective-permute-start(bf16[32,4096]{1,0:T(8,128)(2,1)S(1)} %collective-permute-done.8.refs_1_), channel_id=1, source_target_pairs={{0,1},{1,0},{2,3},{3,2},{4,5},{5,4},{6,7},{7,6},{8,9},{9,8},{10,11... | collective-permute-start | bytes 786440 | tf_op jit(solution)/shard_map/other_late/ppermute | solution.py:50
  34.0 2.2 %collective-permute-start.19 = (bf16[1152,128]{1,0:T(8,128)(2,1)S(1)}, bf16[1152,128]{1,0:T(8,128)(2,1)S(1)}, u32[]{:S(2)}, u32[]{:S(2)}) collective-permute-start(bf16[1152,128]{1,0:T(8,128)(2,1)S(1)} %pad_maximum_fusion), channel_id=1, source_target_pairs={{0,1},{1,0},{2,3},{3,2},{4,5},{5,4},{6,7},{7,6},{8,9},{9,8},{10,11... | collective-permute-start | bytes 884744 | tf_op jit(solution)/shard_map/other_3/ppermute | solution.py:50

commit v7 on v6

--- a/solution.py
+++ b/solution.py
@@ -101,9 +101,8 @@
     for i, (held, kind) in enumerate(block_of):
         column = jnp.where(source // rows == i, shard_of(flips_of(held, kind)) * rows, column)
     columns = (target == column + source % rows).astype(jnp.bfloat16)
-    for part in split_bf16(products):
-        out = out + dot(part, columns, NN)
-    return out
+    both = jnp.concatenate(split_bf16(products), axis=1)
+    return out + dot(both, jnp.concatenate([columns, columns]), NN)
 
 
 def split_bf16(v):
@@ -163,9 +162,8 @@
     own, joined = ab_refs
     blocks = [(own, 0, at[-1], 0)] + [(joined, 1, k, 2 * i) for i, k in enumerate(at)]
     t = add_blocks(h_ref, w_ref, b_own, merged_ref, b_all, blocks, t_ref[...])
-    out = high_ref[...]
-    for part in split_bf16(t):
-        out = out + dot(part, b_all[...], NT)
+    both = jnp.concatenate(split_bf16(t), axis=1)
+    out = high_ref[...] + dot(both, jnp.concatenate([b_all[...], b_all[...]], axis=1), NT)
     out_ref[...] = out.astype(jnp.bfloat16)
 
 

time: 37.9 us -> 37.7 us (level)
  no operation moved by 1% of the time
where the time goes in v7:
time: 37.7 us; the launch traced here: 37.4 us
  starting transfers between devices  15.7 us (42%)
  waiting for transfers between devices  14.5 us (38%)
  Pallas kernels  4.52 us (12%)
  other arithmetic  1.89 us (5%)
  between operations  0.73 us (2%)
    ppermute x20, starting transfers between devices, send(): return lax.ppermute(rows, AXES, pairs)  15.7 us
    ppermute x20, waiting for transfers between devices, send(): return lax.ppermute(rows, AXES, pairs)  14.5 us
    pallas_call x1, Pallas kernels, paired(): pl.pallas_call(functools.partial(last_kernel, (1, 3)), out_shape=[jax.Sha...  1.33 us
    pallas_call x1, Pallas kernels, paired(): pl.pallas_call(weight_kernel, out_shape=[jax.ShapeDtypeStruct((tokens, co...  1.26 us
    pallas_call x1, Pallas kernels, paired(): pl.pallas_call(functools.partial(late_kernel, tuple(range(EARLY, len(HELD...  0.96 us
    pallas_call x1, Pallas kernels, paired(): pl.pallas_call(functools.partial(middle_kernel, middle, (0, 2), EARLY), o...  0.94 us
    concatenate x1, other arithmetic, paired(): mine = jnp.concatenate([grad_a[0], grad_b[0]])  0.93 us
    concatenate x1, other arithmetic, paired(): old = jnp.concatenate([adapter_a, adapter_b])  0.93 us
  transfers between devices with their start and end apart: 20, of which 12 were waited for; matrix products, arithmetic and copies ran while one was open for 5% of the time, Pallas kernels for 9%

profile of v7, /device:TPU:0, one launch (start us, length us, event | category | flops | bytes accessed | tf_op | source)
XLA Modules:
  0.0 37.4 jit_solution(651516789536505251)
XLA Ops:
  1.1 3.7 %collective-permute-start = (bf16[32,4096]{1,0:T(8,128)(2,1)}, bf16[32,4096]{1,0:T(8,128)(2,1)S(1)}, u32[]{:S(2)}, u32[]{:S(2)}) collective-permute-start(bf16[32,4096]{1,0:T(8,128)(2,1)} %w_ref.3), channel_id=1, source_target_pairs={{0,8},{1,5},{2,10},{3,7},{4,12},{5,1},{6,14},{7,3},{8,0},{9,13},{1... | collective-permute-start | bytes 786440 | tf_op jit(solution)/shard_map/w1/ppermute | solution.py:50
  4.8 1.5 %collective-permute-start.1 = (bf16[32,4096]{1,0:T(8,128)(2,1)}, bf16[32,4096]{1,0:T(8,128)(2,1)S(1)}, u32[]{:S(2)}, u32[]{:S(2)}) collective-permute-start(bf16[32,4096]{1,0:T(8,128)(2,1)} %w_ref.3), channel_id=1, source_target_pairs={{0,2},{1,3},{2,0},{3,1},{4,6},{5,7},{6,4},{7,5},{8,10},{9,11},{10,... | collective-permute-start | bytes 786440 | tf_op jit(solution)/shard_map/w2/ppermute | solution.py:50
  6.8 1.5 %collective-permute-start.3 = (f32[1,32,128]{2,1,0:T(8,128)}, f32[1,32,128]{2,1,0:T(8,128)S(1)}, u32[]{:S(2)}, u32[]{:S(2)}) collective-permute-start(f32[1,32,128]{2,1,0:T(8,128)} %param.11), channel_id=1, source_target_pairs={{0,16},{1,17},{2,18},{3,19},{4,20},{5,21},{6,22},{7,23},{8,24},{9,... | collective-permute-start | bytes 49160 | tf_op jit(solution)/shard_map/other_b/ppermute | solution.py:50
  8.4 0.9 %pad_maximum_fusion.1.old_ref = f32[288,128]{1,0:T(8,128)S(1)} fusion(f32[32,128]{1,0:T(8,128)} %param.9, f32[256,128]{1,0:T(8,128)} %param.8), kind=kLoop, calls=%fused_computation.1 | loop fusion | flops 36864 | bytes 294912 | tf_op jit(solution)/shard_map/concatenate | solution.py:187
  9.3 0.9 %pad_maximum_fusion.2.own_ref = f32[288,128]{1,0:T(8,128)S(1)} fusion(f32[32,128]{1,0:T(8,128)} %bitcast.3, f32[256,128]{1,0:T(8,128)} %bitcast.2), kind=kLoop, calls=%fused_computation.2 | loop fusion | flops 36864 | bytes 294912 | tf_op jit(solution)/shard_map/concatenate | solution.py:188
  10.3 1.7 %collective-permute-done.3.ob_ref = f32[1,32,128]{2,1,0:T(8,128)S(1)} collective-permute-done((f32[1,32,128]{2,1,0:T(8,128)}, f32[1,32,128]{2,1,0:T(8,128)S(1)}, u32[]{:S(2)}, u32[]{:S(2)}) %collective-permute-start.3) | collective-permute-done | bytes 16416 | tf_op jit(solution)/shard_map/other_b/ppermute | solution.py:50
  12.0 1.9 %collective-permute-start.10 = (bf16[288,128]{1,0:T(8,128)(2,1)S(1)}, bf16[288,128]{1,0:T(8,128)(2,1)S(1)}, u32[]{:S(2)}, u32[]{:S(2)}) collective-permute-start(bf16[288,128]{1,0:T(8,128)(2,1)S(1)} %update.1), channel_id=1, source_target_pairs={{0,8},{1,9},{2,10},{3,11},{4,12},{5,13},{6,14},{7,15},{8,0},{9,1},... | collective-permute-start | bytes 221192 | tf_op jit(solution)/shard_map/ab_far/ppermute | solution.py:50
  14.2 1.5 %collective-permute-start.5 = (bf16[32,4096]{1,0:T(8,128)(2,1)S(1)}, bf16[32,4096]{1,0:T(8,128)(2,1)S(1)}, u32[]{:S(2)}, u32[]{:S(2)}) collective-permute-start(bf16[32,4096]{1,0:T(8,128)(2,1)S(1)} %collective-permute-done.refs_1_), channel_id=1, source_target_pairs={{0,2},{1,3},{2,0},{3,1},{4,6},{5,7},{6,4},{7,5},{8,10},{9,11},{10,... | collective-permute-start | bytes 786440 | tf_op jit(solution)/shard_map/w4/ppermute | solution.py:50
  16.1 1.2 %collective-permute-done.10 = bf16[288,128]{1,0:T(8,128)(2,1)S(1)} collective-permute-done((bf16[288,128]{1,0:T(8,128)(2,1)S(1)}, bf16[288,128]{1,0:T(8,128)(2,1)S(1)}, u32[]{:S(2)}, u32[]{:S(2)}) %collective-permute-start.10) | collective-permute-done | bytes 73760 | tf_op jit(solution)/shard_map/ab_far/ppermute | solution.py:50
  17.4 4.7 %collective-permute-done.4.refs_3_ = bf16[32,4096]{1,0:T(8,128)(2,1)S(1)} collective-permute-done((bf16[32,4096]{1,0:T(8,128)(2,1)S(1)}, bf16[32,4096]{1,0:T(8,128)(2,1)S(1)}, u32[]{:S(2)}, u32[]{:S(2)}) %collective-permute-start.4) | collective-permute-done | bytes 262176 | tf_op jit(solution)/shard_map/w3/ppermute | solution.py:50
  22.0 0.7 %collective-permute-start.14 = (bf16[576,128]{1,0:T(8,128)(2,1)S(1)}, bf16[576,128]{1,0:T(8,128)(2,1)S(1)}, u32[]{:S(2)}, u32[]{:S(2)}) collective-permute-start(bf16[576,128]{1,0:T(8,128)(2,1)S(1)} %constant_dynamic-update-slice_fusion.refs_0_.first_ref), channel_id=1, source_target_pairs={{0,2},{1,3},{2,0},{3,1},{4,6},{5,7},{6,4},{7,5},{8,10},{9,11},{10,... | collective-permute-start | bytes 442376 | tf_op jit(solution)/shard_map/ab_2/ppermute | solution.py:50
  23.5 0.7 %collective-permute-start.6 = (bf16[32,4096]{1,0:T(8,128)(2,1)S(1)}, bf16[32,4096]{1,0:T(8,128)(2,1)S(1)}, u32[]{:S(2)}, u32[]{:S(2)}) collective-permute-start(bf16[32,4096]{1,0:T(8,128)(2,1)S(1)} %collective-permute-done.5.refs_4_), channel_id=1, source_target_pairs={{0,17},{1,16},{2,19},{3,18},{4,21},{5,20},{6,23},{7,22},{8,25},{9,... | collective-permute-start | bytes 786440 | tf_op jit(solution)/shard_map/w6/ppermute | solution.py:50
  24.1 0.8 %collective-permute-done.7.refs_5_ = bf16[32,4096]{1,0:T(8,128)(2,1)S(1)} collective-permute-done((bf16[32,4096]{1,0:T(8,128)(2,1)S(1)}, bf16[32,4096]{1,0:T(8,128)(2,1)S(1)}, u32[]{:S(2)}, u32[]{:S(2)}) %collective-permute-start.7) | collective-permute-done | bytes 262176 | tf_op jit(solution)/shard_map/w5/ppermute | solution.py:50
  25.0 1.3 %weight_product.1 = (f32[256,192]{1,0:T(8,128)S(1)}, f32[256,192]{1,0:T(8,128)S(1)}) custom-call(bf16[256,4096]{1,0:T(8,128)(2,1)S(1)} %copy-done, bf16[256,4096]{1,0:T(8,128)(2,1)S(1)} %collective-permute-done.9.hs_ref, bf16[32,4096]{1,0:T(8,128)(2,1)S(1)} %copy-done.1, bf16[32,4096]{1,0:T(8,128)(2,1)S(1)} %collective-permute-done.refs_1_, ...), custom_call_target="tpu_custom_call" | custom-call | flops 3221225472 | bytes 5767168 | tf_op jit(solution)/shard_map/weight_product/pallas_call | solution.py:230
  26.2 0.7 %collective-permute-start.12 = (f32[256,192]{1,0:T(8,128)S(1)}, f32[256,192]{1,0:T(8,128)S(1)}, u32[]{:S(2)}, u32[]{:S(2)}) collective-permute-start(f32[256,192]{1,0:T(8,128)S(1)} %get-tuple-element.41), channel_id=1, source_target_pairs={{0,1},{1,0},{2,3},{3,2},{4,5},{5,4},{6,7},{7,6},{8,9},{9,8},{10,11... | collective-permute-start | bytes 589832 | tf_op jit(solution)/shard_map/received/ppermute | solution.py:50
  27.0 0.7 %collective-permute-done.14.refs_2_ = bf16[576,128]{1,0:T(8,128)(2,1)S(1)} collective-permute-done((bf16[576,128]{1,0:T(8,128)(2,1)S(1)}, bf16[576,128]{1,0:T(8,128)(2,1)S(1)}, u32[]{:S(2)}, u32[]{:S(2)}) %collective-permute-start.14) | collective-permute-done | bytes 147488 | tf_op jit(solution)/shard_map/ab_2/ppermute | solution.py:50
  27.6 1.2 %collective-permute-done.13.refs_1_ = bf16[576,128]{1,0:T(8,128)(2,1)S(1)} collective-permute-done((bf16[576,128]{1,0:T(8,128)(2,1)S(1)}, bf16[576,128]{1,0:T(8,128)(2,1)S(1)}, u32[]{:S(2)}, u32[]{:S(2)}) %collective-permute-start.13) | collective-permute-done | bytes 147488 | tf_op jit(solution)/shard_map/ab_1/ppermute | solution.py:50
  28.9 0.7 %collective-permute-start.18 = (bf16[576,128]{1,0:T(8,128)(2,1)S(1)}, bf16[576,128]{1,0:T(8,128)(2,1)S(1)}, u32[]{:S(2)}, u32[]{:S(2)}) collective-permute-start(bf16[576,128]{1,0:T(8,128)(2,1)S(1)} %collective-permute-done.14.refs_2_), channel_id=1, source_target_pairs={{0,4},{1,5},{2,6},{3,7},{4,0},{5,1},{6,2},{7,3},{8,12},{9,13},{10,... | collective-permute-start | bytes 442376 | tf_op jit(solution)/shard_map/ab_3/ppermute | solution.py:50
  29.6 0.9 %middle.1 = (f32[256,128]{1,0:T(8,128)S(1)}, f32[256,512]{1,0:T(8,128)S(1)}, bf16[32,4096]{1,0:T(8,128)(2,1)S(1)}, bf16[512,128]{1,0:T(8,128)(2,1)S(1)}) custom-call(bf16[256,4096]{1,0:T(8,128)(2,1)S(1)} %copy-done, bf16[32,4096]{1,0:T(8,128)(2,1)S(1)} %copy-done.1, f32[256,192]{1,0:T(8,128)S(1)} %get-tuple-element.40.own_ref, ...), custom_call_target="tpu_custom_call" | custom-call | flops 268435456 | bytes 3145728 | tf_op jit(solution)/shard_map/middle/pallas_call | solution.py:242
  30.6 1.3 %collective-permute-done.6.refs_0_ = bf16[32,4096]{1,0:T(8,128)(2,1)S(1)} collective-permute-done((bf16[32,4096]{1,0:T(8,128)(2,1)S(1)}, bf16[32,4096]{1,0:T(8,128)(2,1)S(1)}, u32[]{:S(2)}, u32[]{:S(2)}) %collective-permute-start.6) | collective-permute-done | bytes 262176 | tf_op jit(solution)/shard_map/w6/ppermute | solution.py:50
  31.8 1.3 %collective-permute-done.8.refs_1_ = bf16[32,4096]{1,0:T(8,128)(2,1)S(1)} collective-permute-done((bf16[32,4096]{1,0:T(8,128)(2,1)S(1)}, bf16[32,4096]{1,0:T(8,128)(2,1)S(1)}, u32[]{:S(2)}, u32[]{:S(2)}) %collective-permute-start.8) | collective-permute-done | bytes 262176 | tf_op jit(solution)/shard_map/w7/ppermute | solution.py:50
  34.1 0.6 %collective-permute-done.16.refs_2_ = bf16[32,4096]{1,0:T(8,128)(2,1)S(1)} collective-permute-done((bf16[32,4096]{1,0:T(8,128)(2,1)S(1)}, bf16[32,4096]{1,0:T(8,128)(2,1)S(1)}, u32[]{:S(2)}, u32[]{:S(2)}) %collective-permute-start.16) | collective-permute-done | bytes 262176 | tf_op jit(solution)/shard_map/other_late/ppermute | solution.py:50
  35.1 1.0 %late_product.1.high_ref = f32[256,512]{1,0:T(8,128)S(1)} custom-call(bf16[256,4096]{1,0:T(8,128)(2,1)S(1)} %copy-done, f32[256,512]{1,0:T(8,128)S(1)} %get-tuple-element.45.high_ref, bf16[32,4096]{1,0:T(8,128)(2,1)S(1)} %collective-permute-done.6.refs_0_, bf16[32,4096]{1,0:T(8,128)(2,1)S(1)} %collective-permute-done.8.refs_1_, ...), custom_call_target="tpu_custom_call" | custom-call | flops 1000000000 | bytes 262144 | tf_op jit(solution)/shard_map/late_product/pallas_call | solution.py:258
  36.0 1.3 %last.1 = (bf16[256,512]{1,0:T(8,128)(2,1)}, bf16[32,4096]{1,0:T(8,128)(2,1)}) custom-call(bf16[256,4096]{1,0:T(8,128)(2,1)S(1)} %copy-done, bf16[32,4096]{1,0:T(8,128)(2,1)S(1)} %copy-done.1, f32[256,128]{1,0:T(8,128)S(1)} %get-tuple-element.44.t_ref, f32[256,512]{1,0:T(8,128)S(1)} %late_product.1.high_ref, bf16[32,4096]{1,0:T(8,128)(2,1)S(1)} %get-tuple-element.48.m_ref, ...), custom_call_target="tpu_custom_call" | custom-call | flops 33554432 | bytes 262144 | tf_op jit(solution)/shard_map/last/pallas_call | solution.py:267
  (30 shorter events, 3.9 us)
Async XLA Ops:
  0.6 24.3 %collective-permute-start.9 = (bf16[256,4096]{1,0:T(8,128)(2,1)}, bf16[256,4096]{1,0:T(8,128)(2,1)S(1)}, u32[]{:S(2)}, u32[]{:S(2)}) collective-permute-start(bf16[256,4096]{1,0:T(8,128)(2,1)} %h_ref.7), channel_id=1, source_target_pairs={{0,1},{1,0},{2,3},{3,2},{4,5},{5,4},{6,7},{7,6},{8,9},{9,8},{10,11... | collective-permute-start | bytes 6291464 | tf_op jit(solution)/shard_map/other_hidden/ppermute | solution.py:50
  1.1 12.7 %collective-permute-start = (bf16[32,4096]{1,0:T(8,128)(2,1)}, bf16[32,4096]{1,0:T(8,128)(2,1)S(1)}, u32[]{:S(2)}, u32[]{:S(2)}) collective-permute-start(bf16[32,4096]{1,0:T(8,128)(2,1)} %w_ref.3), channel_id=1, source_target_pairs={{0,8},{1,5},{2,10},{3,7},{4,12},{5,1},{6,14},{7,3},{8,0},{9,13},{1... | collective-permute-start | bytes 786440 | tf_op jit(solution)/shard_map/w1/ppermute | solution.py:50
  4.8 9.0 %collective-permute-start.1 = (bf16[32,4096]{1,0:T(8,128)(2,1)}, bf16[32,4096]{1,0:T(8,128)(2,1)S(1)}, u32[]{:S(2)}, u32[]{:S(2)}) collective-permute-start(bf16[32,4096]{1,0:T(8,128)(2,1)} %w_ref.3), channel_id=1, source_target_pairs={{0,2},{1,3},{2,0},{3,1},{4,6},{5,7},{6,4},{7,5},{8,10},{9,11},{10,... | collective-permute-start | bytes 786440 | tf_op jit(solution)/shard_map/w2/ppermute | solution.py:50
  6.3 5.6 %collective-permute-start.2 = (f32[1,256,128]{2,1,0:T(8,128)}, f32[1,256,128]{2,1,0:T(8,128)S(1)}, u32[]{:S(2)}, u32[]{:S(2)}) collective-permute-start(f32[1,256,128]{2,1,0:T(8,128)} %param.10), channel_id=1, source_target_pairs={{0,16},{1,17},{2,18},{3,19},{4,20},{5,21},{6,22},{7,23},{8,24},{9,... | collective-permute-start | bytes 393224 | tf_op jit(solution)/shard_map/other_a/ppermute | solution.py:50
  6.8 5.1 %collective-permute-start.3 = (f32[1,32,128]{2,1,0:T(8,128)}, f32[1,32,128]{2,1,0:T(8,128)S(1)}, u32[]{:S(2)}, u32[]{:S(2)}) collective-permute-start(f32[1,32,128]{2,1,0:T(8,128)} %param.11), channel_id=1, source_target_pairs={{0,16},{1,17},{2,18},{3,19},{4,20},{5,21},{6,22},{7,23},{8,24},{9,... | collective-permute-start | bytes 49160 | tf_op jit(solution)/shard_map/other_b/ppermute | solution.py:50
  10.2 14.7 %copy-start = (bf16[256,4096]{1,0:T(8,128)(2,1)S(1)}, bf16[256,4096]{1,0:T(8,128)(2,1)}, u32[]{:S(2)}) copy-start(bf16[256,4096]{1,0:T(8,128)(2,1)} %h_ref.7) | copy-start | bytes 6291460
  10.2 14.7 %copy-start.1 = (bf16[32,4096]{1,0:T(8,128)(2,1)S(1)}, bf16[32,4096]{1,0:T(8,128)(2,1)}, u32[]{:S(2)}) copy-start(bf16[32,4096]{1,0:T(8,128)(2,1)} %w_ref.3) | copy-start | bytes 786436
  12.0 5.3 %collective-permute-start.10 = (bf16[288,128]{1,0:T(8,128)(2,1)S(1)}, bf16[288,128]{1,0:T(8,128)(2,1)S(1)}, u32[]{:S(2)}, u32[]{:S(2)}) collective-permute-start(bf16[288,128]{1,0:T(8,128)(2,1)S(1)} %update.1), channel_id=1, source_target_pairs={{0,8},{1,9},{2,10},{3,11},{4,12},{5,13},{6,14},{7,15},{8,0},{9,1},... | collective-permute-start | bytes 221192 | tf_op jit(solution)/shard_map/ab_far/ppermute | solution.py:50
  13.9 8.2 %collective-permute-start.4 = (bf16[32,4096]{1,0:T(8,128)(2,1)S(1)}, bf16[32,4096]{1,0:T(8,128)(2,1)S(1)}, u32[]{:S(2)}, u32[]{:S(2)}) collective-permute-start(bf16[32,4096]{1,0:T(8,128)(2,1)S(1)} %collective-permute-done.refs_1_), channel_id=1, source_target_pairs={{0,17},{1,16},{2,19},{3,18},{4,21},{5,20},{6,23},{7,22},{8,25},{9,... | collective-permute-start | bytes 786440 | tf_op jit(solution)/shard_map/w3/ppermute | solution.py:50
  14.2 9.0 %collective-permute-start.5 = (bf16[32,4096]{1,0:T(8,128)(2,1)S(1)}, bf16[32,4096]{1,0:T(8,128)(2,1)S(1)}, u32[]{:S(2)}, u32[]{:S(2)}) collective-permute-start(bf16[32,4096]{1,0:T(8,128)(2,1)S(1)} %collective-permute-done.refs_1_), channel_id=1, source_target_pairs={{0,2},{1,3},{2,0},{3,1},{4,6},{5,7},{6,4},{7,5},{8,10},{9,11},{10,... | collective-permute-start | bytes 786440 | tf_op jit(solution)/shard_map/w4/ppermute | solution.py:50
  15.7 9.2 %collective-permute-start.7 = (bf16[32,4096]{1,0:T(8,128)(2,1)S(1)}, bf16[32,4096]{1,0:T(8,128)(2,1)S(1)}, u32[]{:S(2)}, u32[]{:S(2)}) collective-permute-start(bf16[32,4096]{1,0:T(8,128)(2,1)S(1)} %collective-permute-done.refs_1_), channel_id=1, source_target_pairs={{0,4},{1,9},{2,6},{3,11},{4,0},{5,13},{6,2},{7,15},{8,12},{9,1},{1... | collective-permute-start | bytes 786440 | tf_op jit(solution)/shard_map/w5/ppermute | solution.py:50
  17.3 6.2 %collective-permute-start.11 = (bf16[576,128]{1,0:T(8,128)(2,1)S(1)}, bf16[576,128]{1,0:T(8,128)(2,1)S(1)}, u32[]{:S(2)}, u32[]{:S(2)}) collective-permute-start(bf16[576,128]{1,0:T(8,128)(2,1)S(1)} %constant_dynamic-update-slice_fusion.refs_0_.first_ref), channel_id=1, source_target_pairs={{0,1},{1,0},{2,3},{3,2},{4,5},{5,4},{6,7},{7,6},{8,9},{9,8},{10,11... | collective-permute-start | bytes 442376 | tf_op jit(solution)/shard_map/other_0/ppermute | solution.py:50
  22.0 5.6 %collective-permute-start.14 = (bf16[576,128]{1,0:T(8,128)(2,1)S(1)}, bf16[576,128]{1,0:T(8,128)(2,1)S(1)}, u32[]{:S(2)}, u32[]{:S(2)}) collective-permute-start(bf16[576,128]{1,0:T(8,128)(2,1)S(1)} %constant_dynamic-update-slice_fusion.refs_0_.first_ref), channel_id=1, source_target_pairs={{0,2},{1,3},{2,0},{3,1},{4,6},{5,7},{6,4},{7,5},{8,10},{9,11},{10,... | collective-permute-start | bytes 442376 | tf_op jit(solution)/shard_map/ab_2/ppermute | solution.py:50
  23.2 5.7 %collective-permute-start.13 = (bf16[576,128]{1,0:T(8,128)(2,1)S(1)}, bf16[576,128]{1,0:T(8,128)(2,1)S(1)}, u32[]{:S(2)}, u32[]{:S(2)}) collective-permute-start(bf16[576,128]{1,0:T(8,128)(2,1)S(1)} %constant_dynamic-update-slice_fusion.refs_0_.first_ref), channel_id=1, source_target_pairs={{0,4},{1,5},{2,6},{3,7},{4,0},{5,1},{6,2},{7,3},{8,12},{9,13},{10,... | collective-permute-start | bytes 442376 | tf_op jit(solution)/shard_map/ab_1/ppermute | solution.py:50
  23.5 8.3 %collective-permute-start.6 = (bf16[32,4096]{1,0:T(8,128)(2,1)S(1)}, bf16[32,4096]{1,0:T(8,128)(2,1)S(1)}, u32[]{:S(2)}, u32[]{:S(2)}) collective-permute-start(bf16[32,4096]{1,0:T(8,128)(2,1)S(1)} %collective-permute-done.5.refs_4_), channel_id=1, source_target_pairs={{0,17},{1,16},{2,19},{3,18},{4,21},{5,20},{6,23},{7,22},{8,25},{9,... | collective-permute-start | bytes 786440 | tf_op jit(solution)/shard_map/w6/ppermute | solution.py:50
  24.9 8.2 %collective-permute-start.8 = (bf16[32,4096]{1,0:T(8,128)(2,1)S(1)}, bf16[32,4096]{1,0:T(8,128)(2,1)S(1)}, u32[]{:S(2)}, u32[]{:S(2)}) collective-permute-start(bf16[32,4096]{1,0:T(8,128)(2,1)S(1)} %collective-permute-done.7.refs_5_), channel_id=1, source_target_pairs={{0,2},{1,3},{2,0},{3,1},{4,6},{5,7},{6,4},{7,5},{8,10},{9,11},{10,... | collective-permute-start | bytes 786440 | tf_op jit(solution)/shard_map/w7/ppermute | solution.py:50
  26.2 3.4 %collective-permute-start.12 = (f32[256,192]{1,0:T(8,128)S(1)}, f32[256,192]{1,0:T(8,128)S(1)}, u32[]{:S(2)}, u32[]{:S(2)}) collective-permute-start(f32[256,192]{1,0:T(8,128)S(1)} %get-tuple-element.41), channel_id=1, source_target_pairs={{0,1},{1,0},{2,3},{3,2},{4,5},{5,4},{6,7},{7,6},{8,9},{9,8},{10,11... | collective-permute-start | bytes 589832 | tf_op jit(solution)/shard_map/received/ppermute | solution.py:50
  27.6 2.0 %collective-permute-start.15 = (bf16[576,128]{1,0:T(8,128)(2,1)S(1)}, bf16[576,128]{1,0:T(8,128)(2,1)S(1)}, u32[]{:S(2)}, u32[]{:S(2)}) collective-permute-start(bf16[576,128]{1,0:T(8,128)(2,1)S(1)} %collective-permute-done.14.refs_2_), channel_id=1, source_target_pairs={{0,1},{1,0},{2,3},{3,2},{4,5},{5,4},{6,7},{7,6},{8,9},{9,8},{10,11... | collective-permute-start | bytes 442376 | tf_op jit(solution)/shard_map/other_2/ppermute | solution.py:50
  28.9 5.1 %collective-permute-start.18 = (bf16[576,128]{1,0:T(8,128)(2,1)S(1)}, bf16[576,128]{1,0:T(8,128)(2,1)S(1)}, u32[]{:S(2)}, u32[]{:S(2)}) collective-permute-start(bf16[576,128]{1,0:T(8,128)(2,1)S(1)} %collective-permute-done.14.refs_2_), channel_id=1, source_target_pairs={{0,4},{1,5},{2,6},{3,7},{4,0},{5,1},{6,2},{7,3},{8,12},{9,13},{10,... | collective-permute-start | bytes 442376 | tf_op jit(solution)/shard_map/ab_3/ppermute | solution.py:50
  33.2 1.5 %collective-permute-start.16 = (bf16[32,4096]{1,0:T(8,128)(2,1)S(1)}, bf16[32,4096]{1,0:T(8,128)(2,1)S(1)}, u32[]{:S(2)}, u32[]{:S(2)}) collective-permute-start(bf16[32,4096]{1,0:T(8,128)(2,1)S(1)} %collective-permute-done.6.refs_0_), channel_id=1, source_target_pairs={{0,1},{1,0},{2,3},{3,2},{4,5},{5,4},{6,7},{7,6},{8,9},{9,8},{10,11... | collective-permute-start | bytes 786440 | tf_op jit(solution)/shard_map/other_late/ppermute | solution.py:50
  33.2 1.9 %collective-permute-start.17 = (bf16[32,4096]{1,0:T(8,128)(2,1)S(1)}, bf16[32,4096]{1,0:T(8,128)(2,1)S(1)}, u32[]{:S(2)}, u32[]{:S(2)}) collective-permute-start(bf16[32,4096]{1,0:T(8,128)(2,1)S(1)} %collective-permute-done.8.refs_1_), channel_id=1, source_target_pairs={{0,1},{1,0},{2,3},{3,2},{4,5},{5,4},{6,7},{7,6},{8,9},{9,8},{10,11... | collective-permute-start | bytes 786440 | tf_op jit(solution)/shard_map/other_late/ppermute | solution.py:50
  34.0 2.0 %collective-permute-start.19 = (bf16[1152,128]{1,0:T(8,128)(2,1)S(1)}, bf16[1152,128]{1,0:T(8,128)(2,1)S(1)}, u32[]{:S(2)}, u32[]{:S(2)}) collective-permute-start(bf16[1152,128]{1,0:T(8,128)(2,1)S(1)} %pad_maximum_fusion), channel_id=1, source_target_pairs={{0,1},{1,0},{2,3},{3,2},{4,5},{5,4},{6,7},{7,6},{8,9},{9,8},{10,11... | collective-permute-start | bytes 884744 | tf_op jit(solution)/shard_map/other_3/ppermute | solution.py:50
